TPU v7x, 256 devices: a whole 4x4x8 slice. The times are simulated.
256 devices in a mesh: seq: 2 (over core), row: 16 (over y, x), head: 8 (over z).
Axes of the slice: x: 4, y: 4, z: 8, core: 2. Of those that a mesh axis runs over, the one named last changes fastest.
Arguments:
- seq_in: bfloat16 [24576, 10240], P(('seq', 'row'), 'head'), may hold values from -6 to 6
- gate_in: bfloat16 [24576, 10240], P(('seq', 'row'), 'head'), may hold values from -6 to 6
- b_in: bfloat16 [24576, 128], P(('seq', 'row')), may hold values from -0.5 to 0.5
- c_in: bfloat16 [24576, 128], P(('seq', 'row')), may hold values from -6 to 6
- step: float32 [80, 24576], P('head', ('seq', 'row')), may hold values from 0 to 1, as said below
- log_gate: float32 [80, 24576], P('head', ('seq', 'row')), may hold values from -1 to 0, as said below
- skip: float32 [80], P('head'), may hold values from 0.2 to 0.6
- out_weight: bfloat16 [2560, 10240], P(('seq', 'row'), 'head'), may hold values from -0.0625 to 0.0625
Outputs:
- result_out: bfloat16 [24576, 2560], P(('seq', 'row'), 'head')
Inputs may be any that keep to these rules, and one draw needn't show every extreme that they name: `step`: positive. `log_gate`: at most zero.
All inputs are finite; a program needn't handle non-finite values.
Results may differ from a plain program's by a relative error of at most 0.022.
Values may be sent and summed in bfloat16 or wider, within the bound.
No kernel may reach another device: no remote copies, remote signals or barrier semaphores. Data moves between devices by JAX's collectives and lax.ppermute only.
A program may use at most 128 MiB of HBM per device.

v0:
```python
import jax
import jax.numpy as jnp
from jax import lax
from jax.sharding import PartitionSpec as P

P_SIZE = 128
N = 128
BLK = 128


def carried_in(value, axis, combine, identity):
    peers, mine = (lax.axis_size(axis), lax.axis_index(axis))
    everything = jax.tree.map(
        lambda part, kind: lax.all_gather(part.astype(kind), axis),
        value,
        (jnp.bfloat16, jnp.bfloat16),
    )
    start = jax.tree.map(
        lambda part, zero: jnp.broadcast_to(jnp.asarray(zero, part.dtype), part.shape),
        value,
        identity,
    )

    def carried_turn(k, before):
        reached = k < mine
        new = combine(
            before, jax.tree.map(lambda part, own: part[k].astype(own.dtype), everything, value)
        )
        return jax.tree.map(lambda a, b: jnp.where(reached, a, b), new, before)

    return lax.fori_loop(0, peers, carried_turn, start)


def for_sending(value):

    def short(part):
        return part.astype(jnp.bfloat16) if part.dtype == jnp.float32 else part

    return jax.tree.map(short, value)


def broadcast(value, axis, root):
    mine = lax.axis_index(axis) == root
    return lax.psum(jnp.where(mine, value, jnp.zeros_like(value)), axis)


def prefix(value, axis, combine, identity):
    peers, mine = (lax.axis_size(axis), lax.axis_index(axis))
    everything = jax.tree.map(
        lambda part, kind: lax.all_gather(part.astype(kind), axis),
        value,
        jax.tree.map(lambda a: jnp.bfloat16 if a.dtype == jnp.float32 else a.dtype, value),
    )
    start = jax.tree.map(
        lambda part, zero: jnp.broadcast_to(jnp.asarray(zero, part.dtype), part.shape),
        value,
        identity,
    )

    def prefix_turn(k, before):
        reached = k < mine
        new = combine(
            before, jax.tree.map(lambda part, own: part[k].astype(own.dtype), everything, value)
        )
        return jax.tree.map(lambda a, b: jnp.where(reached, a, b), new, before)

    return lax.fori_loop(0, peers, prefix_turn, start)


def combine(earlier, latter):
    return (earlier[0] + latter[0], jnp.exp(latter[0])[:, None, None] * earlier[1] + latter[1])


def shards(seq_in, gate_in, b_in, c_in, step, log_gate, skip, out_weight):
    tok_count, channels = seq_in.shape
    head_count = step.shape[0]
    block_count = tok_count // BLK
    inputs = seq_in.reshape(block_count, BLK, head_count, P_SIZE)
    b_rows = b_in.reshape(block_count, BLK, N)
    c_rows = c_in.reshape(block_count, BLK, N)
    steps_blk = step.reshape(head_count, block_count, BLK)
    running = jnp.cumsum(log_gate.reshape(head_count, block_count, BLK), axis=2)
    position = jnp.arange(BLK)
    causal = position[:, None] >= position[None, :]
    log_span = running[:, :, :, None] - running[:, :, None, :]
    decays = jnp.where(causal, jnp.exp(jnp.where(causal, log_span, 0.0)), 0.0)
    scores = jnp.einsum("bin,bjn->bij", c_rows, b_rows, preferred_element_type=jnp.float32)
    weight = (decays * scores[None] * steps_blk[:, :, None, :]).astype(jnp.bfloat16)
    inner_out = jnp.einsum("hbij,bjhp->bihp", weight, inputs, preferred_element_type=jnp.float32)
    tail_decay = jnp.exp(running[:, :, -1:] - running) * steps_blk
    scaled = (jnp.transpose(tail_decay, (1, 2, 0))[:, :, :, None] * inputs).astype(jnp.bfloat16)
    block_state = jnp.einsum("bjhp,bjn->bhpn", scaled, b_rows, preferred_element_type=jnp.float32)
    totals = running[:, :, -1]

    def advance(running_state, element):
        state_here, total_here = element
        return (jnp.exp(total_here)[:, None, None] * running_state + state_here, running_state)

    empty_state = jnp.zeros((head_count, P_SIZE, N), jnp.float32)
    dev_state, local_in = lax.scan(advance, empty_state, (block_state, totals.T))
    dev_log = jnp.sum(totals, axis=1)
    identity = (jnp.zeros((head_count,), jnp.float32), empty_state)
    inner_log, inner_state = carried_in((dev_log, dev_state), "row", combine, identity)
    inclusive = combine((inner_log, inner_state), (dev_log, dev_state))
    group_log, group_state = (
        broadcast(for_sending(inclusive[0]), "row", lax.axis_size("row") - 1),
        broadcast(for_sending(inclusive[1]), "row", lax.axis_size("row") - 1),
    )
    outer = prefix((group_log, group_state), "seq", combine, identity)
    in_log, in_state = combine(outer, (inner_log, inner_state))
    before = jnp.cumsum(totals, axis=1) - totals
    entering = local_in + jnp.exp(before.T)[:, :, None, None] * in_state[None]
    carried_out = jnp.transpose(jnp.exp(running), (1, 2, 0))[:, :, :, None] * jnp.einsum(
        "bin,bhpn->bihp", c_rows.astype(jnp.float32), entering, precision=lax.Precision.HIGHEST
    )
    mixture = inner_out + carried_out + skip[None, None, :, None] * inputs
    hidden = (
        mixture.reshape(tok_count, channels) * jax.nn.silu(gate_in.astype(jnp.float32))
    ).astype(jnp.bfloat16)
    gathered = lax.all_gather(out_weight, ("seq", "row"), axis=0, tiled=True)
    partial_value = lax.dot_general(
        hidden, gathered, (((1,), (1,)), ((), ())), preferred_element_type=jnp.float32
    )
    return lax.psum_scatter(
        partial_value.astype(jnp.bfloat16), "head", scatter_dimension=1, tiled=True
    )


def solution(mesh):
    return jax.shard_map(
        shards,
        mesh=mesh,
        in_specs=(
            P(("seq", "row"), "head"),
            P(("seq", "row"), "head"),
            P(("seq", "row"), None),
            P(("seq", "row"), None),
            P("head", ("seq", "row")),
            P("head", ("seq", "row")),
            P("head"),
            P(("seq", "row"), "head"),
        ),
        out_specs=P(("seq", "row"), "head"),
        check_vma=False,
    )
```

profile of v0, /device:TPU:24, one launch (start us, length us, event | category | flops | bytes accessed | tf_op | source)
XLA Modules:
  0.0 305.4 jit_solution(1515093962028347553)
XLA Ops:
  8.2 1.7 reduce_window_sum.22
  11.0 5.1 %reshape.83 = bf16[6,128,10,128]{3,2,1,0:T(8,128)(2,1)} reshape(bf16[768,1280]{1,0:T(8,128)(2,1)} %param.14) | data formatting | bytes 3932160 | tf_op jit(solution)/shard_map/reshape | solution.py:78
  16.7 5.3 %fusion.16 = f32[6,10,128,128]{3,2,1,0:T(8,128)} fusion(bf16[6,128,128,1]{2,1,3,0:T(8,128)(2,1)S(1)} %bitcast.82, f32[6,128,10]{1,2,0:T(8,128)S(1)} %get-tuple-element.336, bf16[6,128,10,128]{3,2,1,0:T(8,128)(2,1)} %reshape.83), kind=kOutput, calls=%fused_computation.32 | convolution fusion | flops 254607360 | bytes 6125568 | tf_op jit(solution)/shard_map/bjhp,bjn->bhpn/dot_general | solution.py:92
  22.1 12.9 %while.43 = (s32[]{:T(128)}, f32[10,128,128]{2,1,0:T(8,128)S(1)}, f32[6,10,128,128]{3,2,1,0:T(8,128)}, f32[6,10]{1,0:T(8,128)S(1)}, f32[6,10,128,128]{3,2,1,0:T(8,128)}, /*index=5*/s32[]{:T(128)}, s32[]{:T(128)}) while((s32[]{:T(128)}, f32[10,128,128]{2,1,0:T(8,128)S(1)}, f32[6,10,128,128]{3,2,1,0:T(8,128)}, ...), condition=%wide.region_2.3_spmd.clone, body=%wide.region_1.2_spmd.clone.sunk | while | flops 655363 | bytes 3277528 | solution.py:100
  23.0 1.2 bitcast_add_fusion.3
  25.1 1.2 bitcast_add_fusion.3
  27.3 1.2 bitcast_add_fusion.3
  29.5 1.2 bitcast_add_fusion.3
  31.6 1.2 bitcast_add_fusion.3
  33.8 1.2 bitcast_add_fusion.3
  37.4 33.6 %all-reduce = bf16[160]{0:T(256)(128)(2,1)S(1)} all-reduce(bf16[160]{0:T(256)(128)(2,1)S(1)} %dynamic-update-slice), channel_id=2, replica_groups=mesh['seq'=2,'row'=16,'head'=8] {'row'}, use_global_device_ids=true, to_apply=%add | all-reduce | flops 160 | bytes 640
  71.1 29.0 %all-gather.8.cloned.1.call-done = bf16[160,128,128]{2,1,0:T(8,128)(2,1)} async-done(((bf16[10,128,128]{2,1,0:T(8,128)(2,1)}), bf16[160,128,128]{2,1,0:T(8,128)(2,1)}) %all-gather.8.cloned.1.call-update) | async-done | bytes 5242896 | tf_op jit(solution)/shard_map/all_gather | solution.py:14
  100.1 19.0 %while.44 = (s32[]{:T(128)}, f32[10]{0:T(128)S(1)}, f32[10,128,128]{2,1,0:T(8,128)S(1)}, s32[]{:T(128)}, bf16[16,10]{1,0:T(8,128)(2,1)S(1)}, /*index=5*/bf16[16,10,128,128]{3,2,1,0:T(8,128)(2,1)}, s32[]{:T(128)}, s32[]{:T(128)}) while((s32[]{:T(128)}, f32[10]{0:T(128)S(1)}, f32[10,128,128]{2,1,0:T(8,128)S(1)}, s32[]{:T(128)}, ...), condition=%wide.region_6.7_spmd.clone, body=%wide.region_5.6_spmd.clone.sunk | while | flops 819244 | bytes 1638695 | solution.py:31
  100.1 1.3 fusion.46
  101.4 1.1 fusion.46
  102.6 1.1 fusion.46
  103.8 1.1 fusion.46
  105.0 1.1 fusion.46
  106.1 1.1 fusion.46
  107.3 1.1 fusion.46
  108.5 1.1 fusion.46
  120.7 1.9 fusion.36
  122.7 2.4 copy.31
  125.0 32.4 %psum.14 = bf16[1,10]{1,0:T(2,128)(2,1)S(1)} all-reduce(bf16[1,10]{1,0:T(2,128)(2,1)S(1)} %fusion.32), channel_id=1, replica_groups=mesh['seq'=2,'row'=16,'head'=8] {'row'}, use_global_device_ids=true, to_apply=%region_7.8 | all-reduce | flops 10 | bytes 40 | tf_op jit(solution)/shard_map/psum | solution.py:44
  157.4 1.8 all-gather.2
  159.1 57.4 %all-reduce.3.cloned.1.call-done = bf16[1,10,128,128]{3,2,1,0:T(8,128)(2,1)} async-done(((bf16[1,10,128,128]{3,2,1,0:T(8,128)(2,1)}), bf16[1,10,128,128]{3,2,1,0:T(8,128)(2,1)}) %all-reduce.3.cloned.1.call-update) | async-done | bytes 327696 | tf_op jit(solution)/shard_map/psum | solution.py:44
  216.6 2.5 all_gather.31
  219.6 4.9 %fusion.11 = f32[6,10,128,128]{2,3,1,0:T(8,128)S(1)} fusion(bf16[6,128,128,1]{2,1,3,0:T(8,128)(2,1)S(1)} %bitcast.86, f32[6,10,128,128]{3,2,1,0:T(8,128)} %get-tuple-element.237, f32[10,128,128]{2,1,0:T(8,128)S(1)} %multiply_add_fusion, f32[6,10]{1,0:T(8,128)S(1)} %exponential_bitcast_fusion.2), kind=kOutput, calls=%fused_computation.27 | convolution fusion | flops 1511915520 | bytes 8716528 | tf_op jit(solution)/shard_map/bin,bhpn->bihp/dot_general | solution.py:113
  224.5 4.6 %fusion.5 = f32[6,128,10,128]{3,1,2,0:T(8,128)} fusion(f32[6,10,128,128]{2,3,1,0:T(8,128)S(1)} %fusion.11, f32[10]{0:T(128)S(1)} %copy-done.8, f32[6,128,10]{1,2,0:T(8,128)S(1)} %copy-done.6, f32[10,6,128]{2,0,1:T(8,128)S(1)} %copy-done.7, f32[6,128,128]{2,1,0:T(8,128)S(1)} %copy-done.5, f32[10,6,128]{2,0,1:T(8,128)S(1)} %reduce_window_sum.22, ...), kind=kOutput, calls=%fused_computation.20 | convolution fusion | flops 262471680 | bytes 10332200 | tf_op jit(solution)/shard_map/hbij,bjhp->bihp/dot_general | solution.py:89
  229.1 5.8 %copy.30 = f32[6,128,10,128]{1,0,3,2:T(8,128)} copy(f32[6,128,10,128]{3,1,2,0:T(8,128)} %fusion.5) | data formatting | bytes 7864320 | tf_op jit(solution)/shard_map/add | solution.py:116
  234.9 10.5 %convolution_convert_fusion = bf16[768,2560]{0,1:T(8,128)(2,1)} fusion(bf16[2560,1280]{1,0:T(8,128)(2,1)} %all-gather.6.cloned.1.call-done, bf16[768,1280]{0,1:T(8,128)(2,1)S(1)} %copy-done.3, f32[160,8,6,128]{3,2,1,0:T(8,128)} %bitcast.84), kind=kOutput, calls=%fused_computation.14 | convolution fusion | flops 5042012160 | bytes 16384000 | tf_op jit(solution)/shard_map/dot_general | solution.py:121
  245.5 52.8 %reduce-scatter.2.cloned.1.call-done = bf16[768,320]{0,1:T(8,128)(2,1)} async-done(((bf16[768,2560]{0,1:T(8,128)(2,1)}), bf16[768,320]{0,1:T(8,128)(2,1)}) %reduce-scatter.2.cloned.1.call-update) | async-done | bytes 491536 | tf_op jit(solution)/shard_map/reduce_scatter | solution.py:124
  (94 shorter events, 21.7 us)
Async XLA Ops:
  7.4 9.4 %copy-start = (bf16[768,128]{1,0:T(8,128)(2,1)S(1)}, bf16[768,128]{1,0:T(8,128)(2,1)}, u32[]{:S(2)}) copy-start(bf16[768,128]{1,0:T(8,128)(2,1)} %param.16) | copy-start | bytes 589828
  7.4 92.7 %all-gather.8.cloned.1.call-start = ((), (), s32[]{:S(2)}) async-start(), calls=%async_computation.4 | async-start | bytes 5570560 | tf_op jit(solution)/shard_map/all_gather | solution.py:14
  22.1 13.8 %copy-start.9 = (u32[256]{0:T(256)S(1)}, u32[256]{0:T(256)}, u32[]{:S(2)}) copy-start(u32[256]{0:T(256)} %constant.95) | copy-start | bytes 3076
  35.8 180.8 %all-reduce.3.cloned.1.call-start = ((), (), s32[]{:S(2)}) async-start(), calls=%async_computation.1 | async-start | bytes 655360 | tf_op jit(solution)/shard_map/psum | solution.py:44
  100.1 22.6 %copy-start.2 = (bf16[768,1280]{1,0:T(8,128)(2,1)S(1)}, bf16[768,1280]{1,0:T(8,128)(2,1)}, u32[]{:S(2)}) copy-start(bf16[768,1280]{1,0:T(8,128)(2,1)} %param.15) | copy-start | bytes 5898244
  120.0 114.9 %all-gather.6.cloned.1.call-start = ((), (), s32[]{:S(2)}) async-start(), calls=%async_computation.2 | async-start | bytes 6758400 | tf_op jit(solution)/shard_map/all_gather | solution.py:120
  120.6 177.7 %reduce-scatter.2.cloned.1.call-start = ((), (), s32[]{:S(2)}) async-start(), calls=%async_computation.3 | async-start | bytes 4423680 | tf_op jit(solution)/shard_map/reduce_scatter | solution.py:124
  125.0 94.5 %copy-start.4 = (bf16[768,128]{1,0:T(8,128)(2,1)S(1)}, bf16[768,128]{1,0:T(8,128)(2,1)}, u32[]{:S(2)}) copy-start(bf16[768,128]{1,0:T(8,128)(2,1)} %param.17) | copy-start | bytes 589828
  219.5 4.9 %copy-start.1 = (bf16[6,128,10,128]{3,2,1,0:T(8,128)(2,1)S(1)}, bf16[6,128,10,128]{3,2,1,0:T(8,128)(2,1)}, u32[]{:S(2)}) copy-start(bf16[6,128,10,128]{3,2,1,0:T(8,128)(2,1)} %reshape.83) | copy-start | bytes 5898244
  219.5 4.9 %copy-start.5 = (f32[6,128,128]{2,1,0:T(8,128)S(1)}, f32[6,128,128]{2,1,0:T(8,128)}, u32[]{:S(2)}) copy-start(f32[6,128,128]{2,1,0:T(8,128)} %fusion.36) | copy-start | bytes 1179652
  219.6 4.9 %copy-start.6 = (f32[6,128,10]{1,2,0:T(8,128)S(1)}, f32[6,128,10]{1,2,0:T(8,128)}, u32[]{:S(2)}) copy-start(f32[6,128,10]{1,2,0:T(8,128)} %get-tuple-element.335) | copy-start | bytes 92164
  219.6 4.9 %copy-start.7 = (f32[10,6,128]{2,0,1:T(8,128)S(1)}, f32[10,6,128]{2,0,1:T(8,128)}, u32[]{:S(2)}) copy-start(f32[10,6,128]{2,0,1:T(8,128)} %get-tuple-element.337) | copy-start | bytes 92164
  219.6 4.9 %copy-start.8 = (f32[10]{0:T(128)S(1)}, f32[10]{0:T(128)}, u32[]{:S(2)}) copy-start(f32[10]{0:T(128)} %param.20) | copy-start | bytes 124
  229.1 5.8 %copy-start.3 = (bf16[768,1280]{0,1:T(8,128)(2,1)S(1)}, bf16[768,1280]{0,1:T(8,128)(2,1)}, u32[]{:S(2)}) copy-start(bf16[768,1280]{0,1:T(8,128)(2,1)} %copy.31) | copy-start | bytes 5898244
Sparse Core Ops, SparseCore 0:
  35.9 64.1 all-gather.7
  120.1 96.3 all-reduce.2
  245.6 52.6 reduce-scatter.1
Sparse Core Ops, SparseCore 1:
  123.0 53.4 all-gather.5
where the time goes:
time: 308 us; the launch traced here: 305 us
  waiting for transfers between devices  140 us (45%)
  blocking collectives  70.1 us (23%)
  other arithmetic  36.1 us (12%)
  matrix products  27.2 us (9%)
  local copies, waits for them, and re-layouts  16 us (5%)
  between operations  15.4 us (5%)
    psum x1, waiting for transfers between devices, broadcast(): return lax.psum(jnp.where(mine, value, jnp.zeros_like(value)), axis)  57.4 us
    reduce_scatter x1, waiting for transfers between devices, shards(): lax.psum_scatter(partial_value.astype(jnp.bfloat16), 'head', scatter_dime...  52.8 us
    unnamed x1, blocking collectives  33.6 us
    psum x1, blocking collectives, broadcast(): return lax.psum(jnp.where(mine, value, jnp.zeros_like(value)), axis)  32.4 us
    all_gather x1, waiting for transfers between devices, carried_in(): lax.all_gather(part.astype(kind), axis)  29 us
    select_n x16, other arithmetic, carried_turn(): return jax.tree.map(lambda a, b: jnp.where(reached, a, b), new, before)  18.3 us
    dot_general x1, matrix products, shards(): lax.dot_general(hidden, gathered, (((1,), (1,)), ((), ())), preferred_ele...  10.5 us
    add x6, other arithmetic, advance(): jnp.exp(total_here)[:, None, None] * running_state + state_here  7.33 us
  transfers between devices with their start and end apart: 4, of which 3 were waited for; matrix products, arithmetic and copies ran while one was open for 7% of the time, Pallas kernels for 0%

commit v1 on v0

v1 whole, which is shorter than its diff:
```python
import jax
import jax.numpy as jnp
from jax import lax
from jax.experimental import pallas as pl
from jax.experimental.pallas import tpu as pltpu
from jax.sharding import PartitionSpec as P

P_SIZE = 128
N = 128
BLK = 128
TOK = 768
HEADS = 10
CH = HEADS * P_SIZE
HALF = CH // 2
SHARDS = 32
NBLK = TOK // BLK
F32 = jnp.float32
BF16 = jnp.bfloat16
HIGH = lax.Precision.HIGHEST
NT = (((1,), (1,)), ((), ()))
TN = (((0,), (0,)), ((), ()))


def triangle(upto):
    rows = lax.broadcasted_iota(jnp.int32, (BLK, BLK), 0)
    cols = lax.broadcasted_iota(jnp.int32, (BLK, BLK), 1)
    return jnp.where(upto(rows, cols), 1.0, 0.0).astype(F32)


def split3(value):
    high = value.astype(BF16)
    rest = value - high.astype(F32)
    mid = rest.astype(BF16)
    low = (rest - mid.astype(F32)).astype(BF16)
    return high, mid, low


def state_body(x_ref, b_ref, step_ref, log_ref, out_ref):
    half = pl.program_id(0)
    later = triangle(lambda s, t: s > t)
    logs = log_ref[...]
    suffix = jnp.zeros((HEADS, 1), F32)
    pieces = [None] * NBLK
    for k in reversed(range(NBLK)):
        block = logs[:, k * BLK : (k + 1) * BLK]
        within = jnp.dot(block, later, precision=HIGH, preferred_element_type=F32)
        pieces[k] = within + suffix
        suffix = suffix + jnp.sum(block, axis=1, keepdims=True)
    tail = jnp.exp(jnp.concatenate(pieces, axis=1)) * step_ref[...]
    tail = jnp.concatenate([tail, jnp.zeros((16 - HEADS, TOK), F32)], axis=0)
    tail = jnp.transpose(tail)
    first = half == 0
    scaled = []
    for j in range(HEADS // 2):
        factor = jnp.where(first, tail[:, j : j + 1], tail[:, j + 5 : j + 6])
        part = x_ref[:, j * P_SIZE : (j + 1) * P_SIZE].astype(F32)
        scaled.append((factor * part).astype(BF16))
    scaled = jnp.concatenate(scaled, axis=1)
    state = lax.dot_general(b_ref[...], scaled, TN, preferred_element_type=F32)
    state = state.reshape(16, 8, HALF)
    decay = jnp.exp(suffix)
    rows = lax.broadcasted_iota(jnp.int32, (HEADS, P_SIZE), 0)
    cols = lax.broadcasted_iota(jnp.int32, (HEADS, P_SIZE), 1)
    line = jnp.sum(jnp.where(rows == cols, decay, 0.0), axis=0, keepdims=True)
    high, mid, low = (v.astype(F32) for v in split3(line))
    which = lax.broadcasted_iota(jnp.int32, (8, P_SIZE), 0)
    extra = jnp.where(which == 0, high, jnp.where(which == 1, mid, jnp.where(which == 2, low, 0.0)))
    extra = jnp.broadcast_to(extra[None], (16, 8, P_SIZE))
    out_ref[:, 0] = jnp.concatenate([state, extra], axis=2).astype(BF16)


def shard_state(x, b, step, log_gate):
    return pl.pallas_call(
        state_body,
        grid=(2,),
        in_specs=[
            pl.BlockSpec((TOK, HALF), lambda i: (0, i)),
            pl.BlockSpec((TOK, N), lambda i: (0, 0)),
            pl.BlockSpec((HEADS, TOK), lambda i: (0, 0)),
            pl.BlockSpec((HEADS, TOK), lambda i: (0, 0)),
        ],
        out_specs=pl.BlockSpec((16, 1, 8, HALF + P_SIZE), lambda i: (0, i, 0, 0)),
        out_shape=jax.ShapeDtypeStruct((16, 2, 8, HALF + P_SIZE), BF16),
        compiler_params=pltpu.CompilerParams(vmem_limit_bytes=32 << 20),
        cost_estimate=pl.CostEstimate(flops=2 * TOK * N * CH, bytes_accessed=3 << 20, transcendentals=0),
    )(x, b, step, log_gate)


def scan_body(half_ref, in_ref, out_ref, decay_ref):
    lines = in_ref[:, :, HALF:].astype(F32)
    decay = jnp.sum(lines, axis=1)
    rows = lax.broadcasted_iota(jnp.int32, (P_SIZE, HALF), 0)
    cols = lax.broadcasted_iota(jnp.int32, (P_SIZE, HALF), 1)
    spread = jnp.where(rows == cols // P_SIZE + 5 * half_ref[0], 1.0, 0.0).astype(F32)
    decay_ref[...] = jnp.dot(decay, spread, precision=HIGH, preferred_element_type=F32)
    state = jnp.zeros((8, HALF), F32)
    for k in range(SHARDS):
        out_ref[k] = state.astype(BF16)
        state = decay_ref[k : k + 1, :] * state + in_ref[k, :, :HALF].astype(F32)


def scan_shards(half, received):
    return pl.pallas_call(
        scan_body,
        in_specs=[
            pl.BlockSpec(memory_space=pltpu.SMEM),
            pl.BlockSpec(memory_space=pltpu.VMEM),
        ],
        out_specs=pl.BlockSpec(memory_space=pltpu.VMEM),
        out_shape=jax.ShapeDtypeStruct((SHARDS, 8, HALF), BF16),
        scratch_shapes=[pltpu.VMEM((SHARDS, HALF), F32)],
    )(half, received)


def inner_body(x_ref, g_ref, b_ref, c_ref, step_ref, log_ref, skip_ref, pre_ref, gain_ref, state_ref, past_ref):
    k = pl.program_id(0)

    @pl.when(k == 0)
    def _():
        state_ref[...] = jnp.zeros_like(state_ref)
        past_ref[...] = jnp.zeros_like(past_ref)

    logs = log_ref[...]
    steps = step_ref[...]
    upto = triangle(lambda s, t: s <= t)
    running = jnp.dot(logs, upto, precision=HIGH, preferred_element_type=F32)
    total = running[:, BLK - 1 :]
    tail = jnp.exp(total - running) * steps
    pad = jnp.zeros((16 - HEADS, BLK), F32)
    columns = jnp.transpose(jnp.concatenate([running, pad, tail, pad], axis=0))
    past = past_ref[...][:HEADS, :1]
    since = jnp.transpose(jnp.concatenate([jnp.exp(running + past), pad], axis=0))
    b_rows, c_rows = b_ref[...], c_ref[...]
    scores = lax.dot_general(c_rows, b_rows, NT, preferred_element_type=F32)
    rows = lax.broadcasted_iota(jnp.int32, (BLK, BLK), 0)
    cols = lax.broadcasted_iota(jnp.int32, (BLK, BLK), 1)
    causal = rows >= cols
    scores = jnp.where(causal, scores, 0.0)
    grow = jnp.exp(total)
    carried = jnp.dot(c_rows, state_ref[...].astype(BF16), preferred_element_type=F32)
    scaled = []
    for h in range(HEADS):
        here = slice(h * P_SIZE, (h + 1) * P_SIZE)
        run_col = columns[:, h : h + 1]
        span = run_col - running[h : h + 1, :]
        decays = jnp.exp(jnp.where(causal, span, 0.0))
        weight = (decays * scores * steps[h : h + 1, :]).astype(BF16)
        x_here = x_ref[:, here]
        x_wide = x_here.astype(F32)
        out = jnp.dot(weight, x_here, preferred_element_type=F32)
        out = out + jnp.exp(run_col) * carried[:, here] + skip_ref[0, h] * x_wide
        gate = g_ref[:, here].astype(F32)
        silu = gate / (1.0 + jnp.exp(-gate))
        pre_ref[:, here] = out * silu
        gain_ref[:, here] = (silu * since[:, h : h + 1]).astype(BF16)
        scaled.append((columns[:, 16 + h : 17 + h] * x_wide).astype(BF16))
    added = lax.dot_general(b_rows, jnp.concatenate(scaled, axis=1), TN, preferred_element_type=F32)
    for h in range(HEADS):
        here = slice(h * P_SIZE, (h + 1) * P_SIZE)
        state_ref[:, here] = grow[h : h + 1, :] * state_ref[:, here] + added[:, here]
    past_ref[:HEADS, :] = past_ref[:HEADS, :] + total


def inner(x, g, b, c, step, log_gate, skip):
    return pl.pallas_call(
        inner_body,
        grid=(NBLK,),
        in_specs=[
            pl.BlockSpec((BLK, CH), lambda i: (i, 0)),
            pl.BlockSpec((BLK, CH), lambda i: (i, 0)),
            pl.BlockSpec((BLK, N), lambda i: (i, 0)),
            pl.BlockSpec((BLK, N), lambda i: (i, 0)),
            pl.BlockSpec((HEADS, BLK), lambda i: (0, i)),
            pl.BlockSpec((HEADS, BLK), lambda i: (0, i)),
            pl.BlockSpec(memory_space=pltpu.SMEM),
        ],
        out_specs=[
            pl.BlockSpec((BLK, CH), lambda i: (i, 0)),
            pl.BlockSpec((BLK, CH), lambda i: (i, 0)),
        ],
        out_shape=[
            jax.ShapeDtypeStruct((TOK, CH), F32),
            jax.ShapeDtypeStruct((TOK, CH), BF16),
        ],
        scratch_shapes=[pltpu.VMEM((N, CH), F32), pltpu.VMEM((16, BLK), F32)],
        compiler_params=pltpu.CompilerParams(vmem_limit_bytes=32 << 20),
        cost_estimate=pl.CostEstimate(flops=10 * TOK * N * CH, bytes_accessed=10 << 20, transcendentals=3 * TOK * CH),
    )(x, g, b, c, step, log_gate, skip.reshape(1, HEADS))


def hidden_body(c_ref, in_ref, pre_ref, gain_ref, out_ref):
    c_rows = c_ref[...]
    for half in range(2):
        here = slice(half * HALF, (half + 1) * HALF)
        state = in_ref[:, half].astype(F32).reshape(N, HALF).astype(BF16)
        carried = jnp.dot(c_rows, state, preferred_element_type=F32)
        out_ref[:, here] = (pre_ref[:, here] + gain_ref[:, here].astype(F32) * carried).astype(BF16)


def hidden_of(c, entering, pre, gain):
    return pl.pallas_call(
        hidden_body,
        grid=(3,),
        in_specs=[
            pl.BlockSpec((256, N), lambda i: (i, 0)),
            pl.BlockSpec((16, 2, 8, HALF), lambda i: (0, 0, 0, 0)),
            pl.BlockSpec((256, CH), lambda i: (i, 0)),
            pl.BlockSpec((256, CH), lambda i: (i, 0)),
        ],
        out_specs=pl.BlockSpec((256, CH), lambda i: (i, 0)),
        out_shape=jax.ShapeDtypeStruct((TOK, CH), BF16),
        compiler_params=pltpu.CompilerParams(vmem_limit_bytes=32 << 20),
        cost_estimate=pl.CostEstimate(flops=2 * TOK * N * CH, bytes_accessed=8 << 20, transcendentals=0),
    )(c, entering, pre, gain)


def shift(value, axis, by):
    size = lax.axis_size(axis)
    return lax.ppermute(value, axis, [(i, (i + by) % size) for i in range(size)])


def summed_over_head(hidden, weights):
    groups = lax.axis_size("head")
    mine = lax.axis_index("head")
    width = weights.shape[0] // groups

    def part(group, half):
        start = lax.rem(mine + group + groups, groups) * width + half * (width // 2)
        rows = lax.dynamic_slice_in_dim(weights, start, width // 2, 0)
        return lax.dot_general(hidden, rows, NT, preferred_element_type=F32)

    far = groups // 2
    first = [(1, 0, far), (-1, 1, far)]
    second = [(1, 1, far - 1), (-1, 0, far - 1)]
    flying = {}
    for hop in range(far, 0, -1):
        for streams in (first, second):
            for way, half, start in streams:
                if hop > start:
                    continue
                value = part(way * hop, half)
                if hop < start:
                    value = value + flying[way, half].astype(F32)
                flying[way, half] = shift(value.astype(BF16), "head", way)
    halves = [part(0, half) + flying[1, half].astype(F32) + flying[-1, half].astype(F32) for half in range(2)]
    return jnp.concatenate(halves, axis=1).astype(BF16)


def shards(x, g, b, c, step, log_gate, skip, out_weight):
    weights = lax.all_gather(out_weight, ("seq", "row"), axis=0, tiled=True)
    payload = shard_state(x, b, step, log_gate).reshape(SHARDS, 8, HALF + P_SIZE)
    received = lax.all_to_all(payload, ("seq", "row"), 0, 0)
    pre, gain = inner(x, g, b, c, step, log_gate, skip)
    half = lax.rem(lax.axis_index("row"), 2).reshape(1)
    entering = lax.all_to_all(scan_shards(half, received), ("seq", "row"), 0, 0)
    hidden = hidden_of(c, entering.reshape(16, 2, 8, HALF), pre, gain)
    return summed_over_head(hidden, weights)


def solution(mesh):
    return jax.shard_map(
        shards,
        mesh=mesh,
        in_specs=(
            P(("seq", "row"), "head"),
            P(("seq", "row"), "head"),
            P(("seq", "row"), None),
            P(("seq", "row"), None),
            P("head", ("seq", "row")),
            P("head", ("seq", "row")),
            P("head"),
            P(("seq", "row"), "head"),
        ),
        out_specs=P(("seq", "row"), "head"),
        check_vma=False,
    )
```

time: 308 us -> 131 us (0.43)
  the two profiles are of different devices: /device:TPU:24 before, /device:TPU:96 now
where the time goes in v1:
time: 131 us
  starting transfers between devices  35.4 us (27%)
  waiting for transfers between devices  34.9 us (27%)
  Pallas kernels  16.7 us (13%)
  matrix products  15.1 us (12%)
  between operations  13.8 us (11%)
  local copies, waits for them, and re-layouts  13.5 us (10%)
    ppermute x14, starting transfers between devices, shift(): lax.ppermute(value, axis, [(i, (i + by) % size) for i in range(size)])  24.2 us
    dot_general x16, matrix products, part(): return lax.dot_general(hidden, rows, NT, preferred_element_type=F32)  15.1 us
    ppermute x14, waiting for transfers between devices, shift(): lax.ppermute(value, axis, [(i, (i + by) % size) for i in range(size)])  14.7 us
    unnamed x34, local copies, waits for them, and re-layouts  13.5 us
    all_to_all x1, waiting for transfers between devices, shards(): received = lax.all_to_all(payload, ('seq', 'row'), 0, 0)  12.1 us
    pallas_call x1, Pallas kernels, inner(): pl.pallas_call(inner_body, grid=(NBLK,), in_specs=[pl.BlockSpec((BLK, CH)...  9.54 us
    all_gather x1, waiting for transfers between devices, shards(): weights = lax.all_gather(out_weight, ('seq', 'row'), axis=0, tiled=True)  7.35 us
    all_to_all x1, starting transfers between devices, shards(): received = lax.all_to_all(payload, ('seq', 'row'), 0, 0)  7.32 us
  transfers between devices with their start and end apart: 17, of which 9 were waited for; matrix products, arithmetic and copies ran while one was open for 10% of the time, Pallas kernels for 13%

profile of v1, /device:TPU:96, one launch (start us, length us, event | category | flops | bytes accessed | tf_op | source)
XLA Modules:
  0.0 130.6 jit_solution(14350105336954531500)
XLA Ops:
  7.3 1.5 %copy-done.2 = bf16[768,1280]{1,0:T(8,128)(2,1)S(1)} copy-done((bf16[768,1280]{1,0:T(8,128)(2,1)S(1)}, bf16[768,1280]{1,0:T(8,128)(2,1)}, u32[]{:S(2)}) %copy-start.2) | copy-done | bytes 1966104
  8.8 0.9 copy-done.6
  11.4 3.9 %shard_map.82 = bf16[16,2,8,768]{3,2,1,0:T(8,128)(2,1)} custom-call(bf16[768,1280]{1,0:T(8,128)(2,1)S(1)} %copy-done.2, bf16[768,128]{1,0:T(8,128)(2,1)S(1)} %copy-done.6, f32[10,768]{1,0:T(8,128)S(1)} %copy-done.9, f32[10,768]{1,0:T(8,128)S(1)} %copy-done.11), custom_call_target="tpu_custom_call" | custom-call | flops 251658240 | bytes 3145728 | tf_op jit(solution)/shard_map/pallas_call | solution.py:73
  15.3 7.3 %all-to-all-start = ((bf16[32,8,768]{2,1,0:T(8,128)(2,1)}), bf16[32,8,768]{2,1,0:T(8,128)(2,1)S(1)}, u32[]{:S(2)}, u32[]{:S(2)}) async-start(bf16[32,8,768]{2,1,0:T(8,128)(2,1)} %bitcast.1), calls=%async_computation | async-start | bytes 786432 | tf_op jit(solution)/shard_map/all_to_all | solution.py:252
  22.6 12.1 %all-to-all-done.in_ref = bf16[32,8,768]{2,1,0:T(8,128)(2,1)S(1)} async-done(((bf16[32,8,768]{2,1,0:T(8,128)(2,1)}), bf16[32,8,768]{2,1,0:T(8,128)(2,1)S(1)}, u32[]{:S(2)}, u32[]{:S(2)}) %all-to-all-start) | async-done | bytes 393248 | tf_op jit(solution)/shard_map/all_to_all | solution.py:252
  35.5 2.2 %shard_map.83 = bf16[32,8,640]{2,1,0:T(8,128)(2,1)} custom-call(s32[1]{0:T(128)} %bitcast.half_ref, bf16[32,8,768]{2,1,0:T(8,128)(2,1)} %copy-done.16), custom_call_target="tpu_custom_call" | custom-call | tf_op jit(solution)/shard_map/pallas_call | solution.py:103
  37.7 3.9 %all-to-all-start.1 = ((bf16[32,8,640]{2,1,0:T(8,128)(2,1)}), bf16[32,8,640]{2,1,0:T(8,128)(2,1)S(1)}, u32[]{:S(2)}, u32[]{:S(2)}) async-start(bf16[32,8,640]{2,1,0:T(8,128)(2,1)} %shard_map.83), calls=%async_computation.1 | async-start | bytes 655360 | tf_op jit(solution)/shard_map/all_to_all | solution.py:255
  41.8 1.5 %copy-done.13 = bf16[768,1280]{1,0:T(8,128)(2,1)S(1)} copy-done((bf16[768,1280]{1,0:T(8,128)(2,1)S(1)}, bf16[768,1280]{1,0:T(8,128)(2,1)}, u32[]{:S(2)}) %copy-start.13) | copy-done | bytes 1966104
  43.3 9.5 %shard_map.84 = (f32[768,1280]{1,0:T(8,128)S(1)}, bf16[768,1280]{1,0:T(8,128)(2,1)S(1)}) custom-call(bf16[768,1280]{1,0:T(8,128)(2,1)S(1)} %copy-done.3, bf16[768,1280]{1,0:T(8,128)(2,1)S(1)} %copy-done.13, bf16[768,128]{1,0:T(8,128)(2,1)S(1)} %copy-done.7, bf16[768,128]{1,0:T(8,128)(2,1)S(1)} %copy-done.8, f32[10,768]{1,0:T(8,128)S(1)} %copy-done.10, ...), custom_call_target="tpu_custom_call" | custom-call | flops 1258291200 | bytes 10485760 | tf_op jit(solution)/shard_map/pallas_call | solution.py:165
  52.8 2.0 %copy-done = f32[768,1280]{1,0:T(8,128)} copy-done((f32[768,1280]{1,0:T(8,128)}, f32[768,1280]{1,0:T(8,128)S(1)}, u32[]{:S(2)}) %copy-start) | copy-done | bytes 3932184
  54.8 1.3 %copy-done.4 = bf16[768,1280]{1,0:T(8,128)(2,1)} copy-done((bf16[768,1280]{1,0:T(8,128)(2,1)}, bf16[768,1280]{1,0:T(8,128)(2,1)S(1)}, u32[]{:S(2)}) %copy-start.4) | copy-done | bytes 1966104
  56.2 2.2 %copy-done.1 = f32[768,1280]{1,0:T(8,128)S(1)} copy-done((f32[768,1280]{1,0:T(8,128)S(1)}, f32[768,1280]{1,0:T(8,128)}, u32[]{:S(2)}) %copy-start.1) | copy-done | bytes 3932184
  58.4 1.6 %copy-done.5 = bf16[768,1280]{1,0:T(8,128)(2,1)S(1)} copy-done((bf16[768,1280]{1,0:T(8,128)(2,1)S(1)}, bf16[768,1280]{1,0:T(8,128)(2,1)}, u32[]{:S(2)}) %copy-start.5) | copy-done | bytes 1966104
  60.0 1.0 shard_map.85
  61.0 7.3 %all-gather.2.cloned.1.call-done = bf16[2560,1280]{1,0:T(8,128)(2,1)} async-done(((bf16[80,1280]{1,0:T(8,128)(2,1)}), bf16[2560,1280]{1,0:T(8,128)(2,1)}) %all-gather.2.cloned.1.call-update) | async-done | bytes 6553616 | tf_op jit(solution)/shard_map/all_gather | solution.py:250
  68.4 2.0 %convolution_convert_fusion.3 = bf16[768,160]{0,1:T(8,128)(2,1)S(1)} fusion(bf16[768,1280]{1,0:T(8,128)(2,1)S(1)} %shard_map.85, bf16[2560,1280]{1,0:T(8,128)(2,1)} %all-gather.2.cloned.1.call-done, s32[]{:T(128)S(6)} %select_n.52), kind=kOutput, calls=%fused_computation.3 | convolution fusion | flops 314695680 | bytes 2621444 | tf_op jit(solution)/shard_map/dot_general | solution.py:230
  70.3 2.8 %collective-permute-start = (bf16[768,160]{0,1:T(8,128)(2,1)S(1)}, bf16[768,160]{0,1:T(8,128)(2,1)S(1)}, u32[]{:S(2)}, u32[]{:S(2)}) collective-permute-start(bf16[768,160]{0,1:T(8,128)(2,1)S(1)} %convolution_convert_fusion.3), channel_id=1, source_target_pairs={{0,1},{1,2},{2,3},{3,4},{4,5},{5,6},{6,7},{7,0},{8,9},{9,10},{10,1... | collective-permute-start | bytes 737288 | tf_op jit(solution)/shard_map/ppermute | solution.py:219
  73.1 1.8 %convolution_convert_fusion.2 = bf16[768,160]{0,1:T(8,128)(2,1)S(1)} fusion(bf16[768,1280]{1,0:T(8,128)(2,1)S(1)} %shard_map.85, bf16[2560,1280]{1,0:T(8,128)(2,1)} %all-gather.2.cloned.1.call-done, s32[]{:T(128)S(6)} %select_n.55), kind=kOutput, calls=%fused_computation.2 | convolution fusion | flops 314695680 | bytes 2621444 | tf_op jit(solution)/shard_map/dot_general | solution.py:230
  75.8 3.3 %collective-permute-start.7 = (bf16[768,160]{0,1:T(8,128)(2,1)S(1)}, bf16[768,160]{0,1:T(8,128)(2,1)S(1)}, u32[]{:S(2)}, u32[]{:S(2)}) collective-permute-start(bf16[768,160]{0,1:T(8,128)(2,1)S(1)} %convolution_convert_fusion.1), channel_id=1, source_target_pairs={{0,1},{1,2},{2,3},{3,4},{4,5},{5,6},{6,7},{7,0},{8,9},{9,10},{10,1... | collective-permute-start | bytes 737288 | tf_op jit(solution)/shard_map/ppermute | solution.py:219
  81.8 0.8 fusion.23
  83.4 0.8 fusion.14
  85.0 0.8 fusion.7
  86.6 0.8 add_convert_fusion.11
  87.4 3.3 %collective-permute-start.1 = (bf16[768,160]{0,1:T(8,128)(2,1)S(1)}, bf16[768,160]{0,1:T(8,128)(2,1)S(1)}, u32[]{:S(2)}, u32[]{:S(2)}) collective-permute-start(bf16[768,160]{0,1:T(8,128)(2,1)S(1)} %add_convert_fusion.11), channel_id=1, source_target_pairs={{0,1},{1,2},{2,3},{3,4},{4,5},{5,6},{6,7},{7,0},{8,9},{9,10},{10,1... | collective-permute-start | bytes 737288 | tf_op jit(solution)/shard_map/ppermute | solution.py:219
  92.5 3.3 %collective-permute-start.8 = (bf16[768,160]{0,1:T(8,128)(2,1)S(1)}, bf16[768,160]{0,1:T(8,128)(2,1)S(1)}, u32[]{:S(2)}, u32[]{:S(2)}) collective-permute-start(bf16[768,160]{0,1:T(8,128)(2,1)S(1)} %add_convert_fusion.5), channel_id=1, source_target_pairs={{0,1},{1,2},{2,3},{3,4},{4,5},{5,6},{6,7},{7,0},{8,9},{9,10},{10,1... | collective-permute-start | bytes 737288 | tf_op jit(solution)/shard_map/ppermute | solution.py:219
  96.7 3.3 %collective-permute-start.2 = (bf16[768,160]{0,1:T(8,128)(2,1)S(1)}, bf16[768,160]{0,1:T(8,128)(2,1)S(1)}, u32[]{:S(2)}, u32[]{:S(2)}) collective-permute-start(bf16[768,160]{0,1:T(8,128)(2,1)S(1)} %add_convert_fusion.10), channel_id=1, source_target_pairs={{0,1},{1,2},{2,3},{3,4},{4,5},{5,6},{6,7},{7,0},{8,9},{9,10},{10,1... | collective-permute-start | bytes 737288 | tf_op jit(solution)/shard_map/ppermute | solution.py:219
  100.4 1.7 %collective-permute-done.8 = bf16[768,160]{0,1:T(8,128)(2,1)S(1)} collective-permute-done((bf16[768,160]{0,1:T(8,128)(2,1)S(1)}, bf16[768,160]{0,1:T(8,128)(2,1)S(1)}, u32[]{:S(2)}, u32[]{:S(2)}) %collective-permute-start.8) | collective-permute-done | bytes 245792 | tf_op jit(solution)/shard_map/ppermute | solution.py:219
  102.2 3.8 %collective-permute-start.9 = (bf16[768,160]{0,1:T(8,128)(2,1)S(1)}, bf16[768,160]{0,1:T(8,128)(2,1)S(1)}, u32[]{:S(2)}, u32[]{:S(2)}) collective-permute-start(bf16[768,160]{0,1:T(8,128)(2,1)S(1)} %add_convert_fusion.4), channel_id=1, source_target_pairs={{0,1},{1,2},{2,3},{3,4},{4,5},{5,6},{6,7},{7,0},{8,9},{9,10},{10,1... | collective-permute-start | bytes 737288 | tf_op jit(solution)/shard_map/ppermute | solution.py:219
  107.5 3.8 %collective-permute-start.3 = (bf16[768,160]{0,1:T(8,128)(2,1)S(1)}, bf16[768,160]{0,1:T(8,128)(2,1)S(1)}, u32[]{:S(2)}, u32[]{:S(2)}) collective-permute-start(bf16[768,160]{0,1:T(8,128)(2,1)S(1)} %add_convert_fusion.9), channel_id=1, source_target_pairs={{0,1},{1,2},{2,3},{3,4},{4,5},{5,6},{6,7},{7,0},{8,9},{9,10},{10,1... | collective-permute-start | bytes 737288 | tf_op jit(solution)/shard_map/ppermute | solution.py:219
  111.2 4.1 %collective-permute-done.12 = bf16[768,160]{0,1:T(8,128)(2,1)S(1)} collective-permute-done((bf16[768,160]{0,1:T(8,128)(2,1)S(1)}, bf16[768,160]{0,1:T(8,128)(2,1)S(1)}, u32[]{:S(2)}, u32[]{:S(2)}) %collective-permute-start.12) | collective-permute-done | bytes 245792 | tf_op jit(solution)/shard_map/ppermute | solution.py:219
  116.4 6.5 %collective-permute-done.13 = bf16[768,160]{0,1:T(8,128)(2,1)S(1)} collective-permute-done((bf16[768,160]{0,1:T(8,128)(2,1)S(1)}, bf16[768,160]{0,1:T(8,128)(2,1)S(1)}, u32[]{:S(2)}, u32[]{:S(2)}) %collective-permute-start.13) | collective-permute-done | bytes 245792 | tf_op jit(solution)/shard_map/ppermute | solution.py:219
  123.0 0.8 pad_maximum_fusion
  (66 shorter events, 14.8 us)
Async XLA Ops:
  6.5 61.8 %all-gather.2.cloned.1.call-start = ((), (), s32[]{:S(2)}) async-start(), calls=%async_computation.2 | async-start | bytes 6758400 | tf_op jit(solution)/shard_map/all_gather | solution.py:250
  7.3 1.5 %copy-start.2 = (bf16[768,1280]{1,0:T(8,128)(2,1)S(1)}, bf16[768,1280]{1,0:T(8,128)(2,1)}, u32[]{:S(2)}) copy-start(bf16[768,1280]{1,0:T(8,128)(2,1)} %x_ref.3) | copy-start | bytes 5898244
  8.8 0.9 copy-start.6
  9.7 0.8 copy-start.9
  11.3 30.4 %copy-start.3 = (bf16[768,1280]{1,0:T(8,128)(2,1)S(1)}, bf16[768,1280]{1,0:T(8,128)(2,1)}, u32[]{:S(2)}) copy-start(bf16[768,1280]{1,0:T(8,128)(2,1)} %x_ref.3) | copy-start | bytes 5898244
  11.3 30.4 %copy-start.7 = (bf16[768,128]{1,0:T(8,128)(2,1)S(1)}, bf16[768,128]{1,0:T(8,128)(2,1)}, u32[]{:S(2)}) copy-start(bf16[768,128]{1,0:T(8,128)(2,1)} %b_ref.3) | copy-start | bytes 589828
  11.3 30.4 %copy-start.8 = (bf16[768,128]{1,0:T(8,128)(2,1)S(1)}, bf16[768,128]{1,0:T(8,128)(2,1)}, u32[]{:S(2)}) copy-start(bf16[768,128]{1,0:T(8,128)(2,1)} %c_ref.3) | copy-start | bytes 589828
  11.3 30.4 %copy-start.10 = (f32[10,768]{1,0:T(8,128)S(1)}, f32[10,768]{1,0:T(8,128)}, u32[]{:S(2)}) copy-start(f32[10,768]{1,0:T(8,128)} %step_ref.3) | copy-start | bytes 92164
  11.3 30.4 %copy-start.12 = (f32[10,768]{1,0:T(8,128)S(1)}, f32[10,768]{1,0:T(8,128)}, u32[]{:S(2)}) copy-start(f32[10,768]{1,0:T(8,128)} %log_ref.3) | copy-start | bytes 92164
  11.3 30.4 %copy-start.14 = (f32[10]{0:T(128)S(1)}, f32[10]{0:T(128)}, u32[]{:S(2)}) copy-start(f32[10]{0:T(128)} %param.14) | copy-start | bytes 124
  15.3 19.4 %all-to-all-start = ((bf16[32,8,768]{2,1,0:T(8,128)(2,1)}), bf16[32,8,768]{2,1,0:T(8,128)(2,1)S(1)}, u32[]{:S(2)}, u32[]{:S(2)}) async-start(bf16[32,8,768]{2,1,0:T(8,128)(2,1)} %bitcast.1), calls=%async_computation | async-start | bytes 786432 | tf_op jit(solution)/shard_map/all_to_all | solution.py:252
  37.7 18.5 %all-to-all-start.1 = ((bf16[32,8,640]{2,1,0:T(8,128)(2,1)}), bf16[32,8,640]{2,1,0:T(8,128)(2,1)S(1)}, u32[]{:S(2)}, u32[]{:S(2)}) async-start(bf16[32,8,640]{2,1,0:T(8,128)(2,1)} %shard_map.83), calls=%async_computation.1 | async-start | bytes 655360 | tf_op jit(solution)/shard_map/all_to_all | solution.py:255
  41.7 1.5 %copy-start.13 = (bf16[768,1280]{1,0:T(8,128)(2,1)S(1)}, bf16[768,1280]{1,0:T(8,128)(2,1)}, u32[]{:S(2)}) copy-start(bf16[768,1280]{1,0:T(8,128)(2,1)} %g_ref.1) | copy-start | bytes 5898244
  52.8 2.0 %copy-start = (f32[768,1280]{1,0:T(8,128)}, f32[768,1280]{1,0:T(8,128)S(1)}, u32[]{:S(2)}) copy-start(f32[768,1280]{1,0:T(8,128)S(1)} %get-tuple-element.7.pre_ref) | copy-start | bytes 11796484
  54.8 1.3 %copy-start.4 = (bf16[768,1280]{1,0:T(8,128)(2,1)}, bf16[768,1280]{1,0:T(8,128)(2,1)S(1)}, u32[]{:S(2)}) copy-start(bf16[768,1280]{1,0:T(8,128)(2,1)S(1)} %get-tuple-element.8.gain_ref) | copy-start | bytes 5898244
  56.2 2.3 %copy-start.1 = (f32[768,1280]{1,0:T(8,128)S(1)}, f32[768,1280]{1,0:T(8,128)}, u32[]{:S(2)}) copy-start(f32[768,1280]{1,0:T(8,128)} %copy-done) | copy-start | bytes 11796484
  58.4 1.6 %copy-start.5 = (bf16[768,1280]{1,0:T(8,128)(2,1)S(1)}, bf16[768,1280]{1,0:T(8,128)(2,1)}, u32[]{:S(2)}) copy-start(bf16[768,1280]{1,0:T(8,128)(2,1)} %copy-done.4) | copy-start | bytes 5898244
  68.4 6.6 %copy-start.15 = (bf16[2560,1280]{1,0:T(8,128)(2,1)S(1)}, bf16[2560,1280]{1,0:T(8,128)(2,1)}, u32[]{:S(2)}) copy-start(bf16[2560,1280]{1,0:T(8,128)(2,1)} %all-gather.2.cloned.1.call-done) | copy-start | bytes 19660804
  70.3 16.3 %collective-permute-start = (bf16[768,160]{0,1:T(8,128)(2,1)S(1)}, bf16[768,160]{0,1:T(8,128)(2,1)S(1)}, u32[]{:S(2)}, u32[]{:S(2)}) collective-permute-start(bf16[768,160]{0,1:T(8,128)(2,1)S(1)} %convolution_convert_fusion.3), channel_id=1, source_target_pairs={{0,1},{1,2},{2,3},{3,4},{4,5},{5,6},{6,7},{7,0},{8,9},{9,10},{10,1... | collective-permute-start | bytes 737288 | tf_op jit(solution)/shard_map/ppermute | solution.py:219
  74.9 15.9 %collective-permute-start.4 = (bf16[768,160]{0,1:T(8,128)(2,1)S(1)}, bf16[768,160]{0,1:T(8,128)(2,1)S(1)}, u32[]{:S(2)}, u32[]{:S(2)}) collective-permute-start(bf16[768,160]{0,1:T(8,128)(2,1)S(1)} %convolution_convert_fusion.2), channel_id=1, source_target_pairs={{0,7},{1,0},{2,1},{3,2},{4,3},{5,4},{6,5},{7,6},{8,15},{9,8},{10,9... | collective-permute-start | bytes 737288 | tf_op jit(solution)/shard_map/ppermute | solution.py:219
  75.8 15.8 %collective-permute-start.7 = (bf16[768,160]{0,1:T(8,128)(2,1)S(1)}, bf16[768,160]{0,1:T(8,128)(2,1)S(1)}, u32[]{:S(2)}, u32[]{:S(2)}) collective-permute-start(bf16[768,160]{0,1:T(8,128)(2,1)S(1)} %convolution_convert_fusion.1), channel_id=1, source_target_pairs={{0,1},{1,2},{2,3},{3,4},{4,5},{5,6},{6,7},{7,0},{8,9},{9,10},{10,1... | collective-permute-start | bytes 737288 | tf_op jit(solution)/shard_map/ppermute | solution.py:219
  79.9 15.9 %collective-permute-start.10 = (bf16[768,160]{0,1:T(8,128)(2,1)S(1)}, bf16[768,160]{0,1:T(8,128)(2,1)S(1)}, u32[]{:S(2)}, u32[]{:S(2)}) collective-permute-start(bf16[768,160]{0,1:T(8,128)(2,1)S(1)} %convolution_convert_fusion), channel_id=1, source_target_pairs={{0,7},{1,0},{2,1},{3,2},{4,3},{5,4},{6,5},{7,6},{8,15},{9,8},{10,9... | collective-permute-start | bytes 737288 | tf_op jit(solution)/shard_map/ppermute | solution.py:219
  87.4 9.2 %collective-permute-start.1 = (bf16[768,160]{0,1:T(8,128)(2,1)S(1)}, bf16[768,160]{0,1:T(8,128)(2,1)S(1)}, u32[]{:S(2)}, u32[]{:S(2)}) collective-permute-start(bf16[768,160]{0,1:T(8,128)(2,1)S(1)} %add_convert_fusion.11), channel_id=1, source_target_pairs={{0,1},{1,2},{2,3},{3,4},{4,5},{5,6},{6,7},{7,0},{8,9},{9,10},{10,1... | collective-permute-start | bytes 737288 | tf_op jit(solution)/shard_map/ppermute | solution.py:219
  91.6 8.7 %collective-permute-start.5 = (bf16[768,160]{0,1:T(8,128)(2,1)S(1)}, bf16[768,160]{0,1:T(8,128)(2,1)S(1)}, u32[]{:S(2)}, u32[]{:S(2)}) collective-permute-start(bf16[768,160]{0,1:T(8,128)(2,1)S(1)} %add_convert_fusion.8), channel_id=1, source_target_pairs={{0,7},{1,0},{2,1},{3,2},{4,3},{5,4},{6,5},{7,6},{8,15},{9,8},{10,9... | collective-permute-start | bytes 737288 | tf_op jit(solution)/shard_map/ppermute | solution.py:219
  92.5 9.7 %collective-permute-start.8 = (bf16[768,160]{0,1:T(8,128)(2,1)S(1)}, bf16[768,160]{0,1:T(8,128)(2,1)S(1)}, u32[]{:S(2)}, u32[]{:S(2)}) collective-permute-start(bf16[768,160]{0,1:T(8,128)(2,1)S(1)} %add_convert_fusion.5), channel_id=1, source_target_pairs={{0,1},{1,2},{2,3},{3,4},{4,5},{5,6},{6,7},{7,0},{8,9},{9,10},{10,1... | collective-permute-start | bytes 737288 | tf_op jit(solution)/shard_map/ppermute | solution.py:219
  96.6 10.2 %collective-permute-start.11 = (bf16[768,160]{0,1:T(8,128)(2,1)S(1)}, bf16[768,160]{0,1:T(8,128)(2,1)S(1)}, u32[]{:S(2)}, u32[]{:S(2)}) collective-permute-start(bf16[768,160]{0,1:T(8,128)(2,1)S(1)} %add_convert_fusion.3), channel_id=1, source_target_pairs={{0,7},{1,0},{2,1},{3,2},{4,3},{5,4},{6,5},{7,6},{8,15},{9,8},{10,9... | collective-permute-start | bytes 737288 | tf_op jit(solution)/shard_map/ppermute | solution.py:219
  96.7 10.7 %collective-permute-start.2 = (bf16[768,160]{0,1:T(8,128)(2,1)S(1)}, bf16[768,160]{0,1:T(8,128)(2,1)S(1)}, u32[]{:S(2)}, u32[]{:S(2)}) collective-permute-start(bf16[768,160]{0,1:T(8,128)(2,1)S(1)} %add_convert_fusion.10), channel_id=1, source_target_pairs={{0,1},{1,2},{2,3},{3,4},{4,5},{5,6},{6,7},{7,0},{8,9},{9,10},{10,1... | collective-permute-start | bytes 737288 | tf_op jit(solution)/shard_map/ppermute | solution.py:219
  100.3 15.2 %collective-permute-start.6 = (bf16[768,160]{0,1:T(8,128)(2,1)S(1)}, bf16[768,160]{0,1:T(8,128)(2,1)S(1)}, u32[]{:S(2)}, u32[]{:S(2)}) collective-permute-start(bf16[768,160]{0,1:T(8,128)(2,1)S(1)} %add_convert_fusion.7), channel_id=1, source_target_pairs={{0,7},{1,0},{2,1},{3,2},{4,3},{5,4},{6,5},{7,6},{8,15},{9,8},{10,9... | collective-permute-start | bytes 737288 | tf_op jit(solution)/shard_map/ppermute | solution.py:219
  102.2 14.2 %collective-permute-start.9 = (bf16[768,160]{0,1:T(8,128)(2,1)S(1)}, bf16[768,160]{0,1:T(8,128)(2,1)S(1)}, u32[]{:S(2)}, u32[]{:S(2)}) collective-permute-start(bf16[768,160]{0,1:T(8,128)(2,1)S(1)} %add_convert_fusion.4), channel_id=1, source_target_pairs={{0,1},{1,2},{2,3},{3,4},{4,5},{5,6},{6,7},{7,0},{8,9},{9,10},{10,1... | collective-permute-start | bytes 737288 | tf_op jit(solution)/shard_map/ppermute | solution.py:219
  106.8 8.5 %collective-permute-start.12 = (bf16[768,160]{0,1:T(8,128)(2,1)S(1)}, bf16[768,160]{0,1:T(8,128)(2,1)S(1)}, u32[]{:S(2)}, u32[]{:S(2)}) collective-permute-start(bf16[768,160]{0,1:T(8,128)(2,1)S(1)} %add_convert_fusion.2), channel_id=1, source_target_pairs={{0,7},{1,0},{2,1},{3,2},{4,3},{5,4},{6,5},{7,6},{8,15},{9,8},{10,9... | collective-permute-start | bytes 737288 | tf_op jit(solution)/shard_map/ppermute | solution.py:219
  107.5 8.8 %collective-permute-start.3 = (bf16[768,160]{0,1:T(8,128)(2,1)S(1)}, bf16[768,160]{0,1:T(8,128)(2,1)S(1)}, u32[]{:S(2)}, u32[]{:S(2)}) collective-permute-start(bf16[768,160]{0,1:T(8,128)(2,1)S(1)} %add_convert_fusion.9), channel_id=1, source_target_pairs={{0,1},{1,2},{2,3},{3,4},{4,5},{5,6},{6,7},{7,0},{8,9},{9,10},{10,1... | collective-permute-start | bytes 737288 | tf_op jit(solution)/shard_map/ppermute | solution.py:219
  115.4 7.5 %collective-permute-start.13 = (bf16[768,160]{0,1:T(8,128)(2,1)S(1)}, bf16[768,160]{0,1:T(8,128)(2,1)S(1)}, u32[]{:S(2)}, u32[]{:S(2)}) collective-permute-start(bf16[768,160]{0,1:T(8,128)(2,1)S(1)} %add_convert_fusion.1), channel_id=1, source_target_pairs={{0,7},{1,0},{2,1},{3,2},{4,3},{5,4},{6,5},{7,6},{8,15},{9,8},{10,9... | collective-permute-start | bytes 737288 | tf_op jit(solution)/shard_map/ppermute | solution.py:219
  (2 other events, 1.5 us)
Sparse Core Ops, SparseCore 0:
  9.9 58.4 all-gather.1

commit v2 on v1

v2 whole, which is shorter than its diff:
```python
import functools

import jax
import jax.numpy as jnp
from jax import lax
from jax.experimental import pallas as pl
from jax.experimental.pallas import tpu as pltpu
from jax.sharding import PartitionSpec as P

P_SIZE = 128
N = 128
BLK = 128
TOK = 768
HEADS = 10
CH = HEADS * P_SIZE
HALF = CH // 2
SHARDS = 32
ROWS = 80
PIECE = 160
NBLK = TOK // BLK
F32 = jnp.float32
BF16 = jnp.bfloat16
HIGH = lax.Precision.HIGHEST
IN_VMEM = pl.BlockSpec(memory_space=pltpu.VMEM)
IN_SMEM = pl.BlockSpec(memory_space=pltpu.SMEM)
ANYWHERE = pl.BlockSpec(memory_space=pl.ANY)
SMALL = pltpu.CompilerParams(vmem_limit_bytes=24 << 20)
NT = (((1,), (1,)), ((), ()))
TN = (((0,), (0,)), ((), ()))


def in_vmem(value):
    return pltpu.with_memory_space_constraint(value, pltpu.VMEM)


def in_hbm(value):
    return pltpu.with_memory_space_constraint(value, pltpu.HBM)


def triangle(upto):
    rows = lax.broadcasted_iota(jnp.int32, (BLK, BLK), 0)
    cols = lax.broadcasted_iota(jnp.int32, (BLK, BLK), 1)
    return jnp.where(upto(rows, cols), 1.0, 0.0).astype(F32)


def split3(value):
    high = value.astype(BF16)
    rest = value - high.astype(F32)
    mid = rest.astype(BF16)
    low = (rest - mid.astype(F32)).astype(BF16)
    return high, mid, low


def state_body(x_ref, b_ref, step_ref, log_ref, out_ref, tail_ref, decay_ref, turned_ref):
    half = pl.program_id(0)

    @pl.when(half == 0)
    def _():
        pad = jnp.zeros((16 - HEADS, BLK), F32)
        logs = log_ref[...]
        stacked = jnp.concatenate(
            [v for k in range(NBLK) for v in (logs[:, k * BLK : (k + 1) * BLK], pad)], axis=0
        )
        within = jnp.dot(stacked, triangle(lambda s, t: s > t), precision=HIGH, preferred_element_type=F32)
        sums = jnp.sum(stacked, axis=1, keepdims=True)
        suffix = jnp.zeros((16, 1), F32)
        pieces = [None] * NBLK
        for k in reversed(range(NBLK)):
            pieces[k] = within[16 * k : 16 * (k + 1)] + suffix
            suffix = suffix + sums[16 * k : 16 * (k + 1)]
        tail_ref[...] = jnp.exp(jnp.concatenate(pieces, axis=1)[:HEADS]) * step_ref[...]
        turned_ref[...] = jnp.transpose(b_ref[...].astype(F32))
        decay_ref[...] = jnp.broadcast_to(jnp.exp(suffix), (16, P_SIZE))

    turned = turned_ref[...]
    parts = []
    for j in range(HEADS // 2):
        row = tail_ref[pl.ds(half * (HEADS // 2) + j, 1), :]
        scaled = (turned * row).astype(BF16)
        here = slice(j * P_SIZE, (j + 1) * P_SIZE)
        parts.append(jnp.dot(scaled, x_ref[:, here], preferred_element_type=F32))
    state = jnp.concatenate(parts, axis=1).reshape(16, 8, HALF)
    rows = lax.broadcasted_iota(jnp.int32, (16, P_SIZE), 0)
    cols = lax.broadcasted_iota(jnp.int32, (16, P_SIZE), 1)
    line = jnp.sum(jnp.where(rows == cols, decay_ref[...], 0.0), axis=0, keepdims=True)
    high, mid, low = (v.astype(F32) for v in split3(line))
    which = lax.broadcasted_iota(jnp.int32, (8, P_SIZE), 0)
    extra = jnp.where(which == 0, high, jnp.where(which == 1, mid, jnp.where(which == 2, low, 0.0)))
    extra = jnp.broadcast_to(extra[None], (16, 8, P_SIZE))
    out_ref[:, 0] = jnp.concatenate([state, extra], axis=2).astype(BF16)


def shard_state(x, b, step, log_gate):
    return pl.pallas_call(
        state_body,
        grid=(2,),
        in_specs=[
            pl.BlockSpec((TOK, HALF), lambda i: (0, i)),
            pl.BlockSpec((TOK, N), lambda i: (0, 0)),
            pl.BlockSpec((HEADS, TOK), lambda i: (0, 0)),
            pl.BlockSpec((HEADS, TOK), lambda i: (0, 0)),
        ],
        out_specs=pl.BlockSpec((16, 1, 8, HALF + P_SIZE), lambda i: (0, i, 0, 0)),
        out_shape=jax.ShapeDtypeStruct((16, 2, 8, HALF + P_SIZE), BF16),
        scratch_shapes=[pltpu.VMEM((HEADS, TOK), F32), pltpu.VMEM((16, P_SIZE), F32), pltpu.VMEM((N, TOK), F32)],
        compiler_params=SMALL,
        cost_estimate=pl.CostEstimate(flops=2 * TOK * N * CH, bytes_accessed=3 << 20, transcendentals=0),
    )(*[in_hbm(v) for v in (x, b, step, log_gate)])


def scan_body(half_ref, in_ref, out_ref, decay_ref):
    lines = in_ref[:, :, HALF:].astype(F32)
    decay = jnp.sum(lines, axis=1)
    rows = lax.broadcasted_iota(jnp.int32, (P_SIZE, HALF), 0)
    cols = lax.broadcasted_iota(jnp.int32, (P_SIZE, HALF), 1)
    spread = jnp.where(rows == cols // P_SIZE + 5 * half_ref[0], 1.0, 0.0).astype(F32)
    decay_ref[...] = jnp.dot(decay, spread, precision=HIGH, preferred_element_type=F32)
    state = jnp.zeros((8, HALF), F32)
    for k in range(SHARDS):
        out_ref[k] = state.astype(BF16)
        state = decay_ref[k : k + 1, :] * state + in_ref[k, :, :HALF].astype(F32)


def scan_shards(half, received):
    return pl.pallas_call(
        scan_body,
        in_specs=[
            pl.BlockSpec(memory_space=pltpu.SMEM),
            pl.BlockSpec(memory_space=pltpu.VMEM),
        ],
        out_specs=pl.BlockSpec(memory_space=pltpu.VMEM),
        out_shape=jax.ShapeDtypeStruct((SHARDS, 8, HALF), BF16),
        scratch_shapes=[pltpu.VMEM((SHARDS, HALF), F32)],
        compiler_params=SMALL,
    )(half, received)


def inner_body(x_ref, g_ref, b_ref, c_ref, step_ref, log_ref, skip_ref, start_ref, before_ref, pre_ref, gain_ref, keep_ref, state_ref, past_ref):
    k = pl.program_id(0)
    tokens = pl.ds(pl.multiple_of(k * BLK, BLK), BLK)

    @pl.when(k == 0)
    def _():
        state_ref[...] = start_ref[...]
        past_ref[...] = before_ref[...]

    keep_ref[tokens, :] = c_ref[...]
    logs = log_ref[...]
    steps = step_ref[...]
    upto = triangle(lambda s, t: s <= t)
    running = jnp.dot(logs, upto, precision=HIGH, preferred_element_type=F32)
    total = running[:, BLK - 1 :]
    tail = jnp.exp(total - running) * steps
    past = past_ref[...][:HEADS, :]
    pad = jnp.zeros((16 - HEADS, BLK), F32)
    columns = jnp.transpose(
        jnp.concatenate([running, pad, jnp.exp(running), pad, jnp.exp(running + past), pad], axis=0)
    )
    b_rows, c_rows = b_ref[...], c_ref[...]
    turned = jnp.transpose(b_rows.astype(F32))
    c_wide = c_rows.astype(F32)
    scores = lax.dot_general(c_rows, b_rows, NT, preferred_element_type=F32)
    rows = lax.broadcasted_iota(jnp.int32, (BLK, BLK), 0)
    cols = lax.broadcasted_iota(jnp.int32, (BLK, BLK), 1)
    causal = rows >= cols
    scores = jnp.where(causal, scores, 0.0)
    grow = jnp.exp(total)
    for h in range(HEADS):
        here = slice(h * P_SIZE, (h + 1) * P_SIZE)
        span = columns[:, h : h + 1] - running[h : h + 1, :]
        decays = jnp.exp(jnp.where(causal, span, 0.0))
        weight = (decays * scores * steps[h : h + 1, :]).astype(BF16)
        reach = (columns[:, 16 + h : 17 + h] * c_wide).astype(BF16)
        x_here = x_ref[:, here]
        state = state_ref[:, here]
        out = jnp.dot(
            jnp.concatenate([weight, reach], axis=1),
            jnp.concatenate([x_here, state.astype(BF16)], axis=0),
            preferred_element_type=F32,
        )
        out = out + skip_ref[0, h] * x_here.astype(F32)
        gate = g_ref[:, here].astype(F32)
        silu = 0.5 * gate * (1.0 + jnp.tanh(0.5 * gate))
        pre_ref[tokens, here] = out * silu
        gain_ref[tokens, here] = (silu * columns[:, 32 + h : 33 + h]).astype(BF16)
        scaled = (turned * tail[h : h + 1, :]).astype(BF16)
        state_ref[:, here] = grow[h : h + 1, :] * state + jnp.dot(scaled, x_here, preferred_element_type=F32)
    past_ref[:HEADS, :] = past_ref[:HEADS, :] + total


def inner(x, g, b, c, step, log_gate, skip, first, state, past):
    count = NBLK // 2
    rows = count * BLK
    return pl.pallas_call(
        inner_body,
        grid=(count,),
        in_specs=[
            pl.BlockSpec((BLK, CH), lambda i: (i + first, 0)),
            pl.BlockSpec((BLK, CH), lambda i: (i + first, 0)),
            pl.BlockSpec((BLK, N), lambda i: (i + first, 0)),
            pl.BlockSpec((BLK, N), lambda i: (i + first, 0)),
            pl.BlockSpec((HEADS, BLK), lambda i: (0, i + first)),
            pl.BlockSpec((HEADS, BLK), lambda i: (0, i + first)),
            IN_SMEM,
            IN_VMEM,
            IN_VMEM,
        ],
        out_specs=[IN_VMEM] * 5,
        out_shape=[
            pltpu.VMEM((rows, CH), F32),
            pltpu.VMEM((rows, CH), BF16),
            pltpu.VMEM((rows, N), BF16),
            jax.ShapeDtypeStruct((N, CH), F32),
            jax.ShapeDtypeStruct((16, BLK), F32),
        ],
        compiler_params=SMALL,
        cost_estimate=pl.CostEstimate(flops=1 << 20, bytes_accessed=1 << 20, transcendentals=0),
    )(*[in_hbm(v) for v in (x, g, b, c, step, log_gate)], skip.reshape(1, HEADS), state, past)


def fetch(table, refs, held, sems, chunks):
    for slot, chunk in enumerate(chunks):
        for j in range(4):
            array = table[8 * chunk + 2 * j]
            block = table[8 * chunk + 2 * j + 1]
            for k, ref in enumerate(refs):

                @pl.when(array == k)
                def _(ref=ref, block=block, slot=slot, j=j):
                    pltpu.make_async_copy(ref.at[block], held.at[slot, j], sems.at[slot, j]).start()


def arrive(refs, held, sems):
    for slot in range(held.shape[0]):
        for j in range(4):
            pltpu.make_async_copy(refs[0].at[0], held.at[slot, j], sems.at[slot, j]).wait()


def product(held, slot, hidden):
    rows = held[slot].reshape(4 * ROWS, CH)
    return lax.dot_general(rows, hidden, NT, preferred_element_type=F32).astype(BF16)


def held_weights(count):
    return pltpu.VMEM((count, 4, ROWS, CH), BF16)


def first_body(table, in_ref, *refs):
    parts, refs, (hidden_ref, up_ref, down_ref, later, held, sems, later_sems) = refs[:6], refs[6:14], refs[14:]
    rows = TOK // 2
    fetch(table, refs, held, sems, (0,))
    fetch(table, refs, later, later_sems, (1, 2))
    states = [in_ref[:, half].astype(F32).reshape(N, HALF).astype(BF16) for half in range(2)]
    for i in range(2):
        here = slice(i * rows, (i + 1) * rows)
        pre_ref, gain_ref, c_ref = parts[3 * i : 3 * i + 3]
        for half in range(2):
            cols = slice(half * HALF, (half + 1) * HALF)
            carried = jnp.dot(c_ref[...], states[half], preferred_element_type=F32)
            hidden_ref[here, cols] = (pre_ref[:, cols] + gain_ref[:, cols].astype(F32) * carried).astype(BF16)
        if i == 0:
            arrive(refs, held, sems)
        out = product(held, 0, hidden_ref[here, :])
        up_ref[:, here] = out[:PIECE]
        down_ref[:, here] = out[PIECE:]
    arrive(refs, later, later_sems)


def first_parts(table, entering, parts, blocks):
    return pl.pallas_call(
        first_body,
        in_specs=[IN_SMEM] + [IN_VMEM] * 7 + [ANYWHERE] * 8,
        out_specs=[IN_VMEM] * 4,
        out_shape=[pltpu.VMEM((TOK, CH), BF16)] + [jax.ShapeDtypeStruct((PIECE, TOK), BF16)] * 2 + [held_weights(2)],
        scratch_shapes=[held_weights(1), pltpu.SemaphoreType.DMA((1, 4)), pltpu.SemaphoreType.DMA((2, 4))],
        compiler_params=SMALL,
        cost_estimate=pl.CostEstimate(flops=2 * 320 * TOK * CH, bytes_accessed=2 << 20, transcendentals=0),
    )(table, entering, *[in_vmem(v) for v in parts], *[in_hbm(v) for v in blocks])


def near_body(chunks, table, hidden_ref, held, *refs):
    refs, (up_ref, down_ref, keep_ref, later, sems) = refs[:8], refs[8:]
    fetch(table, refs, later, sems, chunks)
    out = product(held, 0, hidden_ref[...])
    up_ref[...] = out[PIECE:]
    keep_ref[0] = out[:PIECE]
    out = product(held, 1, hidden_ref[...])
    down_ref[...] = out[:PIECE]
    keep_ref[1] = out[PIECE:]
    arrive(refs, later, sems)


def near_parts(table, hidden, held, blocks, chunks):
    return pl.pallas_call(
        functools.partial(near_body, chunks),
        in_specs=[IN_SMEM, IN_VMEM, IN_VMEM] + [ANYWHERE] * 8,
        out_specs=[IN_VMEM] * 4,
        out_shape=[jax.ShapeDtypeStruct((PIECE, TOK), BF16)] * 2
        + [jax.ShapeDtypeStruct((2, PIECE, TOK), BF16), held_weights(len(chunks))],
        scratch_shapes=[pltpu.SemaphoreType.DMA((len(chunks), 4))],
        compiler_params=SMALL,
        cost_estimate=pl.CostEstimate(flops=4 * 320 * TOK * CH, bytes_accessed=2 << 20, transcendentals=0),
    )(table, in_vmem(hidden), in_vmem(held), *[in_hbm(v) for v in blocks])


def rest_body(chunks, table, hidden_ref, held, *refs):
    refs, (out_ref, *scratch) = refs[:8], refs[8:]
    if chunks:
        later, sems = scratch
        fetch(table, refs, later, sems, chunks)
    for slot in range(held.shape[0]):
        out_ref[slot] = product(held, slot, hidden_ref[...]).reshape(2, PIECE, TOK)
    if chunks:
        arrive(refs, later, sems)


def rest_parts(table, hidden, held, blocks, chunks):
    count, later = held.shape[0], len(chunks)
    return pl.pallas_call(
        functools.partial(rest_body, chunks),
        in_specs=[IN_SMEM, IN_VMEM, IN_VMEM] + [ANYWHERE] * 8,
        out_specs=[IN_VMEM] * (2 if later else 1),
        out_shape=[jax.ShapeDtypeStruct((count, 2, PIECE, TOK), BF16)] + ([held_weights(later)] if later else []),
        scratch_shapes=[pltpu.SemaphoreType.DMA((later, 4))] if later else [],
        compiler_params=SMALL,
        cost_estimate=pl.CostEstimate(flops=2 * count * 320 * TOK * CH, bytes_accessed=count << 20, transcendentals=0),
    )(table, in_vmem(hidden), in_vmem(held), *[in_hbm(v) for v in blocks])


def shift(value, axis, by):
    size = lax.axis_size(axis)
    return lax.ppermute(value, axis, [(i, (i + by) % size) for i in range(size)])


def after(value, earlier):
    return lax.optimization_barrier((value, earlier))[0]


def add(a, b):
    return (a.astype(F32) + b.astype(F32)).astype(BF16)


def place(seq, y, x):
    return seq * 16 + y * 4 + x


def from_line(value, stage, offset):
    pairs = []
    for seq in range(2):
        for y in range(4):
            for x in range(4):
                if (seq == 0) == (stage == 0):
                    source = place(seq, y, (x + offset) % 4)
                else:
                    source = place(seq, (y + offset) % 4, x)
                pairs.append((source, place(seq, y, x)))
    return lax.ppermute(value, ("seq", "row"), pairs)


def line_body(own, one, two, three, out):
    for k, part in enumerate((own, one, two, three)):
        out[k] = part[...]


def line_of(*parts):
    return pl.pallas_call(
        line_body,
        in_specs=[IN_VMEM] * 4,
        out_specs=IN_VMEM,
        out_shape=pltpu.HBM((4, ROWS, CH), BF16),
        compiler_params=SMALL,
    )(*parts)


def weight_table(order):
    seq, row, head = (lax.axis_index(name) for name in ("seq", "row", "head"))
    group = lax.rem(head + jnp.array(order, jnp.int32) + 8, 8)[:, None]
    source = group // 4
    right = lax.rem(jnp.arange(4, dtype=jnp.int32)[None, :] - lax.rem(row, 4) + 4, 4)
    down = lax.rem(group % 4 - row // 4 + 4, 4)
    down, right = jnp.broadcast_arrays(down, right)
    array = jnp.where(source == seq, 0, 4) + jnp.where(source == 0, down, right)
    block = jnp.where(source == 0, right, down)
    return jnp.stack([array, block], axis=2).astype(jnp.int32).reshape(-1)


def projected(entering, parts, blocks):
    table = weight_table((4, 3, -3, 2, -2, 1, -1, 0))
    hidden, ua, db, held = first_parts(table, entering, parts, blocks)
    ua, db = shift(ua, "head", 1), shift(db, "head", -1)
    ub, da, keep, held = near_parts(table, hidden, held, blocks, (3, 4))
    ub, da = shift(ub, "head", 1), shift(da, "head", -1)
    two, held = rest_parts(table, hidden, held, blocks, (5, 6, 7))
    sent = add(keep[0], after(ua, two))
    ua = shift(sent, "head", 1)
    sent = add(keep[1], after(db, sent))
    db = shift(sent, "head", -1)
    (one,) = rest_parts(table, after(hidden, sent), held, blocks, ())
    sent = add(two[0, 1], after(ub, one))
    ub = shift(sent, "head", 1)
    sent = add(two[1, 0], after(da, sent))
    da = shift(sent, "head", -1)
    sent = add(two[0, 0], after(ua, sent))
    ua = shift(sent, "head", 1)
    sent = add(two[1, 1], after(db, sent))
    db = shift(sent, "head", -1)
    sent = add(one[0, 1], after(ub, sent))
    ub = shift(sent, "head", 1)
    sent = add(one[1, 0], after(da, sent))
    da = shift(sent, "head", -1)
    sent = add(one[0, 0], after(ua, sent))
    ua = shift(sent, "head", 1)
    sent = add(one[1, 1], after(db, sent))
    db = shift(sent, "head", -1)
    up = jnp.concatenate([ua, ub]).astype(F32)
    down = jnp.concatenate([da, db]).astype(F32)
    return (one[2].reshape(2 * PIECE, TOK).astype(F32) + up + down).T.astype(BF16)


def shards(x, g, b, c, step, log_gate, skip, out_weight):
    near = [from_line(out_weight, 0, offset) for offset in (1, 2, 3)]
    payload = shard_state(x, b, step, log_gate).reshape(SHARDS, 8, HALF + P_SIZE)
    payload, near = lax.optimization_barrier((payload, near))
    received = lax.all_to_all(payload, ("seq", "row"), 0, 0)
    nothing = (jnp.zeros((N, CH), F32), jnp.zeros((16, BLK), F32))
    *early, state, past = inner(after(x, payload), g, b, c, step, log_gate, skip, 0, *nothing)
    line = line_of(out_weight, *near)
    one, two, three = (from_line(line, 1, offset) for offset in (1, 2, 3))
    half = lax.rem(lax.axis_index("row"), 2).reshape(1)
    slices = scan_shards(half, after(received, past))
    entering = lax.all_to_all(slices, ("seq", "row"), 0, 0)
    *late, _, past = inner(after(x, slices), g, b, c, step, log_gate, skip, NBLK // 2, state, past)
    mine = [line, one, two, three]
    other = [shift(v, "seq", 1) for v in [line] + after(mine[1:], past)]
    return projected(entering.reshape(16, 2, 8, HALF), early + late, mine + other)


def solution(mesh):
    return jax.shard_map(
        shards,
        mesh=mesh,
        in_specs=(
            P(("seq", "row"), "head"),
            P(("seq", "row"), "head"),
            P(("seq", "row"), None),
            P(("seq", "row"), None),
            P("head", ("seq", "row")),
            P("head", ("seq", "row")),
            P("head"),
            P(("seq", "row"), "head"),
        ),
        out_specs=P(("seq", "row"), "head"),
        check_vma=False,
    )
```

time: 131 us -> 120 us (0.916)
  the two profiles are of different devices: /device:TPU:96 before, /device:TPU:24 now
where the time goes in v2:
time: 120 us; the launch traced here: 119 us
  starting transfers between devices  46.1 us (38%)
  waiting for transfers between devices  35 us (29%)
  Pallas kernels  29 us (24%)
  local copies, waits for them, and re-layouts  7.23 us (6%)
  other arithmetic  1.71 us (1%)
    ppermute x18, starting transfers between devices, shift(): lax.ppermute(value, axis, [(i, (i + by) % size) for i in range(size)])  25.3 us
    ppermute x6, waiting for transfers between devices, from_line(): return lax.ppermute(value, ('seq', 'row'), pairs)  20.4 us
    ppermute x18, waiting for transfers between devices, shift(): lax.ppermute(value, axis, [(i, (i + by) % size) for i in range(size)])  14.6 us
    pallas_call x2, Pallas kernels, inner(): pl.pallas_call(inner_body, grid=(count,), in_specs=[pl.BlockSpec((BLK, CH...  10.6 us
    ppermute x6, starting transfers between devices, from_line(): return lax.ppermute(value, ('seq', 'row'), pairs)  7.86 us
    unnamed x18, local copies, waits for them, and re-layouts  6.94 us
    all_to_all x1, starting transfers between devices, shards(): received = lax.all_to_all(payload, ('seq', 'row'), 0, 0)  6.85 us
    pallas_call x2, Pallas kernels, rest_parts(): pl.pallas_call(functools.partial(rest_body, chunks), in_specs=[IN_SMEM, I...  6.19 us
  transfers between devices with their start and end apart: 26, of which 12 were waited for; matrix products, arithmetic and copies ran while one was open for 1% of the time, Pallas kernels for 20%

profile of v2, /device:TPU:24, one launch (start us, length us, event | category | flops | bytes accessed | tf_op | source)
XLA Modules:
  0.0 119.4 jit_solution(6717643448730136017)
XLA Ops:
  0.0 3.0 %collective-permute-start.1 = (bf16[80,1280]{1,0:T(8,128)(2,1)}, bf16[80,1280]{1,0:T(8,128)(2,1)S(1)}, u32[]{:S(2)}, u32[]{:S(2)}) collective-permute-start(bf16[80,1280]{1,0:T(8,128)(2,1)} %own.1), channel_id=1, source_target_pairs={{16,0},{24,8},{0,16},{8,24},{48,32},{56,40},{32,48},{40,56},{80,64... | collective-permute-start | bytes 614408 | tf_op jit(solution)/shard_map/ppermute | solution.py:357
  5.1 3.0 %shard_map.91 = bf16[16,2,8,768]{3,2,1,0:T(8,128)(2,1)} custom-call(bf16[768,1280]{1,0:T(8,128)(2,1)} %x_ref.3, bf16[768,128]{1,0:T(8,128)(2,1)} %b_ref.5, f32[10,768]{1,0:T(8,128)} %step_ref.5, f32[10,768]{1,0:T(8,128)} %log_ref.5), custom_call_target="tpu_custom_call" | custom-call | flops 251658240 | bytes 3145728 | tf_op jit(solution)/shard_map/pallas_call | solution.py:94
  8.0 1.7 %collective-permute-done.one = bf16[80,1280]{1,0:T(8,128)(2,1)S(1)} collective-permute-done((bf16[80,1280]{1,0:T(8,128)(2,1)}, bf16[80,1280]{1,0:T(8,128)(2,1)S(1)}, u32[]{:S(2)}, u32[]{:S(2)}) %collective-permute-start) | collective-permute-done | bytes 204832 | tf_op jit(solution)/shard_map/ppermute | solution.py:357
  9.8 1.6 %collective-permute-done.2.three = bf16[80,1280]{1,0:T(8,128)(2,1)S(1)} collective-permute-done((bf16[80,1280]{1,0:T(8,128)(2,1)}, bf16[80,1280]{1,0:T(8,128)(2,1)S(1)}, u32[]{:S(2)}, u32[]{:S(2)}) %collective-permute-start.2) | collective-permute-done | bytes 204832 | tf_op jit(solution)/shard_map/ppermute | solution.py:357
  12.6 2.5 %collective-permute-start.4 = (bf16[4,80,1280]{2,1,0:T(8,128)(2,1)}, bf16[4,80,1280]{2,1,0:T(8,128)(2,1)}, u32[]{:S(2)}, u32[]{:S(2)}) collective-permute-start(bf16[4,80,1280]{2,1,0:T(8,128)(2,1)} %shard_map.95.refs_6_.refs_0_), channel_id=1, source_target_pairs={{64,0},{72,8},{80,16},{88,24},{96,32},{104,40},{112,48},{120,56},{... | collective-permute-start | bytes 2457608 | tf_op jit(solution)/shard_map/ppermute | solution.py:357
  15.2 6.9 %all-to-all-start = ((bf16[32,8,768]{2,1,0:T(8,128)(2,1)}), bf16[32,8,768]{2,1,0:T(8,128)(2,1)S(1)}, u32[]{:S(2)}, u32[]{:S(2)}) async-start(bf16[32,8,768]{2,1,0:T(8,128)(2,1)} %bitcast.1), calls=%async_computation | async-start | bytes 786432 | tf_op jit(solution)/shard_map/all_to_all | solution.py:424
  22.1 3.4 %collective-permute-done.5.refs_9_.refs_3_ = bf16[4,80,1280]{2,1,0:T(8,128)(2,1)} collective-permute-done((bf16[4,80,1280]{2,1,0:T(8,128)(2,1)}, bf16[4,80,1280]{2,1,0:T(8,128)(2,1)}, u32[]{:S(2)}, u32[]{:S(2)}) %collective-permute-start.5) | collective-permute-done | bytes 819232 | tf_op jit(solution)/shard_map/ppermute | solution.py:357
  25.5 2.1 %collective-permute-done.4.refs_8_.refs_2_ = bf16[4,80,1280]{2,1,0:T(8,128)(2,1)} collective-permute-done((bf16[4,80,1280]{2,1,0:T(8,128)(2,1)}, bf16[4,80,1280]{2,1,0:T(8,128)(2,1)}, u32[]{:S(2)}, u32[]{:S(2)}) %collective-permute-start.4) | collective-permute-done | bytes 819232 | tf_op jit(solution)/shard_map/ppermute | solution.py:357
  27.6 11.6 %collective-permute-done.3.refs_7_.refs_1_ = bf16[4,80,1280]{2,1,0:T(8,128)(2,1)} collective-permute-done((bf16[4,80,1280]{2,1,0:T(8,128)(2,1)}, bf16[4,80,1280]{2,1,0:T(8,128)(2,1)}, u32[]{:S(2)}, u32[]{:S(2)}) %collective-permute-start.3) | collective-permute-done | bytes 819232 | tf_op jit(solution)/shard_map/ppermute | solution.py:357
  39.8 5.0 %shard_map.92 = (f32[384,1280]{1,0:T(8,128)S(1)}, bf16[384,1280]{1,0:T(8,128)(2,1)S(1)}, bf16[384,128]{1,0:T(8,128)(2,1)S(1)}, f32[128,1280]{1,0:T(8,128)S(1)}, f32[16,128]{1,0:T(8,128)S(1)}) custom-call(bf16[768,1280]{1,0:T(8,128)(2,1)} %x_ref.3, bf16[768,1280]{1,0:T(8,128)(2,1)} %g_ref.3, bf16[768,128]{1,0:T(8,128)(2,1)} %b_ref.5, bf16[768,128]{1,0:T(8,128)(2,1)} %c_ref.3, ...), custom_call_target="tpu_custom_call" | custom-call | flops 1048576 | bytes 1048576 | tf_op jit(solution)/shard_map/pallas_call | solution.py:194
  46.8 6.1 %all-to-all-start.1 = ((bf16[32,8,640]{2,1,0:T(8,128)(2,1)}), bf16[32,8,640]{2,1,0:T(8,128)(2,1)S(1)}, u32[]{:S(2)}, u32[]{:S(2)}) async-start(bf16[32,8,640]{2,1,0:T(8,128)(2,1)} %shard_map.93), calls=%async_computation.1 | async-start | bytes 655360 | tf_op jit(solution)/shard_map/all_to_all | solution.py:431
  54.3 5.6 %shard_map.94 = (f32[384,1280]{1,0:T(8,128)S(1)}, bf16[384,1280]{1,0:T(8,128)(2,1)S(1)}, bf16[384,128]{1,0:T(8,128)(2,1)S(1)}, f32[128,1280]{1,0:T(8,128)}, f32[16,128]{1,0:T(8,128)}) custom-call(bf16[768,1280]{1,0:T(8,128)(2,1)} %x_ref.3, bf16[768,1280]{1,0:T(8,128)(2,1)} %g_ref.3, bf16[768,128]{1,0:T(8,128)(2,1)} %b_ref.5, bf16[768,128]{1,0:T(8,128)(2,1)} %c_ref.3, ...), custom_call_target="tpu_custom_call" | custom-call | flops 1048576 | bytes 1048576 | tf_op jit(solution)/shard_map/pallas_call | solution.py:194
  60.0 1.3 %copy-done = f32[384,1280]{1,0:T(8,128)} copy-done((f32[384,1280]{1,0:T(8,128)}, f32[384,1280]{1,0:T(8,128)S(1)}, u32[]{:S(2)}) %copy-start) | copy-done | bytes 1966104
  62.3 1.5 %copy-done.1 = f32[384,1280]{1,0:T(8,128)S(1)} copy-done((f32[384,1280]{1,0:T(8,128)S(1)}, f32[384,1280]{1,0:T(8,128)}, u32[]{:S(2)}) %copy-start.1) | copy-done | bytes 1966104
  65.0 3.9 %shard_map.96 = (bf16[768,1280]{1,0:T(8,128)(2,1)S(1)}, bf16[160,768]{1,0:T(8,128)(2,1)S(1)}, bf16[160,768]{1,0:T(8,128)(2,1)S(1)}, bf16[2,4,80,1280]{3,2,1,0:T(8,128)(2,1)S(1)}) custom-call(s32[64]{0:T(128)S(1)} %reshape.245.table, bf16[16,2,8,640]{3,2,1,0:T(8,128)(2,1)S(1)} %bitcast.47, f32[384,1280]{1,0:T(8,128)S(1)} %get-tuple-element.48.refs_0_, ...), custom_call_target="tpu_custom_call" | custom-call | flops 629145600 | bytes 2097152 | tf_op jit(solution)/shard_map/pallas_call | solution.py:270
  68.9 2.0 %collective-permute-start.11 = (bf16[160,768]{1,0:T(8,128)(2,1)S(1)}, bf16[160,768]{1,0:T(8,128)(2,1)S(1)}, u32[]{:S(2)}, u32[]{:S(2)}) collective-permute-start(bf16[160,768]{1,0:T(8,128)(2,1)S(1)} %get-tuple-element.66), channel_id=1, source_target_pairs={{0,1},{1,2},{2,3},{3,4},{4,5},{5,6},{6,7},{7,0},{8,9},{9,10},{10,1... | collective-permute-start | bytes 737288 | tf_op jit(solution)/shard_map/ppermute | solution.py:332
  70.9 4.0 %collective-permute-start.10 = (bf16[160,768]{1,0:T(8,128)(2,1)S(1)}, bf16[160,768]{1,0:T(8,128)(2,1)S(1)}, u32[]{:S(2)}, u32[]{:S(2)}) collective-permute-start(bf16[160,768]{1,0:T(8,128)(2,1)S(1)} %get-tuple-element.65), channel_id=1, source_target_pairs={{0,7},{1,0},{2,1},{3,2},{4,3},{5,4},{6,5},{7,6},{8,15},{9,8},{10,9... | collective-permute-start | bytes 737288 | tf_op jit(solution)/shard_map/ppermute | solution.py:332
  74.9 3.2 %shard_map.97 = (bf16[160,768]{1,0:T(8,128)(2,1)S(1)}, bf16[160,768]{1,0:T(8,128)(2,1)S(1)}, bf16[2,160,768]{2,1,0:T(8,128)(2,1)S(1)}, bf16[2,4,80,1280]{3,2,1,0:T(8,128)(2,1)S(1)}) custom-call(s32[64]{0:T(128)S(1)} %reshape.245.table, bf16[768,1280]{1,0:T(8,128)(2,1)S(1)} %get-tuple-element.71.hidden_ref, ...), custom_call_target="tpu_custom_call" | custom-call | flops 1258291200 | bytes 2097152 | tf_op jit(solution)/shard_map/pallas_call | solution.py:294
  78.1 2.0 %collective-permute-start.13 = (bf16[160,768]{1,0:T(8,128)(2,1)S(1)}, bf16[160,768]{1,0:T(8,128)(2,1)S(1)}, u32[]{:S(2)}, u32[]{:S(2)}) collective-permute-start(bf16[160,768]{1,0:T(8,128)(2,1)S(1)} %get-tuple-element.73), channel_id=1, source_target_pairs={{0,7},{1,0},{2,1},{3,2},{4,3},{5,4},{6,5},{7,6},{8,15},{9,8},{10,9... | collective-permute-start | bytes 737288 | tf_op jit(solution)/shard_map/ppermute | solution.py:332
  80.2 3.5 %shard_map.98 = (bf16[2,2,160,768]{3,2,1,0:T(8,128)(2,1)S(1)}, bf16[3,4,80,1280]{3,2,1,0:T(8,128)(2,1)S(1)}) custom-call(s32[64]{0:T(128)S(1)} %reshape.245.table, bf16[768,1280]{1,0:T(8,128)(2,1)S(1)} %get-tuple-element.71.hidden_ref, bf16[2,4,80,1280]{3,2,1,0:T(8,128)(2,1)S(1)} %get-tuple-element.67.held, bf16[4,80,1280]{2,1,0:T(8,128)(2,1)} %shard_map.95.refs_6_.refs_0_, ...), custom_call_target="tpu_custom_call" | custom-call | flops 1258291200 | bytes 2097152 | tf_op jit(solution)/shard_map/pallas_call | solution.py:319
  83.9 3.2 %collective-permute-start.18 = (bf16[160,768]{1,0:T(8,128)(2,1)S(1)}, bf16[160,768]{1,0:T(8,128)(2,1)S(1)}, u32[]{:S(2)}, u32[]{:S(2)}) collective-permute-start(bf16[160,768]{1,0:T(8,128)(2,1)S(1)} %fusion.12), channel_id=1, source_target_pairs={{0,7},{1,0},{2,1},{3,2},{4,3},{5,4},{6,5},{7,6},{8,15},{9,8},{10,9... | collective-permute-start | bytes 737288 | tf_op jit(solution)/shard_map/ppermute | solution.py:332
  87.2 2.6 %shard_map.99 = bf16[3,2,160,768]{3,2,1,0:T(8,128)(2,1)S(1)} custom-call(s32[64]{0:T(128)S(1)} %reshape.245.table, bf16[768,1280]{1,0:T(8,128)(2,1)S(1)} %get-tuple-element.71.hidden_ref, bf16[3,4,80,1280]{3,2,1,0:T(8,128)(2,1)S(1)} %get-tuple-element.72.held, bf16[4,80,1280]{2,1,0:T(8,128)(2,1)} %shard_map.95.refs_6_.refs_0_, ...), custom_call_target="tpu_custom_call" | custom-call | flops 1887436800 | bytes 3145728 | tf_op jit(solution)/shard_map/pallas_call | solution.py:319
  90.1 3.5 %collective-permute-start.16 = (bf16[160,768]{1,0:T(8,128)(2,1)S(1)}, bf16[160,768]{1,0:T(8,128)(2,1)S(1)}, u32[]{:S(2)}, u32[]{:S(2)}) collective-permute-start(bf16[160,768]{1,0:T(8,128)(2,1)S(1)} %fusion.8), channel_id=1, source_target_pairs={{0,7},{1,0},{2,1},{3,2},{4,3},{5,4},{6,5},{7,6},{8,15},{9,8},{10,9... | collective-permute-start | bytes 737288 | tf_op jit(solution)/shard_map/ppermute | solution.py:332
  93.6 3.7 %collective-permute-done.12 = bf16[160,768]{1,0:T(8,128)(2,1)S(1)} collective-permute-done((bf16[160,768]{1,0:T(8,128)(2,1)S(1)}, bf16[160,768]{1,0:T(8,128)(2,1)S(1)}, u32[]{:S(2)}, u32[]{:S(2)}) %collective-permute-start.12) | collective-permute-done | bytes 245792 | tf_op jit(solution)/shard_map/ppermute | solution.py:332
  97.5 3.3 %collective-permute-start.22 = (bf16[160,768]{1,0:T(8,128)(2,1)S(1)}, bf16[160,768]{1,0:T(8,128)(2,1)S(1)}, u32[]{:S(2)}, u32[]{:S(2)}) collective-permute-start(bf16[160,768]{1,0:T(8,128)(2,1)S(1)} %fusion.4), channel_id=1, source_target_pairs={{0,7},{1,0},{2,1},{3,2},{4,3},{5,4},{6,5},{7,6},{8,15},{9,8},{10,9... | collective-permute-start | bytes 737288 | tf_op jit(solution)/shard_map/ppermute | solution.py:332
  100.8 1.7 %collective-permute-done.17 = bf16[160,768]{1,0:T(8,128)(2,1)S(1)} collective-permute-done((bf16[160,768]{1,0:T(8,128)(2,1)S(1)}, bf16[160,768]{1,0:T(8,128)(2,1)S(1)}, u32[]{:S(2)}, u32[]{:S(2)}) %collective-permute-start.17) | collective-permute-done | bytes 245792 | tf_op jit(solution)/shard_map/ppermute | solution.py:332
  102.8 3.3 %collective-permute-start.21 = (bf16[160,768]{1,0:T(8,128)(2,1)S(1)}, bf16[160,768]{1,0:T(8,128)(2,1)S(1)}, u32[]{:S(2)}, u32[]{:S(2)}) collective-permute-start(bf16[160,768]{1,0:T(8,128)(2,1)S(1)} %fusion.6), channel_id=1, source_target_pairs={{0,7},{1,0},{2,1},{3,2},{4,3},{5,4},{6,5},{7,6},{8,15},{9,8},{10,9... | collective-permute-start | bytes 737288 | tf_op jit(solution)/shard_map/ppermute | solution.py:332
  106.0 1.7 %collective-permute-done.15 = bf16[160,768]{1,0:T(8,128)(2,1)S(1)} collective-permute-done((bf16[160,768]{1,0:T(8,128)(2,1)S(1)}, bf16[160,768]{1,0:T(8,128)(2,1)S(1)}, u32[]{:S(2)}, u32[]{:S(2)}) %collective-permute-start.15) | collective-permute-done | bytes 245792 | tf_op jit(solution)/shard_map/ppermute | solution.py:332
  107.9 3.0 %collective-permute-start.23 = (bf16[160,768]{1,0:T(8,128)(2,1)S(1)}, bf16[160,768]{1,0:T(8,128)(2,1)S(1)}, u32[]{:S(2)}, u32[]{:S(2)}) collective-permute-start(bf16[160,768]{1,0:T(8,128)(2,1)S(1)} %fusion.3), channel_id=1, source_target_pairs={{0,7},{1,0},{2,1},{3,2},{4,3},{5,4},{6,5},{7,6},{8,15},{9,8},{10,9... | collective-permute-start | bytes 737288 | tf_op jit(solution)/shard_map/ppermute | solution.py:332
  111.0 1.3 %collective-permute-done.21 = bf16[160,768]{1,0:T(8,128)(2,1)S(1)} collective-permute-done((bf16[160,768]{1,0:T(8,128)(2,1)S(1)}, bf16[160,768]{1,0:T(8,128)(2,1)S(1)}, u32[]{:S(2)}, u32[]{:S(2)}) %collective-permute-start.21) | collective-permute-done | bytes 245792 | tf_op jit(solution)/shard_map/ppermute | solution.py:332
  113.1 1.9 %collective-permute-done.23 = bf16[160,768]{1,0:T(8,128)(2,1)S(1)} collective-permute-done((bf16[160,768]{1,0:T(8,128)(2,1)S(1)}, bf16[160,768]{1,0:T(8,128)(2,1)S(1)}, u32[]{:S(2)}, u32[]{:S(2)}) %collective-permute-start.23) | collective-permute-done | bytes 245792 | tf_op jit(solution)/shard_map/ppermute | solution.py:332
  114.9 3.4 %collective-permute-done.19 = bf16[160,768]{1,0:T(8,128)(2,1)S(1)} collective-permute-done((bf16[160,768]{1,0:T(8,128)(2,1)S(1)}, bf16[160,768]{1,0:T(8,128)(2,1)S(1)}, u32[]{:S(2)}, u32[]{:S(2)}) %collective-permute-start.19) | collective-permute-done | bytes 245792 | tf_op jit(solution)/shard_map/ppermute | solution.py:332
  (69 shorter events, 12.3 us)
Async XLA Ops:
  0.0 15.1 %copy-start.8 = (s32[8]{0:T(128)S(1)}, s32[8]{0:T(128)}, u32[]{:S(2)}) copy-start(s32[8]{0:T(128)} %constant.72.clone) | copy-start | bytes 100
  0.0 11.3 %copy-start.6 = (bf16[80,1280]{1,0:T(8,128)(2,1)S(1)}, bf16[80,1280]{1,0:T(8,128)(2,1)}, u32[]{:S(2)}) copy-start(bf16[80,1280]{1,0:T(8,128)(2,1)} %own.1) | copy-start | bytes 614404
  0.0 8.0 %collective-permute-start.1 = (bf16[80,1280]{1,0:T(8,128)(2,1)}, bf16[80,1280]{1,0:T(8,128)(2,1)S(1)}, u32[]{:S(2)}, u32[]{:S(2)}) collective-permute-start(bf16[80,1280]{1,0:T(8,128)(2,1)} %own.1), channel_id=1, source_target_pairs={{16,0},{24,8},{0,16},{8,24},{48,32},{56,40},{32,48},{40,56},{80,64... | collective-permute-start | bytes 614408 | tf_op jit(solution)/shard_map/ppermute | solution.py:357
  3.0 6.7 %collective-permute-start = (bf16[80,1280]{1,0:T(8,128)(2,1)}, bf16[80,1280]{1,0:T(8,128)(2,1)S(1)}, u32[]{:S(2)}, u32[]{:S(2)}) collective-permute-start(bf16[80,1280]{1,0:T(8,128)(2,1)} %own.1), channel_id=1, source_target_pairs={{8,0},{16,8},{24,16},{0,24},{40,32},{48,40},{56,48},{32,56},{72,64... | collective-permute-start | bytes 614408 | tf_op jit(solution)/shard_map/ppermute | solution.py:357
  4.2 7.2 %collective-permute-start.2 = (bf16[80,1280]{1,0:T(8,128)(2,1)}, bf16[80,1280]{1,0:T(8,128)(2,1)S(1)}, u32[]{:S(2)}, u32[]{:S(2)}) collective-permute-start(bf16[80,1280]{1,0:T(8,128)(2,1)} %own.1), channel_id=1, source_target_pairs={{24,0},{0,8},{8,16},{16,24},{56,32},{32,40},{40,48},{48,56},{88,64... | collective-permute-start | bytes 614408 | tf_op jit(solution)/shard_map/ppermute | solution.py:357
  8.0 31.8 %copy-start.7 = (f32[10]{0:T(128)S(1)}, f32[10]{0:T(128)}, u32[]{:S(2)}) copy-start(f32[10]{0:T(128)} %param.15) | copy-start | bytes 124
  12.3 13.2 %collective-permute-start.5 = (bf16[4,80,1280]{2,1,0:T(8,128)(2,1)}, bf16[4,80,1280]{2,1,0:T(8,128)(2,1)}, u32[]{:S(2)}, u32[]{:S(2)}) collective-permute-start(bf16[4,80,1280]{2,1,0:T(8,128)(2,1)} %shard_map.95.refs_6_.refs_0_), channel_id=1, source_target_pairs={{96,0},{104,8},{112,16},{120,24},{0,32},{8,40},{16,48},{24,56},{32... | collective-permute-start | bytes 2457608 | tf_op jit(solution)/shard_map/ppermute | solution.py:357
  12.6 15.0 %collective-permute-start.4 = (bf16[4,80,1280]{2,1,0:T(8,128)(2,1)}, bf16[4,80,1280]{2,1,0:T(8,128)(2,1)}, u32[]{:S(2)}, u32[]{:S(2)}) collective-permute-start(bf16[4,80,1280]{2,1,0:T(8,128)(2,1)} %shard_map.95.refs_6_.refs_0_), channel_id=1, source_target_pairs={{64,0},{72,8},{80,16},{88,24},{96,32},{104,40},{112,48},{120,56},{... | collective-permute-start | bytes 2457608 | tf_op jit(solution)/shard_map/ppermute | solution.py:357
  15.1 24.1 %collective-permute-start.3 = (bf16[4,80,1280]{2,1,0:T(8,128)(2,1)}, bf16[4,80,1280]{2,1,0:T(8,128)(2,1)}, u32[]{:S(2)}, u32[]{:S(2)}) collective-permute-start(bf16[4,80,1280]{2,1,0:T(8,128)(2,1)} %shard_map.95.refs_6_.refs_0_), channel_id=1, source_target_pairs={{32,0},{40,8},{48,16},{56,24},{64,32},{72,40},{80,48},{88,56},{96,... | collective-permute-start | bytes 2457608 | tf_op jit(solution)/shard_map/ppermute | solution.py:357
  15.1 47.1 %collective-permute-start.6 = (bf16[4,80,1280]{2,1,0:T(8,128)(2,1)}, bf16[4,80,1280]{2,1,0:T(8,128)(2,1)}, u32[]{:S(2)}, u32[]{:S(2)}) collective-permute-start(bf16[4,80,1280]{2,1,0:T(8,128)(2,1)} %shard_map.95.refs_6_.refs_0_), channel_id=1, source_target_pairs={{0,128},{128,0},{1,129},{129,1},{2,130},{130,2},{3,131},{131,3},{4... | collective-permute-start | bytes 2457608 | tf_op jit(solution)/shard_map/ppermute | solution.py:332
  15.2 30.4 %all-to-all-start = ((bf16[32,8,768]{2,1,0:T(8,128)(2,1)}), bf16[32,8,768]{2,1,0:T(8,128)(2,1)S(1)}, u32[]{:S(2)}, u32[]{:S(2)}) async-start(bf16[32,8,768]{2,1,0:T(8,128)(2,1)} %bitcast.1), calls=%async_computation | async-start | bytes 786432 | tf_op jit(solution)/shard_map/all_to_all | solution.py:424
  39.2 23.0 %collective-permute-start.7 = (bf16[4,80,1280]{2,1,0:T(8,128)(2,1)}, bf16[4,80,1280]{2,1,0:T(8,128)(2,1)}, u32[]{:S(2)}, u32[]{:S(2)}) collective-permute-start(bf16[4,80,1280]{2,1,0:T(8,128)(2,1)} %collective-permute-done.3.refs_7_.refs_1_), channel_id=1, source_target_pairs={{0,128},{128,0},{1,129},{129,1},{2,130},{130,2},{3,131},{131,3},{4... | collective-permute-start | bytes 2457608 | tf_op jit(solution)/shard_map/ppermute | solution.py:332
  39.2 23.0 %collective-permute-start.8 = (bf16[4,80,1280]{2,1,0:T(8,128)(2,1)}, bf16[4,80,1280]{2,1,0:T(8,128)(2,1)}, u32[]{:S(2)}, u32[]{:S(2)}) collective-permute-start(bf16[4,80,1280]{2,1,0:T(8,128)(2,1)} %collective-permute-done.4.refs_8_.refs_2_), channel_id=1, source_target_pairs={{0,128},{128,0},{1,129},{129,1},{2,130},{130,2},{3,131},{131,3},{4... | collective-permute-start | bytes 2457608 | tf_op jit(solution)/shard_map/ppermute | solution.py:332
  39.7 22.5 %collective-permute-start.9 = (bf16[4,80,1280]{2,1,0:T(8,128)(2,1)}, bf16[4,80,1280]{2,1,0:T(8,128)(2,1)}, u32[]{:S(2)}, u32[]{:S(2)}) collective-permute-start(bf16[4,80,1280]{2,1,0:T(8,128)(2,1)} %collective-permute-done.5.refs_9_.refs_3_), channel_id=1, source_target_pairs={{0,128},{128,0},{1,129},{129,1},{2,130},{130,2},{3,131},{131,3},{4... | collective-permute-start | bytes 2457608 | tf_op jit(solution)/shard_map/ppermute | solution.py:332
  46.8 15.4 %all-to-all-start.1 = ((bf16[32,8,640]{2,1,0:T(8,128)(2,1)}), bf16[32,8,640]{2,1,0:T(8,128)(2,1)S(1)}, u32[]{:S(2)}, u32[]{:S(2)}) async-start(bf16[32,8,640]{2,1,0:T(8,128)(2,1)} %shard_map.93), calls=%async_computation.1 | async-start | bytes 655360 | tf_op jit(solution)/shard_map/all_to_all | solution.py:431
  60.0 1.3 %copy-start = (f32[384,1280]{1,0:T(8,128)}, f32[384,1280]{1,0:T(8,128)S(1)}, u32[]{:S(2)}) copy-start(f32[384,1280]{1,0:T(8,128)S(1)} %get-tuple-element.53.refs_3_) | copy-start | bytes 5898244
  62.3 1.5 %copy-start.1 = (f32[384,1280]{1,0:T(8,128)S(1)}, f32[384,1280]{1,0:T(8,128)}, u32[]{:S(2)}) copy-start(f32[384,1280]{1,0:T(8,128)} %copy-done) | copy-start | bytes 5898244
  63.8 1.2 %copy-start.3 = (bf16[384,1280]{1,0:T(8,128)(2,1)S(1)}, bf16[384,1280]{1,0:T(8,128)(2,1)}, u32[]{:S(2)}) copy-start(bf16[384,1280]{1,0:T(8,128)(2,1)} %copy-done.2) | copy-start | bytes 2949124
  68.9 14.9 %collective-permute-start.11 = (bf16[160,768]{1,0:T(8,128)(2,1)S(1)}, bf16[160,768]{1,0:T(8,128)(2,1)S(1)}, u32[]{:S(2)}, u32[]{:S(2)}) collective-permute-start(bf16[160,768]{1,0:T(8,128)(2,1)S(1)} %get-tuple-element.66), channel_id=1, source_target_pairs={{0,1},{1,2},{2,3},{3,4},{4,5},{5,6},{6,7},{7,0},{8,9},{9,10},{10,1... | collective-permute-start | bytes 737288 | tf_op jit(solution)/shard_map/ppermute | solution.py:332
  70.9 13.0 %collective-permute-start.10 = (bf16[160,768]{1,0:T(8,128)(2,1)S(1)}, bf16[160,768]{1,0:T(8,128)(2,1)S(1)}, u32[]{:S(2)}, u32[]{:S(2)}) collective-permute-start(bf16[160,768]{1,0:T(8,128)(2,1)S(1)} %get-tuple-element.65), channel_id=1, source_target_pairs={{0,7},{1,0},{2,1},{3,2},{4,3},{5,4},{6,5},{7,6},{8,15},{9,8},{10,9... | collective-permute-start | bytes 737288 | tf_op jit(solution)/shard_map/ppermute | solution.py:332
  78.1 11.9 %collective-permute-start.13 = (bf16[160,768]{1,0:T(8,128)(2,1)S(1)}, bf16[160,768]{1,0:T(8,128)(2,1)S(1)}, u32[]{:S(2)}, u32[]{:S(2)}) collective-permute-start(bf16[160,768]{1,0:T(8,128)(2,1)S(1)} %get-tuple-element.73), channel_id=1, source_target_pairs={{0,7},{1,0},{2,1},{3,2},{4,3},{5,4},{6,5},{7,6},{8,15},{9,8},{10,9... | collective-permute-start | bytes 737288 | tf_op jit(solution)/shard_map/ppermute | solution.py:332
  80.1 9.7 %collective-permute-start.14 = (bf16[160,768]{1,0:T(8,128)(2,1)S(1)}, bf16[160,768]{1,0:T(8,128)(2,1)S(1)}, u32[]{:S(2)}, u32[]{:S(2)}) collective-permute-start(bf16[160,768]{1,0:T(8,128)(2,1)S(1)} %get-tuple-element.74), channel_id=1, source_target_pairs={{0,1},{1,2},{2,3},{3,4},{4,5},{5,6},{6,7},{7,0},{8,9},{9,10},{10,1... | collective-permute-start | bytes 737288 | tf_op jit(solution)/shard_map/ppermute | solution.py:332
  83.9 13.5 %collective-permute-start.18 = (bf16[160,768]{1,0:T(8,128)(2,1)S(1)}, bf16[160,768]{1,0:T(8,128)(2,1)S(1)}, u32[]{:S(2)}, u32[]{:S(2)}) collective-permute-start(bf16[160,768]{1,0:T(8,128)(2,1)S(1)} %fusion.12), channel_id=1, source_target_pairs={{0,7},{1,0},{2,1},{3,2},{4,3},{5,4},{6,5},{7,6},{8,15},{9,8},{10,9... | collective-permute-start | bytes 737288 | tf_op jit(solution)/shard_map/ppermute | solution.py:332
  87.2 10.1 %collective-permute-start.12 = (bf16[160,768]{1,0:T(8,128)(2,1)S(1)}, bf16[160,768]{1,0:T(8,128)(2,1)S(1)}, u32[]{:S(2)}, u32[]{:S(2)}) collective-permute-start(bf16[160,768]{1,0:T(8,128)(2,1)S(1)} %fusion.11), channel_id=1, source_target_pairs={{0,1},{1,2},{2,3},{3,4},{4,5},{5,6},{6,7},{7,0},{8,9},{9,10},{10,1... | collective-permute-start | bytes 737288 | tf_op jit(solution)/shard_map/ppermute | solution.py:332
  89.9 12.6 %collective-permute-start.17 = (bf16[160,768]{1,0:T(8,128)(2,1)S(1)}, bf16[160,768]{1,0:T(8,128)(2,1)S(1)}, u32[]{:S(2)}, u32[]{:S(2)}) collective-permute-start(bf16[160,768]{1,0:T(8,128)(2,1)S(1)} %fusion.7), channel_id=1, source_target_pairs={{0,1},{1,2},{2,3},{3,4},{4,5},{5,6},{6,7},{7,0},{8,9},{9,10},{10,1... | collective-permute-start | bytes 737288 | tf_op jit(solution)/shard_map/ppermute | solution.py:332
  90.1 12.6 %collective-permute-start.16 = (bf16[160,768]{1,0:T(8,128)(2,1)S(1)}, bf16[160,768]{1,0:T(8,128)(2,1)S(1)}, u32[]{:S(2)}, u32[]{:S(2)}) collective-permute-start(bf16[160,768]{1,0:T(8,128)(2,1)S(1)} %fusion.8), channel_id=1, source_target_pairs={{0,7},{1,0},{2,1},{3,2},{4,3},{5,4},{6,5},{7,6},{8,15},{9,8},{10,9... | collective-permute-start | bytes 737288 | tf_op jit(solution)/shard_map/ppermute | solution.py:332
  97.3 10.5 %collective-permute-start.15 = (bf16[160,768]{1,0:T(8,128)(2,1)S(1)}, bf16[160,768]{1,0:T(8,128)(2,1)S(1)}, u32[]{:S(2)}, u32[]{:S(2)}) collective-permute-start(bf16[160,768]{1,0:T(8,128)(2,1)S(1)} %fusion.9), channel_id=1, source_target_pairs={{0,1},{1,2},{2,3},{3,4},{4,5},{5,6},{6,7},{7,0},{8,9},{9,10},{10,1... | collective-permute-start | bytes 737288 | tf_op jit(solution)/shard_map/ppermute | solution.py:332
  97.5 10.4 %collective-permute-start.22 = (bf16[160,768]{1,0:T(8,128)(2,1)S(1)}, bf16[160,768]{1,0:T(8,128)(2,1)S(1)}, u32[]{:S(2)}, u32[]{:S(2)}) collective-permute-start(bf16[160,768]{1,0:T(8,128)(2,1)S(1)} %fusion.4), channel_id=1, source_target_pairs={{0,7},{1,0},{2,1},{3,2},{4,3},{5,4},{6,5},{7,6},{8,15},{9,8},{10,9... | collective-permute-start | bytes 737288 | tf_op jit(solution)/shard_map/ppermute | solution.py:332
  102.6 10.5 %collective-permute-start.20 = (bf16[160,768]{1,0:T(8,128)(2,1)S(1)}, bf16[160,768]{1,0:T(8,128)(2,1)S(1)}, u32[]{:S(2)}, u32[]{:S(2)}) collective-permute-start(bf16[160,768]{1,0:T(8,128)(2,1)S(1)} %fusion.5), channel_id=1, source_target_pairs={{0,1},{1,2},{2,3},{3,4},{4,5},{5,6},{6,7},{7,0},{8,9},{9,10},{10,1... | collective-permute-start | bytes 737288 | tf_op jit(solution)/shard_map/ppermute | solution.py:332
  102.8 9.5 %collective-permute-start.21 = (bf16[160,768]{1,0:T(8,128)(2,1)S(1)}, bf16[160,768]{1,0:T(8,128)(2,1)S(1)}, u32[]{:S(2)}, u32[]{:S(2)}) collective-permute-start(bf16[160,768]{1,0:T(8,128)(2,1)S(1)} %fusion.6), channel_id=1, source_target_pairs={{0,7},{1,0},{2,1},{3,2},{4,3},{5,4},{6,5},{7,6},{8,15},{9,8},{10,9... | collective-permute-start | bytes 737288 | tf_op jit(solution)/shard_map/ppermute | solution.py:332
  107.9 7.0 %collective-permute-start.23 = (bf16[160,768]{1,0:T(8,128)(2,1)S(1)}, bf16[160,768]{1,0:T(8,128)(2,1)S(1)}, u32[]{:S(2)}, u32[]{:S(2)}) collective-permute-start(bf16[160,768]{1,0:T(8,128)(2,1)S(1)} %fusion.3), channel_id=1, source_target_pairs={{0,7},{1,0},{2,1},{3,2},{4,3},{5,4},{6,5},{7,6},{8,15},{9,8},{10,9... | collective-permute-start | bytes 737288 | tf_op jit(solution)/shard_map/ppermute | solution.py:332
  111.0 7.4 %collective-permute-start.19 = (bf16[160,768]{1,0:T(8,128)(2,1)S(1)}, bf16[160,768]{1,0:T(8,128)(2,1)S(1)}, u32[]{:S(2)}, u32[]{:S(2)}) collective-permute-start(bf16[160,768]{1,0:T(8,128)(2,1)S(1)} %fusion.10), channel_id=1, source_target_pairs={{0,1},{1,2},{2,3},{3,4},{4,5},{5,6},{6,7},{7,0},{8,9},{9,10},{10,1... | collective-permute-start | bytes 737288 | tf_op jit(solution)/shard_map/ppermute | solution.py:332
  (3 other events, 2.9 us)

commit v3 on v2

--- a/solution.py
+++ b/solution.py
@@ -17,6 +17,7 @@
 SHARDS = 32
 ROWS = 80
 PIECE = 160
+FAR, NEAR, NEXT, REST = (4,), (3, -3), (2, -2), (1, -1, 0)
 NBLK = TOK // BLK
 F32 = jnp.float32
 BF16 = jnp.bfloat16
@@ -41,6 +42,14 @@
     rows = lax.broadcasted_iota(jnp.int32, (BLK, BLK), 0)
     cols = lax.broadcasted_iota(jnp.int32, (BLK, BLK), 1)
     return jnp.where(upto(rows, cols), 1.0, 0.0).astype(F32)
+
+
+def columns_of():
+    return lax.rem(lax.axis_index("row"), 4)
+
+
+def rows_of():
+    return lax.axis_index("row") // 4
 
 
 def split3(value):
@@ -101,14 +110,14 @@
             pl.BlockSpec((HEADS, TOK), lambda i: (0, 0)),
         ],
         out_specs=pl.BlockSpec((16, 1, 8, HALF + P_SIZE), lambda i: (0, i, 0, 0)),
-        out_shape=jax.ShapeDtypeStruct((16, 2, 8, HALF + P_SIZE), BF16),
+        out_shape=pltpu.HBM((16, 2, 8, HALF + P_SIZE), BF16),
         scratch_shapes=[pltpu.VMEM((HEADS, TOK), F32), pltpu.VMEM((16, P_SIZE), F32), pltpu.VMEM((N, TOK), F32)],
         compiler_params=SMALL,
         cost_estimate=pl.CostEstimate(flops=2 * TOK * N * CH, bytes_accessed=3 << 20, transcendentals=0),
     )(*[in_hbm(v) for v in (x, b, step, log_gate)])
 
 
-def scan_body(half_ref, in_ref, out_ref, decay_ref):
+def scan_body(half_ref, in_ref, mark_ref, out_ref, decay_ref):
     lines = in_ref[:, :, HALF:].astype(F32)
     decay = jnp.sum(lines, axis=1)
     rows = lax.broadcasted_iota(jnp.int32, (P_SIZE, HALF), 0)
@@ -121,30 +130,27 @@
         state = decay_ref[k : k + 1, :] * state + in_ref[k, :, :HALF].astype(F32)
 
 
-def scan_shards(half, received):
+def scan_shards(half, received, mark):
     return pl.pallas_call(
         scan_body,
         in_specs=[
-            pl.BlockSpec(memory_space=pltpu.SMEM),
-            pl.BlockSpec(memory_space=pltpu.VMEM),
+            IN_SMEM,
+            IN_VMEM,
+            ANYWHERE,
         ],
-        out_specs=pl.BlockSpec(memory_space=pltpu.VMEM),
-        out_shape=jax.ShapeDtypeStruct((SHARDS, 8, HALF), BF16),
+        out_specs=IN_VMEM,
+        out_shape=pltpu.HBM((SHARDS, 8, HALF), BF16),
         scratch_shapes=[pltpu.VMEM((SHARDS, HALF), F32)],
         compiler_params=SMALL,
-    )(half, received)
-
-
-def inner_body(x_ref, g_ref, b_ref, c_ref, step_ref, log_ref, skip_ref, start_ref, before_ref, pre_ref, gain_ref, keep_ref, state_ref, past_ref):
-    k = pl.program_id(0)
-    tokens = pl.ds(pl.multiple_of(k * BLK, BLK), BLK)
-
-    @pl.when(k == 0)
+    )(half, received, mark)
+
+
+def inner_body(x_ref, g_ref, b_ref, c_ref, step_ref, log_ref, skip_ref, mark_ref, pre_ref, gain_ref, state_ref, past_ref):
+    @pl.when(pl.program_id(0) == 0)
     def _():
-        state_ref[...] = start_ref[...]
-        past_ref[...] = before_ref[...]
-
-    keep_ref[tokens, :] = c_ref[...]
+        state_ref[...] = jnp.zeros_like(state_ref)
+        past_ref[...] = jnp.zeros_like(past_ref)
+
     logs = log_ref[...]
     steps = step_ref[...]
     upto = triangle(lambda s, t: s <= t)
@@ -181,48 +187,63 @@
         out = out + skip_ref[0, h] * x_here.astype(F32)
         gate = g_ref[:, here].astype(F32)
         silu = 0.5 * gate * (1.0 + jnp.tanh(0.5 * gate))
-        pre_ref[tokens, here] = out * silu
-        gain_ref[tokens, here] = (silu * columns[:, 32 + h : 33 + h]).astype(BF16)
+        pre_ref[:, here] = (out * silu).astype(BF16)
+        gain_ref[:, here] = (silu * columns[:, 32 + h : 33 + h]).astype(BF16)
         scaled = (turned * tail[h : h + 1, :]).astype(BF16)
         state_ref[:, here] = grow[h : h + 1, :] * state + jnp.dot(scaled, x_here, preferred_element_type=F32)
     past_ref[:HEADS, :] = past_ref[:HEADS, :] + total
 
 
-def inner(x, g, b, c, step, log_gate, skip, first, state, past):
-    count = NBLK // 2
-    rows = count * BLK
+def inner(x, g, b, c, step, log_gate, skip, mark):
     return pl.pallas_call(
         inner_body,
-        grid=(count,),
+        grid=(NBLK,),
         in_specs=[
-            pl.BlockSpec((BLK, CH), lambda i: (i + first, 0)),
-            pl.BlockSpec((BLK, CH), lambda i: (i + first, 0)),
-            pl.BlockSpec((BLK, N), lambda i: (i + first, 0)),
-            pl.BlockSpec((BLK, N), lambda i: (i + first, 0)),
-            pl.BlockSpec((HEADS, BLK), lambda i: (0, i + first)),
-            pl.BlockSpec((HEADS, BLK), lambda i: (0, i + first)),
+            pl.BlockSpec((BLK, CH), lambda i: (i, 0)),
+            pl.BlockSpec((BLK, CH), lambda i: (i, 0)),
+            pl.BlockSpec((BLK, N), lambda i: (i, 0)),
+            pl.BlockSpec((BLK, N), lambda i: (i, 0)),
+            pl.BlockSpec((HEADS, BLK), lambda i: (0, i)),
+            pl.BlockSpec((HEADS, BLK), lambda i: (0, i)),
             IN_SMEM,
-            IN_VMEM,
-            IN_VMEM,
+            ANYWHERE,
         ],
-        out_specs=[IN_VMEM] * 5,
-        out_shape=[
-            pltpu.VMEM((rows, CH), F32),
-            pltpu.VMEM((rows, CH), BF16),
-            pltpu.VMEM((rows, N), BF16),
-            jax.ShapeDtypeStruct((N, CH), F32),
-            jax.ShapeDtypeStruct((16, BLK), F32),
-        ],
-        compiler_params=SMALL,
-        cost_estimate=pl.CostEstimate(flops=1 << 20, bytes_accessed=1 << 20, transcendentals=0),
-    )(*[in_hbm(v) for v in (x, g, b, c, step, log_gate)], skip.reshape(1, HEADS), state, past)
-
-
-def fetch(table, refs, held, sems, chunks):
-    for slot, chunk in enumerate(chunks):
+        out_specs=[pl.BlockSpec((BLK, CH), lambda i: (i, 0))] * 2,
+        out_shape=[pltpu.HBM((TOK, CH), BF16)] * 2,
+        scratch_shapes=[pltpu.VMEM((N, CH), F32), pltpu.VMEM((16, BLK), F32)],
+        compiler_params=SMALL,
+        cost_estimate=pl.CostEstimate(flops=1 << 20, bytes_accessed=40 << 20, transcendentals=0),
+    )(*[in_hbm(v) for v in (x, g, b, c, step, log_gate)], skip.reshape(1, HEADS), in_hbm(mark))
+
+
+def hold_body(*refs):
+    pass
+
+
+def hold(values, *marks):
+    count = len(values)
+    return pl.pallas_call(
+        hold_body,
+        in_specs=[ANYWHERE] * (count + len(marks)),
+        out_specs=[ANYWHERE] * count,
+        out_shape=[pltpu.HBM(v.shape, v.dtype) for v in values],
+        input_output_aliases={i: i for i in range(count)},
+        compiler_params=SMALL,
+        cost_estimate=pl.CostEstimate(flops=0, bytes_accessed=0, transcendentals=0),
+    )(*[in_hbm(v) for v in values], *marks)
+
+
+def fetch(refs, held, sems, ups):
+    seq, head = lax.axis_index("seq"), lax.axis_index("head")
+    for slot, up in enumerate(ups):
+        group = lax.rem(head + (up + 8), 8)
+        first = group < 4
+        down = lax.rem(lax.rem(group, 4) - rows_of() + 4, 4)
+        base = jnp.where((seq == 0) == first, 0, 4)
         for j in range(4):
-            array = table[8 * chunk + 2 * j]
-            block = table[8 * chunk + 2 * j + 1]
+            right = lax.rem(j - columns_of() + 4, 4)
+            array = base + jnp.where(first, down, right)
+            block = jnp.where(first, right, down)
             for k, ref in enumerate(refs):
 
                 @pl.when(array == k)
@@ -245,19 +266,28 @@
     return pltpu.VMEM((count, 4, ROWS, CH), BF16)
 
 
-def first_body(table, in_ref, *refs):
-    parts, refs, (hidden_ref, up_ref, down_ref, later, held, sems, later_sems) = refs[:6], refs[6:14], refs[14:]
+def first_body(in_ref, c_ref, *refs):
+    parts, refs = refs[:2], refs[2:]
+    refs, (hidden_ref, up_ref, down_ref, later, pre, gain, part_sems, held, sems, later_sems) = refs[:8], refs[8:]
     rows = TOK // 2
-    fetch(table, refs, held, sems, (0,))
-    fetch(table, refs, later, later_sems, (1, 2))
+    copies = []
+    for i in range(2):
+        here = pl.ds(i * rows, rows)
+        for j, (part, held_part) in enumerate(zip(parts, (pre, gain))):
+            copies.append(pltpu.make_async_copy(part.at[here], held_part.at[here], part_sems.at[i, j]))
+            copies[-1].start()
+        if i == 0:
+            fetch(refs, held, sems, FAR)
+    fetch(refs, later, later_sems, NEAR)
     states = [in_ref[:, half].astype(F32).reshape(N, HALF).astype(BF16) for half in range(2)]
     for i in range(2):
         here = slice(i * rows, (i + 1) * rows)
-        pre_ref, gain_ref, c_ref = parts[3 * i : 3 * i + 3]
+        copies[2 * i].wait()
+        copies[2 * i + 1].wait()
         for half in range(2):
             cols = slice(half * HALF, (half + 1) * HALF)
-            carried = jnp.dot(c_ref[...], states[half], preferred_element_type=F32)
-            hidden_ref[here, cols] = (pre_ref[:, cols] + gain_ref[:, cols].astype(F32) * carried).astype(BF16)
+            carried = jnp.dot(c_ref[here, :], states[half], preferred_element_type=F32)
+            hidden_ref[here, cols] = (pre[here, cols].astype(F32) + gain[here, cols].astype(F32) * carried).astype(BF16)
         if i == 0:
             arrive(refs, held, sems)
         out = product(held, 0, hidden_ref[here, :])
@@ -266,21 +296,28 @@
     arrive(refs, later, later_sems)
 
 
-def first_parts(table, entering, parts, blocks):
+def first_parts(entering, c, parts, blocks):
     return pl.pallas_call(
         first_body,
-        in_specs=[IN_SMEM] + [IN_VMEM] * 7 + [ANYWHERE] * 8,
+        in_specs=[IN_VMEM] * 2 + [ANYWHERE] * 10,
         out_specs=[IN_VMEM] * 4,
         out_shape=[pltpu.VMEM((TOK, CH), BF16)] + [jax.ShapeDtypeStruct((PIECE, TOK), BF16)] * 2 + [held_weights(2)],
-        scratch_shapes=[held_weights(1), pltpu.SemaphoreType.DMA((1, 4)), pltpu.SemaphoreType.DMA((2, 4))],
+        scratch_shapes=[
+            pltpu.VMEM((TOK, CH), BF16),
+            pltpu.VMEM((TOK, CH), BF16),
+            pltpu.SemaphoreType.DMA((2, 2)),
+            held_weights(1),
+            pltpu.SemaphoreType.DMA((1, 4)),
+            pltpu.SemaphoreType.DMA((2, 4)),
+        ],
         compiler_params=SMALL,
         cost_estimate=pl.CostEstimate(flops=2 * 320 * TOK * CH, bytes_accessed=2 << 20, transcendentals=0),
-    )(table, entering, *[in_vmem(v) for v in parts], *[in_hbm(v) for v in blocks])
-
-
-def near_body(chunks, table, hidden_ref, held, *refs):
+    )(entering, *[in_hbm(v) for v in (c, *parts, *blocks)])
+
+
+def near_body(ups, hidden_ref, held, *refs):
     refs, (up_ref, down_ref, keep_ref, later, sems) = refs[:8], refs[8:]
-    fetch(table, refs, later, sems, chunks)
+    fetch(refs, later, sems, ups)
     out = product(held, 0, hidden_ref[...])
     up_ref[...] = out[PIECE:]
     keep_ref[0] = out[:PIECE]
@@ -290,41 +327,41 @@
     arrive(refs, later, sems)
 
 
-def near_parts(table, hidden, held, blocks, chunks):
-    return pl.pallas_call(
-        functools.partial(near_body, chunks),
-        in_specs=[IN_SMEM, IN_VMEM, IN_VMEM] + [ANYWHERE] * 8,
+def near_parts(hidden, held, blocks, ups):
+    return pl.pallas_call(
+        functools.partial(near_body, ups),
+        in_specs=[IN_VMEM, IN_VMEM] + [ANYWHERE] * 8,
         out_specs=[IN_VMEM] * 4,
         out_shape=[jax.ShapeDtypeStruct((PIECE, TOK), BF16)] * 2
-        + [jax.ShapeDtypeStruct((2, PIECE, TOK), BF16), held_weights(len(chunks))],
-        scratch_shapes=[pltpu.SemaphoreType.DMA((len(chunks), 4))],
+        + [jax.ShapeDtypeStruct((2, PIECE, TOK), BF16), held_weights(len(ups))],
+        scratch_shapes=[pltpu.SemaphoreType.DMA((len(ups), 4))],
         compiler_params=SMALL,
         cost_estimate=pl.CostEstimate(flops=4 * 320 * TOK * CH, bytes_accessed=2 << 20, transcendentals=0),
-    )(table, in_vmem(hidden), in_vmem(held), *[in_hbm(v) for v in blocks])
-
-
-def rest_body(chunks, table, hidden_ref, held, *refs):
+    )(in_vmem(hidden), in_vmem(held), *[in_hbm(v) for v in blocks])
+
+
+def rest_body(ups, hidden_ref, held, *refs):
     refs, (out_ref, *scratch) = refs[:8], refs[8:]
-    if chunks:
+    if ups:
         later, sems = scratch
-        fetch(table, refs, later, sems, chunks)
+        fetch(refs, later, sems, ups)
     for slot in range(held.shape[0]):
         out_ref[slot] = product(held, slot, hidden_ref[...]).reshape(2, PIECE, TOK)
-    if chunks:
+    if ups:
         arrive(refs, later, sems)
 
 
-def rest_parts(table, hidden, held, blocks, chunks):
-    count, later = held.shape[0], len(chunks)
-    return pl.pallas_call(
-        functools.partial(rest_body, chunks),
-        in_specs=[IN_SMEM, IN_VMEM, IN_VMEM] + [ANYWHERE] * 8,
+def rest_parts(hidden, held, blocks, ups):
+    count, later = held.shape[0], len(ups)
+    return pl.pallas_call(
+        functools.partial(rest_body, ups),
+        in_specs=[IN_VMEM, IN_VMEM] + [ANYWHERE] * 8,
         out_specs=[IN_VMEM] * (2 if later else 1),
         out_shape=[jax.ShapeDtypeStruct((count, 2, PIECE, TOK), BF16)] + ([held_weights(later)] if later else []),
         scratch_shapes=[pltpu.SemaphoreType.DMA((later, 4))] if later else [],
         compiler_params=SMALL,
         cost_estimate=pl.CostEstimate(flops=2 * count * 320 * TOK * CH, bytes_accessed=count << 20, transcendentals=0),
-    )(table, in_vmem(hidden), in_vmem(held), *[in_hbm(v) for v in blocks])
+    )(in_vmem(hidden), in_vmem(held), *[in_hbm(v) for v in blocks])
 
 
 def shift(value, axis, by):
@@ -357,7 +394,7 @@
     return lax.ppermute(value, ("seq", "row"), pairs)
 
 
-def line_body(own, one, two, three, out):
+def line_body(own, one, two, three, mark, out):
     for k, part in enumerate((own, one, two, three)):
         out[k] = part[...]
 
@@ -365,37 +402,25 @@
 def line_of(*parts):
     return pl.pallas_call(
         line_body,
-        in_specs=[IN_VMEM] * 4,
+        in_specs=[IN_VMEM] * 4 + [ANYWHERE],
         out_specs=IN_VMEM,
         out_shape=pltpu.HBM((4, ROWS, CH), BF16),
         compiler_params=SMALL,
+        cost_estimate=pl.CostEstimate(flops=0, bytes_accessed=1 << 10, transcendentals=0),
     )(*parts)
 
 
-def weight_table(order):
-    seq, row, head = (lax.axis_index(name) for name in ("seq", "row", "head"))
-    group = lax.rem(head + jnp.array(order, jnp.int32) + 8, 8)[:, None]
-    source = group // 4
-    right = lax.rem(jnp.arange(4, dtype=jnp.int32)[None, :] - lax.rem(row, 4) + 4, 4)
-    down = lax.rem(group % 4 - row // 4 + 4, 4)
-    down, right = jnp.broadcast_arrays(down, right)
-    array = jnp.where(source == seq, 0, 4) + jnp.where(source == 0, down, right)
-    block = jnp.where(source == 0, right, down)
-    return jnp.stack([array, block], axis=2).astype(jnp.int32).reshape(-1)
-
-
-def projected(entering, parts, blocks):
-    table = weight_table((4, 3, -3, 2, -2, 1, -1, 0))
-    hidden, ua, db, held = first_parts(table, entering, parts, blocks)
+def projected(entering, c, parts, blocks):
+    hidden, ua, db, held = first_parts(entering, c, parts, blocks)
     ua, db = shift(ua, "head", 1), shift(db, "head", -1)
-    ub, da, keep, held = near_parts(table, hidden, held, blocks, (3, 4))
+    ub, da, keep, held = near_parts(hidden, held, blocks, NEXT)
     ub, da = shift(ub, "head", 1), shift(da, "head", -1)
-    two, held = rest_parts(table, hidden, held, blocks, (5, 6, 7))
+    two, held = rest_parts(hidden, held, blocks, REST)
     sent = add(keep[0], after(ua, two))
     ua = shift(sent, "head", 1)
     sent = add(keep[1], after(db, sent))
     db = shift(sent, "head", -1)
-    (one,) = rest_parts(table, after(hidden, sent), held, blocks, ())
+    (one,) = rest_parts(after(hidden, sent), held, blocks, ())
     sent = add(two[0, 1], after(ub, one))
     ub = shift(sent, "head", 1)
     sent = add(two[1, 0], after(da, sent))
@@ -419,20 +444,20 @@
 
 def shards(x, g, b, c, step, log_gate, skip, out_weight):
     near = [from_line(out_weight, 0, offset) for offset in (1, 2, 3)]
-    payload = shard_state(x, b, step, log_gate).reshape(SHARDS, 8, HALF + P_SIZE)
-    payload, near = lax.optimization_barrier((payload, near))
-    received = lax.all_to_all(payload, ("seq", "row"), 0, 0)
-    nothing = (jnp.zeros((N, CH), F32), jnp.zeros((16, BLK), F32))
-    *early, state, past = inner(after(x, payload), g, b, c, step, log_gate, skip, 0, *nothing)
-    line = line_of(out_weight, *near)
-    one, two, three = (from_line(line, 1, offset) for offset in (1, 2, 3))
+    payload = shard_state(x, b, step, log_gate)
+    line = line_of(out_weight, *near, in_hbm(payload))
+    one, three = (from_line(line, 1, offset) for offset in (1, 3))
+    received = lax.all_to_all(payload.reshape(SHARDS, 8, HALF + P_SIZE), ("seq", "row"), 0, 0)
+    parts = inner(x, g, b, c, step, log_gate, skip, payload)
+    line, one, three = hold([line, one, three], received, in_hbm(parts[0]))
+    two = from_line(line, 1, 2)
+    other = [shift(v, "seq", 1) for v in (line, one, three)]
     half = lax.rem(lax.axis_index("row"), 2).reshape(1)
-    slices = scan_shards(half, after(received, past))
+    slices = scan_shards(half, received, in_hbm(parts[0]))
     entering = lax.all_to_all(slices, ("seq", "row"), 0, 0)
-    *late, _, past = inner(after(x, slices), g, b, c, step, log_gate, skip, NBLK // 2, state, past)
-    mine = [line, one, two, three]
-    other = [shift(v, "seq", 1) for v in [line] + after(mine[1:], past)]
-    return projected(entering.reshape(16, 2, 8, HALF), early + late, mine + other)
+    (two,) = hold([two], entering)
+    other.insert(2, shift(two, "seq", 1))
+    return projected(entering.reshape(16, 2, 8, HALF), c, parts, [line, one, two, three] + other)
 
 
 def solution(mesh):

time: 120 us -> 109 us (0.908)
  local copies, waits for them, and re-layouts: 7.23 us -> 2.09 us
  waiting for transfers between devices: 35 us -> 30.7 us
    ppermute x6, waiting for transfers between devices: 20.4 us -> 3.32 us  [from_line(): return lax.ppermute(value, ('seq', 'row'), pairs)]
    all_to_all x1, waiting for transfers between devices: 0.01 us -> 8.53 us  [shards(): entering = lax.all_to_all(slices, ('seq', 'row'), 0, 0)]
    unnamed x18 -> x16, local copies, waits for them, and re-layouts: 6.94 us -> 2.06 us
    ppermute x18, waiting for transfers between devices: 14.6 us -> 17.7 us  [shift(): lax.ppermute(value, axis, [(i, (i + by) % size) for i in range(size)])]
    all_to_all x1, starting transfers between devices: 6.85 us -> 5.64 us  [shards(): lax.all_to_all(payload.reshape(SHARDS, 8, HALF + P_SIZE), ('seq', 'row'),...]
    pallas_call x8 -> x9, Pallas kernels: 26 us -> 25 us  [the longest x1 9.34 us: inner(): pl.pallas_call(inner_body, grid=(NBLK,), in_specs=[pl.BlockSpec((BLK, CH)...]
where the time goes in v3:
time: 109 us; the launch traced here: 108 us
  starting transfers between devices  45.6 us (42%)
  waiting for transfers between devices  30.7 us (28%)
  Pallas kernels  28 us (26%)
  local copies, waits for them, and re-layouts  2.09 us (2%)
  other arithmetic  1.59 us (1%)
    ppermute x18, starting transfers between devices, shift(): lax.ppermute(value, axis, [(i, (i + by) % size) for i in range(size)])  25.5 us
    ppermute x18, waiting for transfers between devices, shift(): lax.ppermute(value, axis, [(i, (i + by) % size) for i in range(size)])  17.7 us
    pallas_call x1, Pallas kernels, inner(): pl.pallas_call(inner_body, grid=(NBLK,), in_specs=[pl.BlockSpec((BLK, CH)...  9.34 us
    ppermute x6, starting transfers between devices, from_line(): return lax.ppermute(value, ('seq', 'row'), pairs)  8.85 us
    all_to_all x1, waiting for transfers between devices, shards(): entering = lax.all_to_all(slices, ('seq', 'row'), 0, 0)  8.53 us
    all_to_all x1, starting transfers between devices, shards(): entering = lax.all_to_all(slices, ('seq', 'row'), 0, 0)  5.67 us
    all_to_all x1, starting transfers between devices, shards(): lax.all_to_all(payload.reshape(SHARDS, 8, HALF + P_SIZE), ('seq', 'row'),...  5.64 us
    pallas_call x1, Pallas kernels, first_parts(): pl.pallas_call(first_body, in_specs=[IN_VMEM] * 2 + [ANYWHERE] * 10, out_...  5.38 us
  transfers between devices with their start and end apart: 26, of which 12 were waited for; matrix products, arithmetic and copies ran while one was open for 1% of the time, Pallas kernels for 20%

profile of v3, /device:TPU:24, one launch (start us, length us, event | category | flops | bytes accessed | tf_op | source)
XLA Modules:
  0.0 108.2 jit_solution(18324893856944569708)
XLA Ops:
  0.0 3.0 %collective-permute-start.1 = (bf16[80,1280]{1,0:T(8,128)(2,1)}, bf16[80,1280]{1,0:T(8,128)(2,1)S(1)}, u32[]{:S(2)}, u32[]{:S(2)}) collective-permute-start(bf16[80,1280]{1,0:T(8,128)(2,1)} %own.1), channel_id=1, source_target_pairs={{16,0},{24,8},{0,16},{8,24},{48,32},{56,40},{32,48},{40,56},{80,64... | collective-permute-start | bytes 614408 | tf_op jit(solution)/shard_map/ppermute | solution.py:394
  3.0 1.1 %collective-permute-start = (bf16[80,1280]{1,0:T(8,128)(2,1)}, bf16[80,1280]{1,0:T(8,128)(2,1)S(1)}, u32[]{:S(2)}, u32[]{:S(2)}) collective-permute-start(bf16[80,1280]{1,0:T(8,128)(2,1)} %own.1), channel_id=1, source_target_pairs={{8,0},{16,8},{24,16},{0,24},{40,32},{48,40},{56,48},{32,56},{72,64... | collective-permute-start | bytes 614408 | tf_op jit(solution)/shard_map/ppermute | solution.py:394
  5.1 3.0 %shard_map.82.mark_ref.mark = bf16[16,2,8,768]{3,2,1,0:T(8,128)(2,1)} custom-call(bf16[768,1280]{1,0:T(8,128)(2,1)} %x_ref.3, bf16[768,128]{1,0:T(8,128)(2,1)} %b_ref.3, f32[10,768]{1,0:T(8,128)} %step_ref.3, f32[10,768]{1,0:T(8,128)} %log_ref.3), custom_call_target="tpu_custom_call" | custom-call | flops 251658240 | bytes 3145728 | tf_op jit(solution)/shard_map/pallas_call | solution.py:103
  8.0 1.7 %collective-permute-done.one = bf16[80,1280]{1,0:T(8,128)(2,1)S(1)} collective-permute-done((bf16[80,1280]{1,0:T(8,128)(2,1)}, bf16[80,1280]{1,0:T(8,128)(2,1)S(1)}, u32[]{:S(2)}, u32[]{:S(2)}) %collective-permute-start) | collective-permute-done | bytes 204832 | tf_op jit(solution)/shard_map/ppermute | solution.py:394
  9.8 1.6 %collective-permute-done.2.three = bf16[80,1280]{1,0:T(8,128)(2,1)S(1)} collective-permute-done((bf16[80,1280]{1,0:T(8,128)(2,1)}, bf16[80,1280]{1,0:T(8,128)(2,1)S(1)}, u32[]{:S(2)}, u32[]{:S(2)}) %collective-permute-start.2) | collective-permute-done | bytes 204832 | tf_op jit(solution)/shard_map/ppermute | solution.py:394
  12.6 1.7 %collective-permute-start.3 = (bf16[4,80,1280]{2,1,0:T(8,128)(2,1)}, bf16[4,80,1280]{2,1,0:T(8,128)(2,1)S(1)}, u32[]{:S(2)}, u32[]{:S(2)}) collective-permute-start(bf16[4,80,1280]{2,1,0:T(8,128)(2,1)} %shard_map.85.refs_0_), channel_id=1, source_target_pairs={{32,0},{40,8},{48,16},{56,24},{64,32},{72,40},{80,48},{88,56},{96,... | collective-permute-start | bytes 2457608 | tf_op jit(solution)/shard_map/ppermute | solution.py:394
  14.4 5.6 %all-to-all-start = ((bf16[32,8,768]{2,1,0:T(8,128)(2,1)}), bf16[32,8,768]{2,1,0:T(8,128)(2,1)S(1)}, u32[]{:S(2)}, u32[]{:S(2)}) async-start(bf16[32,8,768]{2,1,0:T(8,128)(2,1)} %bitcast.1), calls=%async_computation | async-start | bytes 786432 | tf_op jit(solution)/shard_map/all_to_all | solution.py:450
  20.0 9.3 %shard_map.83 = (bf16[768,1280]{1,0:T(8,128)(2,1)}, bf16[768,1280]{1,0:T(8,128)(2,1)}) custom-call(bf16[768,1280]{1,0:T(8,128)(2,1)} %x_ref.3, bf16[768,1280]{1,0:T(8,128)(2,1)} %g_ref.1, bf16[768,128]{1,0:T(8,128)(2,1)} %b_ref.3, bf16[768,128]{1,0:T(8,128)(2,1)} %c_ref.3, f32[10,768]{1,0:T(8,128)} %step_ref.3, f32[10,768]{1,0:T(8,128)} %log_ref.3, ...), custom_call_target="tpu_custom_call" | custom-call | flops 1048576 | bytes 41943040 | tf_op jit(solution)/shard_map/pallas_call | solution.py:198
  29.4 1.1 %all-to-all-done.in_ref.refs_3_ = bf16[32,8,768]{2,1,0:T(8,128)(2,1)S(1)} async-done(((bf16[32,8,768]{2,1,0:T(8,128)(2,1)}), bf16[32,8,768]{2,1,0:T(8,128)(2,1)S(1)}, u32[]{:S(2)}, u32[]{:S(2)}) %all-to-all-start) | async-done | bytes 393248 | tf_op jit(solution)/shard_map/all_to_all | solution.py:450
  31.7 1.8 %collective-permute-start.5 = (bf16[4,80,1280]{2,1,0:T(8,128)(2,1)}, bf16[4,80,1280]{2,1,0:T(8,128)(2,1)}, u32[]{:S(2)}, u32[]{:S(2)}) collective-permute-start(bf16[4,80,1280]{2,1,0:T(8,128)(2,1)} %get-tuple-element.33.refs_2_.refs_0_), channel_id=1, source_target_pairs={{64,0},{72,8},{80,16},{88,24},{96,32},{104,40},{112,48},{120,56},{... | collective-permute-start | bytes 2457608 | tf_op jit(solution)/shard_map/ppermute | solution.py:394
  33.4 1.2 %shard_map.84 = bf16[32,8,640]{2,1,0:T(8,128)(2,1)} custom-call(s32[1]{0:T(128)} %bitcast.half_ref, bf16[32,8,768]{2,1,0:T(8,128)(2,1)S(1)} %all-to-all-done.in_ref.refs_3_, bf16[768,1280]{1,0:T(8,128)(2,1)} %get-tuple-element.31.mark_ref.refs_4_.refs_0_), custom_call_target="tpu_custom_call" | custom-call | tf_op jit(solution)/shard_map/pallas_call | solution.py:134
  34.6 5.7 %all-to-all-start.1 = ((bf16[32,8,640]{2,1,0:T(8,128)(2,1)}), bf16[32,8,640]{2,1,0:T(8,128)(2,1)S(1)}, u32[]{:S(2)}, u32[]{:S(2)}) async-start(bf16[32,8,640]{2,1,0:T(8,128)(2,1)} %shard_map.84), calls=%async_computation.1 | async-start | bytes 655360 | tf_op jit(solution)/shard_map/all_to_all | solution.py:457
  41.1 8.5 %all-to-all-done.1.refs_1_ = bf16[32,8,640]{2,1,0:T(8,128)(2,1)S(1)} async-done(((bf16[32,8,640]{2,1,0:T(8,128)(2,1)}), bf16[32,8,640]{2,1,0:T(8,128)(2,1)S(1)}, u32[]{:S(2)}, u32[]{:S(2)}) %all-to-all-start.1) | async-done | bytes 327712 | tf_op jit(solution)/shard_map/all_to_all | solution.py:457
  49.8 2.4 %collective-permute-done.8.refs_8_.refs_6_ = bf16[4,80,1280]{2,1,0:T(8,128)(2,1)S(1)} collective-permute-done((bf16[4,80,1280]{2,1,0:T(8,128)(2,1)}, bf16[4,80,1280]{2,1,0:T(8,128)(2,1)S(1)}, u32[]{:S(2)}, u32[]{:S(2)}) %collective-permute-start.8) | collective-permute-done | bytes 819232 | tf_op jit(solution)/shard_map/ppermute | solution.py:369
  53.1 5.4 %shard_map.88 = (bf16[768,1280]{1,0:T(8,128)(2,1)S(1)}, bf16[160,768]{1,0:T(8,128)(2,1)S(1)}, bf16[160,768]{1,0:T(8,128)(2,1)S(1)}, bf16[2,4,80,1280]{3,2,1,0:T(8,128)(2,1)S(1)}) custom-call(bf16[16,2,8,640]{3,2,1,0:T(8,128)(2,1)S(1)} %bitcast.47, bf16[768,128]{1,0:T(8,128)(2,1)} %c_ref.3, bf16[768,1280]{1,0:T(8,128)(2,1)} %get-tuple-element.31.mark_ref.refs_4_.refs_0_, ...), custom_call_target="tpu_custom_call" | custom-call | flops 629145600 | bytes 2097152 | tf_op jit(solution)/shard_map/pallas_call | solution.py:300
  58.5 2.0 %collective-permute-start.11 = (bf16[160,768]{1,0:T(8,128)(2,1)S(1)}, bf16[160,768]{1,0:T(8,128)(2,1)S(1)}, u32[]{:S(2)}, u32[]{:S(2)}) collective-permute-start(bf16[160,768]{1,0:T(8,128)(2,1)S(1)} %get-tuple-element.40), channel_id=1, source_target_pairs={{0,1},{1,2},{2,3},{3,4},{4,5},{5,6},{6,7},{7,0},{8,9},{9,10},{10,1... | collective-permute-start | bytes 737288 | tf_op jit(solution)/shard_map/ppermute | solution.py:369
  60.5 4.3 %collective-permute-start.10 = (bf16[160,768]{1,0:T(8,128)(2,1)S(1)}, bf16[160,768]{1,0:T(8,128)(2,1)S(1)}, u32[]{:S(2)}, u32[]{:S(2)}) collective-permute-start(bf16[160,768]{1,0:T(8,128)(2,1)S(1)} %get-tuple-element.39), channel_id=1, source_target_pairs={{0,7},{1,0},{2,1},{3,2},{4,3},{5,4},{6,5},{7,6},{8,15},{9,8},{10,9... | collective-permute-start | bytes 737288 | tf_op jit(solution)/shard_map/ppermute | solution.py:369
  64.7 2.9 %shard_map.89 = (bf16[160,768]{1,0:T(8,128)(2,1)S(1)}, bf16[160,768]{1,0:T(8,128)(2,1)S(1)}, bf16[2,160,768]{2,1,0:T(8,128)(2,1)S(1)}, bf16[2,4,80,1280]{3,2,1,0:T(8,128)(2,1)S(1)}) custom-call(bf16[768,1280]{1,0:T(8,128)(2,1)S(1)} %get-tuple-element.45.hidden_ref, bf16[2,4,80,1280]{3,2,1,0:T(8,128)(2,1)S(1)} %get-tuple-element.37.held, ...), custom_call_target="tpu_custom_call" | custom-call | flops 1258291200 | bytes 2097152 | tf_op jit(solution)/shard_map/pallas_call | solution.py:331
  67.6 1.8 %collective-permute-start.13 = (bf16[160,768]{1,0:T(8,128)(2,1)S(1)}, bf16[160,768]{1,0:T(8,128)(2,1)S(1)}, u32[]{:S(2)}, u32[]{:S(2)}) collective-permute-start(bf16[160,768]{1,0:T(8,128)(2,1)S(1)} %get-tuple-element.47), channel_id=1, source_target_pairs={{0,7},{1,0},{2,1},{3,2},{4,3},{5,4},{6,5},{7,6},{8,15},{9,8},{10,9... | collective-permute-start | bytes 737288 | tf_op jit(solution)/shard_map/ppermute | solution.py:369
  69.7 3.1 %shard_map.90 = (bf16[2,2,160,768]{3,2,1,0:T(8,128)(2,1)S(1)}, bf16[3,4,80,1280]{3,2,1,0:T(8,128)(2,1)S(1)}) custom-call(bf16[768,1280]{1,0:T(8,128)(2,1)S(1)} %get-tuple-element.45.hidden_ref, bf16[2,4,80,1280]{3,2,1,0:T(8,128)(2,1)S(1)} %get-tuple-element.41.held, bf16[4,80,1280]{2,1,0:T(8,128)(2,1)} %get-tuple-element.33.refs_2_.refs_0_, ...), custom_call_target="tpu_custom_call" | custom-call | flops 1258291200 | bytes 2097152 | tf_op jit(solution)/shard_map/pallas_call | solution.py:356
  73.0 3.0 %collective-permute-start.18 = (bf16[160,768]{1,0:T(8,128)(2,1)S(1)}, bf16[160,768]{1,0:T(8,128)(2,1)S(1)}, u32[]{:S(2)}, u32[]{:S(2)}) collective-permute-start(bf16[160,768]{1,0:T(8,128)(2,1)S(1)} %fusion.12), channel_id=1, source_target_pairs={{0,7},{1,0},{2,1},{3,2},{4,3},{5,4},{6,5},{7,6},{8,15},{9,8},{10,9... | collective-permute-start | bytes 737288 | tf_op jit(solution)/shard_map/ppermute | solution.py:369
  76.0 2.1 %shard_map.91 = bf16[3,2,160,768]{3,2,1,0:T(8,128)(2,1)S(1)} custom-call(bf16[768,1280]{1,0:T(8,128)(2,1)S(1)} %get-tuple-element.45.hidden_ref, bf16[3,4,80,1280]{3,2,1,0:T(8,128)(2,1)S(1)} %get-tuple-element.46.held, bf16[4,80,1280]{2,1,0:T(8,128)(2,1)} %get-tuple-element.33.refs_2_.refs_0_, bf16[4,80,1280]{2,1,0:T(8,128)(2,1)} %get-tuple-element.34.refs_3_.refs_1_, ...), custom_call_target="tpu_custom_call" | custom-call | flops 1887436800 | bytes 3145728 | tf_op jit(solution)/shard_map/pallas_call | solution.py:356
  78.4 3.3 %collective-permute-start.16 = (bf16[160,768]{1,0:T(8,128)(2,1)S(1)}, bf16[160,768]{1,0:T(8,128)(2,1)S(1)}, u32[]{:S(2)}, u32[]{:S(2)}) collective-permute-start(bf16[160,768]{1,0:T(8,128)(2,1)S(1)} %fusion.8), channel_id=1, source_target_pairs={{0,7},{1,0},{2,1},{3,2},{4,3},{5,4},{6,5},{7,6},{8,15},{9,8},{10,9... | collective-permute-start | bytes 737288 | tf_op jit(solution)/shard_map/ppermute | solution.py:369
  81.7 4.4 %collective-permute-done.12 = bf16[160,768]{1,0:T(8,128)(2,1)S(1)} collective-permute-done((bf16[160,768]{1,0:T(8,128)(2,1)S(1)}, bf16[160,768]{1,0:T(8,128)(2,1)S(1)}, u32[]{:S(2)}, u32[]{:S(2)}) %collective-permute-start.12) | collective-permute-done | bytes 245792 | tf_op jit(solution)/shard_map/ppermute | solution.py:369
  86.4 3.3 %collective-permute-start.22 = (bf16[160,768]{1,0:T(8,128)(2,1)S(1)}, bf16[160,768]{1,0:T(8,128)(2,1)S(1)}, u32[]{:S(2)}, u32[]{:S(2)}) collective-permute-start(bf16[160,768]{1,0:T(8,128)(2,1)S(1)} %fusion.4), channel_id=1, source_target_pairs={{0,7},{1,0},{2,1},{3,2},{4,3},{5,4},{6,5},{7,6},{8,15},{9,8},{10,9... | collective-permute-start | bytes 737288 | tf_op jit(solution)/shard_map/ppermute | solution.py:369
  89.6 1.7 %collective-permute-done.17 = bf16[160,768]{1,0:T(8,128)(2,1)S(1)} collective-permute-done((bf16[160,768]{1,0:T(8,128)(2,1)S(1)}, bf16[160,768]{1,0:T(8,128)(2,1)S(1)}, u32[]{:S(2)}, u32[]{:S(2)}) %collective-permute-start.17) | collective-permute-done | bytes 245792 | tf_op jit(solution)/shard_map/ppermute | solution.py:369
  91.6 3.3 %collective-permute-start.21 = (bf16[160,768]{1,0:T(8,128)(2,1)S(1)}, bf16[160,768]{1,0:T(8,128)(2,1)S(1)}, u32[]{:S(2)}, u32[]{:S(2)}) collective-permute-start(bf16[160,768]{1,0:T(8,128)(2,1)S(1)} %fusion.6), channel_id=1, source_target_pairs={{0,7},{1,0},{2,1},{3,2},{4,3},{5,4},{6,5},{7,6},{8,15},{9,8},{10,9... | collective-permute-start | bytes 737288 | tf_op jit(solution)/shard_map/ppermute | solution.py:369
  94.9 1.7 %collective-permute-done.15 = bf16[160,768]{1,0:T(8,128)(2,1)S(1)} collective-permute-done((bf16[160,768]{1,0:T(8,128)(2,1)S(1)}, bf16[160,768]{1,0:T(8,128)(2,1)S(1)}, u32[]{:S(2)}, u32[]{:S(2)}) %collective-permute-start.15) | collective-permute-done | bytes 245792 | tf_op jit(solution)/shard_map/ppermute | solution.py:369
  96.8 3.0 %collective-permute-start.23 = (bf16[160,768]{1,0:T(8,128)(2,1)S(1)}, bf16[160,768]{1,0:T(8,128)(2,1)S(1)}, u32[]{:S(2)}, u32[]{:S(2)}) collective-permute-start(bf16[160,768]{1,0:T(8,128)(2,1)S(1)} %fusion.3), channel_id=1, source_target_pairs={{0,7},{1,0},{2,1},{3,2},{4,3},{5,4},{6,5},{7,6},{8,15},{9,8},{10,9... | collective-permute-start | bytes 737288 | tf_op jit(solution)/shard_map/ppermute | solution.py:369
  99.9 1.1 collective-permute-done.21
  101.9 1.6 %collective-permute-done.23 = bf16[160,768]{1,0:T(8,128)(2,1)S(1)} collective-permute-done((bf16[160,768]{1,0:T(8,128)(2,1)S(1)}, bf16[160,768]{1,0:T(8,128)(2,1)S(1)}, u32[]{:S(2)}, u32[]{:S(2)}) %collective-permute-start.23) | collective-permute-done | bytes 245792 | tf_op jit(solution)/shard_map/ppermute | solution.py:369
  103.6 3.7 %collective-permute-done.19 = bf16[160,768]{1,0:T(8,128)(2,1)S(1)} collective-permute-done((bf16[160,768]{1,0:T(8,128)(2,1)S(1)}, bf16[160,768]{1,0:T(8,128)(2,1)S(1)}, u32[]{:S(2)}, u32[]{:S(2)}) %collective-permute-start.19) | collective-permute-done | bytes 245792 | tf_op jit(solution)/shard_map/ppermute | solution.py:369
  (58 shorter events, 8.3 us)
Async XLA Ops:
  0.0 11.3 %copy-start = (bf16[80,1280]{1,0:T(8,128)(2,1)S(1)}, bf16[80,1280]{1,0:T(8,128)(2,1)}, u32[]{:S(2)}) copy-start(bf16[80,1280]{1,0:T(8,128)(2,1)} %own.1) | copy-start | bytes 614404
  0.0 8.0 %collective-permute-start.1 = (bf16[80,1280]{1,0:T(8,128)(2,1)}, bf16[80,1280]{1,0:T(8,128)(2,1)S(1)}, u32[]{:S(2)}, u32[]{:S(2)}) collective-permute-start(bf16[80,1280]{1,0:T(8,128)(2,1)} %own.1), channel_id=1, source_target_pairs={{16,0},{24,8},{0,16},{8,24},{48,32},{56,40},{32,48},{40,56},{80,64... | collective-permute-start | bytes 614408 | tf_op jit(solution)/shard_map/ppermute | solution.py:394
  3.0 6.7 %collective-permute-start = (bf16[80,1280]{1,0:T(8,128)(2,1)}, bf16[80,1280]{1,0:T(8,128)(2,1)S(1)}, u32[]{:S(2)}, u32[]{:S(2)}) collective-permute-start(bf16[80,1280]{1,0:T(8,128)(2,1)} %own.1), channel_id=1, source_target_pairs={{8,0},{16,8},{24,16},{0,24},{40,32},{48,40},{56,48},{32,56},{72,64... | collective-permute-start | bytes 614408 | tf_op jit(solution)/shard_map/ppermute | solution.py:394
  4.2 7.2 %collective-permute-start.2 = (bf16[80,1280]{1,0:T(8,128)(2,1)}, bf16[80,1280]{1,0:T(8,128)(2,1)S(1)}, u32[]{:S(2)}, u32[]{:S(2)}) collective-permute-start(bf16[80,1280]{1,0:T(8,128)(2,1)} %own.1), channel_id=1, source_target_pairs={{24,0},{0,8},{8,16},{16,24},{56,32},{32,40},{40,48},{48,56},{88,64... | collective-permute-start | bytes 614408 | tf_op jit(solution)/shard_map/ppermute | solution.py:394
  8.0 12.0 %copy-start.1 = (f32[10]{0:T(128)S(1)}, f32[10]{0:T(128)}, u32[]{:S(2)}) copy-start(f32[10]{0:T(128)} %param.14) | copy-start | bytes 124
  12.4 18.1 %collective-permute-start.4 = (bf16[4,80,1280]{2,1,0:T(8,128)(2,1)}, bf16[4,80,1280]{2,1,0:T(8,128)(2,1)S(1)}, u32[]{:S(2)}, u32[]{:S(2)}) collective-permute-start(bf16[4,80,1280]{2,1,0:T(8,128)(2,1)} %shard_map.85.refs_0_), channel_id=1, source_target_pairs={{96,0},{104,8},{112,16},{120,24},{0,32},{8,40},{16,48},{24,56},{32... | collective-permute-start | bytes 2457608 | tf_op jit(solution)/shard_map/ppermute | solution.py:394
  12.6 17.9 %collective-permute-start.3 = (bf16[4,80,1280]{2,1,0:T(8,128)(2,1)}, bf16[4,80,1280]{2,1,0:T(8,128)(2,1)S(1)}, u32[]{:S(2)}, u32[]{:S(2)}) collective-permute-start(bf16[4,80,1280]{2,1,0:T(8,128)(2,1)} %shard_map.85.refs_0_), channel_id=1, source_target_pairs={{32,0},{40,8},{48,16},{56,24},{64,32},{72,40},{80,48},{88,56},{96,... | collective-permute-start | bytes 2457608 | tf_op jit(solution)/shard_map/ppermute | solution.py:394
  14.4 16.1 %all-to-all-start = ((bf16[32,8,768]{2,1,0:T(8,128)(2,1)}), bf16[32,8,768]{2,1,0:T(8,128)(2,1)S(1)}, u32[]{:S(2)}, u32[]{:S(2)}) async-start(bf16[32,8,768]{2,1,0:T(8,128)(2,1)} %bitcast.1), calls=%async_computation | async-start | bytes 786432 | tf_op jit(solution)/shard_map/all_to_all | solution.py:450
  30.5 1.2 %copy-start.5 = (bf16[4,80,1280]{2,1,0:T(8,128)(2,1)}, bf16[4,80,1280]{2,1,0:T(8,128)(2,1)S(1)}, u32[]{:S(2)}) copy-start(bf16[4,80,1280]{2,1,0:T(8,128)(2,1)S(1)} %collective-permute-done.3.refs_1_) | copy-start | bytes 2457604
  31.7 18.0 %collective-permute-start.5 = (bf16[4,80,1280]{2,1,0:T(8,128)(2,1)}, bf16[4,80,1280]{2,1,0:T(8,128)(2,1)}, u32[]{:S(2)}, u32[]{:S(2)}) collective-permute-start(bf16[4,80,1280]{2,1,0:T(8,128)(2,1)} %get-tuple-element.33.refs_2_.refs_0_), channel_id=1, source_target_pairs={{64,0},{72,8},{80,16},{88,24},{96,32},{104,40},{112,48},{120,56},{... | collective-permute-start | bytes 2457608 | tf_op jit(solution)/shard_map/ppermute | solution.py:394
  33.4 6.9 %copy-start.2 = (bf16[4,80,1280]{2,1,0:T(8,128)(2,1)S(1)}, bf16[4,80,1280]{2,1,0:T(8,128)(2,1)}, u32[]{:S(2)}) copy-start(bf16[4,80,1280]{2,1,0:T(8,128)(2,1)} %get-tuple-element.33.refs_2_.refs_0_) | copy-start | bytes 2457604
  33.4 7.1 %copy-start.6 = (bf16[4,80,1280]{2,1,0:T(8,128)(2,1)S(1)}, bf16[4,80,1280]{2,1,0:T(8,128)(2,1)}, u32[]{:S(2)}) copy-start(bf16[4,80,1280]{2,1,0:T(8,128)(2,1)} %get-tuple-element.34.refs_3_.refs_1_) | copy-start | bytes 2457604
  33.4 7.5 %copy-start.4 = (bf16[4,80,1280]{2,1,0:T(8,128)(2,1)S(1)}, bf16[4,80,1280]{2,1,0:T(8,128)(2,1)}, u32[]{:S(2)}) copy-start(bf16[4,80,1280]{2,1,0:T(8,128)(2,1)} %get-tuple-element.35.refs_5_.refs_3_) | copy-start | bytes 2457604
  34.6 15.0 %all-to-all-start.1 = ((bf16[32,8,640]{2,1,0:T(8,128)(2,1)}), bf16[32,8,640]{2,1,0:T(8,128)(2,1)S(1)}, u32[]{:S(2)}, u32[]{:S(2)}) async-start(bf16[32,8,640]{2,1,0:T(8,128)(2,1)} %shard_map.84), calls=%async_computation.1 | async-start | bytes 655360 | tf_op jit(solution)/shard_map/all_to_all | solution.py:457
  40.3 9.4 %collective-permute-start.6 = (bf16[4,80,1280]{2,1,0:T(8,128)(2,1)S(1)}, bf16[4,80,1280]{2,1,0:T(8,128)(2,1)}, u32[]{:S(2)}, u32[]{:S(2)}) collective-permute-start(bf16[4,80,1280]{2,1,0:T(8,128)(2,1)S(1)} %copy-done.2), channel_id=1, source_target_pairs={{0,128},{128,0},{1,129},{129,1},{2,130},{130,2},{3,131},{131,3},{4... | collective-permute-start | bytes 2457608 | tf_op jit(solution)/shard_map/ppermute | solution.py:369
  40.6 9.2 %collective-permute-start.7 = (bf16[4,80,1280]{2,1,0:T(8,128)(2,1)S(1)}, bf16[4,80,1280]{2,1,0:T(8,128)(2,1)}, u32[]{:S(2)}, u32[]{:S(2)}) collective-permute-start(bf16[4,80,1280]{2,1,0:T(8,128)(2,1)S(1)} %copy-done.6), channel_id=1, source_target_pairs={{0,128},{128,0},{1,129},{129,1},{2,130},{130,2},{3,131},{131,3},{4... | collective-permute-start | bytes 2457608 | tf_op jit(solution)/shard_map/ppermute | solution.py:369
  40.9 8.8 %collective-permute-start.9 = (bf16[4,80,1280]{2,1,0:T(8,128)(2,1)S(1)}, bf16[4,80,1280]{2,1,0:T(8,128)(2,1)}, u32[]{:S(2)}, u32[]{:S(2)}) collective-permute-start(bf16[4,80,1280]{2,1,0:T(8,128)(2,1)S(1)} %copy-done.4), channel_id=1, source_target_pairs={{0,128},{128,0},{1,129},{129,1},{2,130},{130,2},{3,131},{131,3},{4... | collective-permute-start | bytes 2457608 | tf_op jit(solution)/shard_map/ppermute | solution.py:369
  49.6 2.5 %collective-permute-start.8 = (bf16[4,80,1280]{2,1,0:T(8,128)(2,1)}, bf16[4,80,1280]{2,1,0:T(8,128)(2,1)S(1)}, u32[]{:S(2)}, u32[]{:S(2)}) collective-permute-start(bf16[4,80,1280]{2,1,0:T(8,128)(2,1)} %shard_map.87.refs_4_.refs_2_), channel_id=1, source_target_pairs={{0,128},{128,0},{1,129},{129,1},{2,130},{130,2},{3,131},{131,3},{4... | collective-permute-start | bytes 2457608 | tf_op jit(solution)/shard_map/ppermute | solution.py:369
  58.5 14.4 %collective-permute-start.11 = (bf16[160,768]{1,0:T(8,128)(2,1)S(1)}, bf16[160,768]{1,0:T(8,128)(2,1)S(1)}, u32[]{:S(2)}, u32[]{:S(2)}) collective-permute-start(bf16[160,768]{1,0:T(8,128)(2,1)S(1)} %get-tuple-element.40), channel_id=1, source_target_pairs={{0,1},{1,2},{2,3},{3,4},{4,5},{5,6},{6,7},{7,0},{8,9},{9,10},{10,1... | collective-permute-start | bytes 737288 | tf_op jit(solution)/shard_map/ppermute | solution.py:369
  60.5 12.5 %collective-permute-start.10 = (bf16[160,768]{1,0:T(8,128)(2,1)S(1)}, bf16[160,768]{1,0:T(8,128)(2,1)S(1)}, u32[]{:S(2)}, u32[]{:S(2)}) collective-permute-start(bf16[160,768]{1,0:T(8,128)(2,1)S(1)} %get-tuple-element.39), channel_id=1, source_target_pairs={{0,7},{1,0},{2,1},{3,2},{4,3},{5,4},{6,5},{7,6},{8,15},{9,8},{10,9... | collective-permute-start | bytes 737288 | tf_op jit(solution)/shard_map/ppermute | solution.py:369
  67.6 10.7 %collective-permute-start.13 = (bf16[160,768]{1,0:T(8,128)(2,1)S(1)}, bf16[160,768]{1,0:T(8,128)(2,1)S(1)}, u32[]{:S(2)}, u32[]{:S(2)}) collective-permute-start(bf16[160,768]{1,0:T(8,128)(2,1)S(1)} %get-tuple-element.47), channel_id=1, source_target_pairs={{0,7},{1,0},{2,1},{3,2},{4,3},{5,4},{6,5},{7,6},{8,15},{9,8},{10,9... | collective-permute-start | bytes 737288 | tf_op jit(solution)/shard_map/ppermute | solution.py:369
  69.4 8.7 %collective-permute-start.14 = (bf16[160,768]{1,0:T(8,128)(2,1)S(1)}, bf16[160,768]{1,0:T(8,128)(2,1)S(1)}, u32[]{:S(2)}, u32[]{:S(2)}) collective-permute-start(bf16[160,768]{1,0:T(8,128)(2,1)S(1)} %get-tuple-element.48), channel_id=1, source_target_pairs={{0,1},{1,2},{2,3},{3,4},{4,5},{5,6},{6,7},{7,0},{8,9},{9,10},{10,1... | collective-permute-start | bytes 737288 | tf_op jit(solution)/shard_map/ppermute | solution.py:369
  73.0 13.3 %collective-permute-start.18 = (bf16[160,768]{1,0:T(8,128)(2,1)S(1)}, bf16[160,768]{1,0:T(8,128)(2,1)S(1)}, u32[]{:S(2)}, u32[]{:S(2)}) collective-permute-start(bf16[160,768]{1,0:T(8,128)(2,1)S(1)} %fusion.12), channel_id=1, source_target_pairs={{0,7},{1,0},{2,1},{3,2},{4,3},{5,4},{6,5},{7,6},{8,15},{9,8},{10,9... | collective-permute-start | bytes 737288 | tf_op jit(solution)/shard_map/ppermute | solution.py:369
  76.0 10.1 %collective-permute-start.12 = (bf16[160,768]{1,0:T(8,128)(2,1)S(1)}, bf16[160,768]{1,0:T(8,128)(2,1)S(1)}, u32[]{:S(2)}, u32[]{:S(2)}) collective-permute-start(bf16[160,768]{1,0:T(8,128)(2,1)S(1)} %fusion.11), channel_id=1, source_target_pairs={{0,1},{1,2},{2,3},{3,4},{4,5},{5,6},{6,7},{7,0},{8,9},{9,10},{10,1... | collective-permute-start | bytes 737288 | tf_op jit(solution)/shard_map/ppermute | solution.py:369
  78.2 13.2 %collective-permute-start.17 = (bf16[160,768]{1,0:T(8,128)(2,1)S(1)}, bf16[160,768]{1,0:T(8,128)(2,1)S(1)}, u32[]{:S(2)}, u32[]{:S(2)}) collective-permute-start(bf16[160,768]{1,0:T(8,128)(2,1)S(1)} %fusion.7), channel_id=1, source_target_pairs={{0,1},{1,2},{2,3},{3,4},{4,5},{5,6},{6,7},{7,0},{8,9},{9,10},{10,1... | collective-permute-start | bytes 737288 | tf_op jit(solution)/shard_map/ppermute | solution.py:369
  78.4 13.2 %collective-permute-start.16 = (bf16[160,768]{1,0:T(8,128)(2,1)S(1)}, bf16[160,768]{1,0:T(8,128)(2,1)S(1)}, u32[]{:S(2)}, u32[]{:S(2)}) collective-permute-start(bf16[160,768]{1,0:T(8,128)(2,1)S(1)} %fusion.8), channel_id=1, source_target_pairs={{0,7},{1,0},{2,1},{3,2},{4,3},{5,4},{6,5},{7,6},{8,15},{9,8},{10,9... | collective-permute-start | bytes 737288 | tf_op jit(solution)/shard_map/ppermute | solution.py:369
  86.2 10.5 %collective-permute-start.15 = (bf16[160,768]{1,0:T(8,128)(2,1)S(1)}, bf16[160,768]{1,0:T(8,128)(2,1)S(1)}, u32[]{:S(2)}, u32[]{:S(2)}) collective-permute-start(bf16[160,768]{1,0:T(8,128)(2,1)S(1)} %fusion.9), channel_id=1, source_target_pairs={{0,1},{1,2},{2,3},{3,4},{4,5},{5,6},{6,7},{7,0},{8,9},{9,10},{10,1... | collective-permute-start | bytes 737288 | tf_op jit(solution)/shard_map/ppermute | solution.py:369
  86.4 10.4 %collective-permute-start.22 = (bf16[160,768]{1,0:T(8,128)(2,1)S(1)}, bf16[160,768]{1,0:T(8,128)(2,1)S(1)}, u32[]{:S(2)}, u32[]{:S(2)}) collective-permute-start(bf16[160,768]{1,0:T(8,128)(2,1)S(1)} %fusion.4), channel_id=1, source_target_pairs={{0,7},{1,0},{2,1},{3,2},{4,3},{5,4},{6,5},{7,6},{8,15},{9,8},{10,9... | collective-permute-start | bytes 737288 | tf_op jit(solution)/shard_map/ppermute | solution.py:369
  91.5 10.5 %collective-permute-start.20 = (bf16[160,768]{1,0:T(8,128)(2,1)S(1)}, bf16[160,768]{1,0:T(8,128)(2,1)S(1)}, u32[]{:S(2)}, u32[]{:S(2)}) collective-permute-start(bf16[160,768]{1,0:T(8,128)(2,1)S(1)} %fusion.5), channel_id=1, source_target_pairs={{0,1},{1,2},{2,3},{3,4},{4,5},{5,6},{6,7},{7,0},{8,9},{9,10},{10,1... | collective-permute-start | bytes 737288 | tf_op jit(solution)/shard_map/ppermute | solution.py:369
  91.6 9.3 %collective-permute-start.21 = (bf16[160,768]{1,0:T(8,128)(2,1)S(1)}, bf16[160,768]{1,0:T(8,128)(2,1)S(1)}, u32[]{:S(2)}, u32[]{:S(2)}) collective-permute-start(bf16[160,768]{1,0:T(8,128)(2,1)S(1)} %fusion.6), channel_id=1, source_target_pairs={{0,7},{1,0},{2,1},{3,2},{4,3},{5,4},{6,5},{7,6},{8,15},{9,8},{10,9... | collective-permute-start | bytes 737288 | tf_op jit(solution)/shard_map/ppermute | solution.py:369
  96.8 6.8 %collective-permute-start.23 = (bf16[160,768]{1,0:T(8,128)(2,1)S(1)}, bf16[160,768]{1,0:T(8,128)(2,1)S(1)}, u32[]{:S(2)}, u32[]{:S(2)}) collective-permute-start(bf16[160,768]{1,0:T(8,128)(2,1)S(1)} %fusion.3), channel_id=1, source_target_pairs={{0,7},{1,0},{2,1},{3,2},{4,3},{5,4},{6,5},{7,6},{8,15},{9,8},{10,9... | collective-permute-start | bytes 737288 | tf_op jit(solution)/shard_map/ppermute | solution.py:369
  99.8 7.4 %collective-permute-start.19 = (bf16[160,768]{1,0:T(8,128)(2,1)S(1)}, bf16[160,768]{1,0:T(8,128)(2,1)S(1)}, u32[]{:S(2)}, u32[]{:S(2)}) collective-permute-start(bf16[160,768]{1,0:T(8,128)(2,1)S(1)} %fusion.10), channel_id=1, source_target_pairs={{0,1},{1,2},{2,3},{3,4},{4,5},{5,6},{6,7},{7,0},{8,9},{9,10},{10,1... | collective-permute-start | bytes 737288 | tf_op jit(solution)/shard_map/ppermute | solution.py:369
  (2 other events, 1.8 us)

commit v4 on v3

--- a/solution.py
+++ b/solution.py
@@ -266,53 +266,65 @@
     return pltpu.VMEM((count, 4, ROWS, CH), BF16)
 
 
-def first_body(in_ref, c_ref, *refs):
-    parts, refs = refs[:2], refs[2:]
-    refs, (hidden_ref, up_ref, down_ref, later, pre, gain, part_sems, held, sems, later_sems) = refs[:8], refs[8:]
-    rows = TOK // 2
-    copies = []
-    for i in range(2):
-        here = pl.ds(i * rows, rows)
-        for j, (part, held_part) in enumerate(zip(parts, (pre, gain))):
-            copies.append(pltpu.make_async_copy(part.at[here], held_part.at[here], part_sems.at[i, j]))
-            copies[-1].start()
-        if i == 0:
-            fetch(refs, held, sems, FAR)
+def hidden_body(in_ref, c_ref, pre_ref, gain_ref, hidden_ref, state_ref):
+    rows = c_ref.shape[0]
+    here = pl.ds(pl.multiple_of(pl.program_id(0) * rows, rows), rows)
+
+    @pl.when(pl.program_id(0) == 0)
+    def _():
+        for half in range(2):
+            state_ref[half] = in_ref[:, half].astype(F32).reshape(N, HALF).astype(BF16)
+
+    for half in range(2):
+        cols = slice(half * HALF, (half + 1) * HALF)
+        carried = jnp.dot(c_ref[...], state_ref[half], preferred_element_type=F32)
+        hidden_ref[here, cols] = (pre_ref[:, cols].astype(F32) + gain_ref[:, cols].astype(F32) * carried).astype(BF16)
+
+
+def hidden_of(entering, c, pre, gain):
+    rows = 256
+    return pl.pallas_call(
+        hidden_body,
+        grid=(TOK // rows,),
+        in_specs=[
+            pl.BlockSpec((16, 2, 8, HALF), lambda i: (0, 0, 0, 0)),
+            pl.BlockSpec((rows, N), lambda i: (i, 0)),
+            pl.BlockSpec((rows, CH), lambda i: (i, 0)),
+            pl.BlockSpec((rows, CH), lambda i: (i, 0)),
+        ],
+        out_specs=IN_VMEM,
+        out_shape=pltpu.VMEM((TOK, CH), BF16),
+        scratch_shapes=[pltpu.VMEM((2, N, HALF), BF16)],
+        compiler_params=SMALL,
+        cost_estimate=pl.CostEstimate(flops=2 * TOK * N * CH, bytes_accessed=5 << 20, transcendentals=0),
+    )(entering, *[in_hbm(v) for v in (c, pre, gain)])
+
+
+def in_place(blocks):
+    return [v if k == 6 else in_hbm(v) for k, v in enumerate(blocks)]
+
+
+def far_body(hidden_ref, *refs):
+    refs, (up_ref, down_ref, later, held, sems, later_sems) = refs[:8], refs[8:]
+    fetch(refs, held, sems, FAR)
     fetch(refs, later, later_sems, NEAR)
-    states = [in_ref[:, half].astype(F32).reshape(N, HALF).astype(BF16) for half in range(2)]
-    for i in range(2):
-        here = slice(i * rows, (i + 1) * rows)
-        copies[2 * i].wait()
-        copies[2 * i + 1].wait()
-        for half in range(2):
-            cols = slice(half * HALF, (half + 1) * HALF)
-            carried = jnp.dot(c_ref[here, :], states[half], preferred_element_type=F32)
-            hidden_ref[here, cols] = (pre[here, cols].astype(F32) + gain[here, cols].astype(F32) * carried).astype(BF16)
-        if i == 0:
-            arrive(refs, held, sems)
-        out = product(held, 0, hidden_ref[here, :])
-        up_ref[:, here] = out[:PIECE]
-        down_ref[:, here] = out[PIECE:]
+    arrive(refs, held, sems)
+    out = product(held, 0, hidden_ref[...])
+    up_ref[...] = out[:PIECE]
+    down_ref[...] = out[PIECE:]
     arrive(refs, later, later_sems)
 
 
-def first_parts(entering, c, parts, blocks):
-    return pl.pallas_call(
-        first_body,
-        in_specs=[IN_VMEM] * 2 + [ANYWHERE] * 10,
-        out_specs=[IN_VMEM] * 4,
-        out_shape=[pltpu.VMEM((TOK, CH), BF16)] + [jax.ShapeDtypeStruct((PIECE, TOK), BF16)] * 2 + [held_weights(2)],
-        scratch_shapes=[
-            pltpu.VMEM((TOK, CH), BF16),
-            pltpu.VMEM((TOK, CH), BF16),
-            pltpu.SemaphoreType.DMA((2, 2)),
-            held_weights(1),
-            pltpu.SemaphoreType.DMA((1, 4)),
-            pltpu.SemaphoreType.DMA((2, 4)),
-        ],
+def far_parts(hidden, blocks):
+    return pl.pallas_call(
+        far_body,
+        in_specs=[IN_VMEM] + [ANYWHERE] * 8,
+        out_specs=[IN_VMEM] * 3,
+        out_shape=[jax.ShapeDtypeStruct((PIECE, TOK), BF16)] * 2 + [held_weights(2)],
+        scratch_shapes=[held_weights(1), pltpu.SemaphoreType.DMA((1, 4)), pltpu.SemaphoreType.DMA((2, 4))],
         compiler_params=SMALL,
         cost_estimate=pl.CostEstimate(flops=2 * 320 * TOK * CH, bytes_accessed=2 << 20, transcendentals=0),
-    )(entering, *[in_hbm(v) for v in (c, *parts, *blocks)])
+    )(in_vmem(hidden), *in_place(blocks))
 
 
 def near_body(ups, hidden_ref, held, *refs):
@@ -337,7 +349,7 @@
         scratch_shapes=[pltpu.SemaphoreType.DMA((len(ups), 4))],
         compiler_params=SMALL,
         cost_estimate=pl.CostEstimate(flops=4 * 320 * TOK * CH, bytes_accessed=2 << 20, transcendentals=0),
-    )(in_vmem(hidden), in_vmem(held), *[in_hbm(v) for v in blocks])
+    )(in_vmem(hidden), in_vmem(held), *in_place(blocks))
 
 
 def rest_body(ups, hidden_ref, held, *refs):
@@ -361,7 +373,7 @@
         scratch_shapes=[pltpu.SemaphoreType.DMA((later, 4))] if later else [],
         compiler_params=SMALL,
         cost_estimate=pl.CostEstimate(flops=2 * count * 320 * TOK * CH, bytes_accessed=count << 20, transcendentals=0),
-    )(in_vmem(hidden), in_vmem(held), *[in_hbm(v) for v in blocks])
+    )(in_vmem(hidden), in_vmem(held), *in_place(blocks))
 
 
 def shift(value, axis, by):
@@ -411,7 +423,8 @@
 
 
 def projected(entering, c, parts, blocks):
-    hidden, ua, db, held = first_parts(entering, c, parts, blocks)
+    hidden = hidden_of(entering, c, *parts)
+    ua, db, held = far_parts(hidden, blocks)
     ua, db = shift(ua, "head", 1), shift(db, "head", -1)
     ub, da, keep, held = near_parts(hidden, held, blocks, NEXT)
     ub, da = shift(ub, "head", 1), shift(da, "head", -1)

time: 109 us -> 105 us (0.963)
  waiting for transfers between devices: 30.7 us -> 28.3 us
  Pallas kernels: 28 us -> 26.6 us
    ppermute x18, waiting for transfers between devices: 17.7 us -> 15.4 us  [shift(): lax.ppermute(value, axis, [(i, (i + by) % size) for i in range(size)])]
    pallas_call x2, Pallas kernels: 5.24 us -> 4.03 us  [rest_parts(): pl.pallas_call(functools.partial(rest_body, ups), in_specs=[IN_VMEM, IN_V...]
    pallas_call x1 -> x2, Pallas kernels: 5.38 us -> 5.69 us  [the longest x1 3.41 us: hidden_of(): pl.pallas_call(hidden_body, grid=(TOK // rows,), in_specs=[pl.BlockSpec((...]
  transfers between devices with their start and end apart: 26 -> 26, of which waited for: 12 -> 12; matrix products, arithmetic and copies ran while one was open for 1% -> 1% of each run, Pallas kernels for 20% -> 22%
where the time goes in v4:
time: 105 us; the launch traced here: 104 us
  starting transfers between devices  46.4 us (44%)
  waiting for transfers between devices  28.3 us (27%)
  Pallas kernels  26.6 us (25%)
  other arithmetic  1.59 us (2%)
  local copies, waits for them, and re-layouts  1.27 us (1%)
    ppermute x18, starting transfers between devices, shift(): lax.ppermute(value, axis, [(i, (i + by) % size) for i in range(size)])  26.2 us
    ppermute x18, waiting for transfers between devices, shift(): lax.ppermute(value, axis, [(i, (i + by) % size) for i in range(size)])  15.4 us
    pallas_call x1, Pallas kernels, inner(): pl.pallas_call(inner_body, grid=(NBLK,), in_specs=[pl.BlockSpec((BLK, CH)...  9.34 us
    ppermute x6, starting transfers between devices, from_line(): return lax.ppermute(value, ('seq', 'row'), pairs)  8.85 us
    all_to_all x1, waiting for transfers between devices, shards(): entering = lax.all_to_all(slices, ('seq', 'row'), 0, 0)  8.53 us
    all_to_all x1, starting transfers between devices, shards(): entering = lax.all_to_all(slices, ('seq', 'row'), 0, 0)  5.67 us
    all_to_all x1, starting transfers between devices, shards(): lax.all_to_all(payload.reshape(SHARDS, 8, HALF + P_SIZE), ('seq', 'row'),...  5.64 us
    pallas_call x2, Pallas kernels, rest_parts(): pl.pallas_call(functools.partial(rest_body, ups), in_specs=[IN_VMEM, IN_V...  4.03 us
  transfers between devices with their start and end apart: 26, of which 12 were waited for; matrix products, arithmetic and copies ran while one was open for 1% of the time, Pallas kernels for 22%

profile of v4, /device:TPU:24, one launch (start us, length us, event | category | flops | bytes accessed | tf_op | source)
XLA Modules:
  0.0 104.5 jit_solution(3360656793943189140)
XLA Ops:
  0.0 3.0 %collective-permute-start.1 = (bf16[80,1280]{1,0:T(8,128)(2,1)}, bf16[80,1280]{1,0:T(8,128)(2,1)S(1)}, u32[]{:S(2)}, u32[]{:S(2)}) collective-permute-start(bf16[80,1280]{1,0:T(8,128)(2,1)} %own.1), channel_id=1, source_target_pairs={{16,0},{24,8},{0,16},{8,24},{48,32},{56,40},{32,48},{40,56},{80,64... | collective-permute-start | bytes 614408 | tf_op jit(solution)/shard_map/ppermute | solution.py:406
  3.0 1.1 %collective-permute-start = (bf16[80,1280]{1,0:T(8,128)(2,1)}, bf16[80,1280]{1,0:T(8,128)(2,1)S(1)}, u32[]{:S(2)}, u32[]{:S(2)}) collective-permute-start(bf16[80,1280]{1,0:T(8,128)(2,1)} %own.1), channel_id=1, source_target_pairs={{8,0},{16,8},{24,16},{0,24},{40,32},{48,40},{56,48},{32,56},{72,64... | collective-permute-start | bytes 614408 | tf_op jit(solution)/shard_map/ppermute | solution.py:406
  5.1 3.0 %shard_map.82.mark_ref.mark = bf16[16,2,8,768]{3,2,1,0:T(8,128)(2,1)} custom-call(bf16[768,1280]{1,0:T(8,128)(2,1)} %x_ref.3, bf16[768,128]{1,0:T(8,128)(2,1)} %b_ref.3, f32[10,768]{1,0:T(8,128)} %step_ref.3, f32[10,768]{1,0:T(8,128)} %log_ref.3), custom_call_target="tpu_custom_call" | custom-call | flops 251658240 | bytes 3145728 | tf_op jit(solution)/shard_map/pallas_call | solution.py:103
  8.0 1.7 %collective-permute-done.one = bf16[80,1280]{1,0:T(8,128)(2,1)S(1)} collective-permute-done((bf16[80,1280]{1,0:T(8,128)(2,1)}, bf16[80,1280]{1,0:T(8,128)(2,1)S(1)}, u32[]{:S(2)}, u32[]{:S(2)}) %collective-permute-start) | collective-permute-done | bytes 204832 | tf_op jit(solution)/shard_map/ppermute | solution.py:406
  9.8 1.6 %collective-permute-done.2.three = bf16[80,1280]{1,0:T(8,128)(2,1)S(1)} collective-permute-done((bf16[80,1280]{1,0:T(8,128)(2,1)}, bf16[80,1280]{1,0:T(8,128)(2,1)S(1)}, u32[]{:S(2)}, u32[]{:S(2)}) %collective-permute-start.2) | collective-permute-done | bytes 204832 | tf_op jit(solution)/shard_map/ppermute | solution.py:406
  12.6 1.7 %collective-permute-start.3 = (bf16[4,80,1280]{2,1,0:T(8,128)(2,1)}, bf16[4,80,1280]{2,1,0:T(8,128)(2,1)S(1)}, u32[]{:S(2)}, u32[]{:S(2)}) collective-permute-start(bf16[4,80,1280]{2,1,0:T(8,128)(2,1)} %shard_map.86.refs_0_), channel_id=1, source_target_pairs={{32,0},{40,8},{48,16},{56,24},{64,32},{72,40},{80,48},{88,56},{96,... | collective-permute-start | bytes 2457608 | tf_op jit(solution)/shard_map/ppermute | solution.py:406
  14.3 5.6 %all-to-all-start = ((bf16[32,8,768]{2,1,0:T(8,128)(2,1)}), bf16[32,8,768]{2,1,0:T(8,128)(2,1)S(1)}, u32[]{:S(2)}, u32[]{:S(2)}) async-start(bf16[32,8,768]{2,1,0:T(8,128)(2,1)} %bitcast.1), calls=%async_computation | async-start | bytes 786432 | tf_op jit(solution)/shard_map/all_to_all | solution.py:463
  20.0 9.3 %shard_map.83 = (bf16[768,1280]{1,0:T(8,128)(2,1)}, bf16[768,1280]{1,0:T(8,128)(2,1)}) custom-call(bf16[768,1280]{1,0:T(8,128)(2,1)} %x_ref.3, bf16[768,1280]{1,0:T(8,128)(2,1)} %g_ref.1, bf16[768,128]{1,0:T(8,128)(2,1)} %b_ref.3, bf16[768,128]{1,0:T(8,128)(2,1)} %c_ref.3, f32[10,768]{1,0:T(8,128)} %step_ref.3, f32[10,768]{1,0:T(8,128)} %log_ref.3, ...), custom_call_target="tpu_custom_call" | custom-call | flops 1048576 | bytes 41943040 | tf_op jit(solution)/shard_map/pallas_call | solution.py:198
  29.3 1.1 %all-to-all-done.in_ref.refs_3_ = bf16[32,8,768]{2,1,0:T(8,128)(2,1)S(1)} async-done(((bf16[32,8,768]{2,1,0:T(8,128)(2,1)}), bf16[32,8,768]{2,1,0:T(8,128)(2,1)S(1)}, u32[]{:S(2)}, u32[]{:S(2)}) %all-to-all-start) | async-done | bytes 393248 | tf_op jit(solution)/shard_map/all_to_all | solution.py:463
  31.7 1.8 %collective-permute-start.5 = (bf16[4,80,1280]{2,1,0:T(8,128)(2,1)}, bf16[4,80,1280]{2,1,0:T(8,128)(2,1)}, u32[]{:S(2)}, u32[]{:S(2)}) collective-permute-start(bf16[4,80,1280]{2,1,0:T(8,128)(2,1)} %get-tuple-element.32.refs_0_), channel_id=1, source_target_pairs={{64,0},{72,8},{80,16},{88,24},{96,32},{104,40},{112,48},{120,56},{... | collective-permute-start | bytes 2457608 | tf_op jit(solution)/shard_map/ppermute | solution.py:406
  33.4 1.2 %shard_map.84 = bf16[32,8,640]{2,1,0:T(8,128)(2,1)} custom-call(s32[1]{0:T(128)} %bitcast.half_ref, bf16[32,8,768]{2,1,0:T(8,128)(2,1)S(1)} %all-to-all-done.in_ref.refs_3_, bf16[768,1280]{1,0:T(8,128)(2,1)} %get-tuple-element.30.mark_ref.pre_ref.refs_4_), custom_call_target="tpu_custom_call" | custom-call | tf_op jit(solution)/shard_map/pallas_call | solution.py:134
  34.6 5.7 %all-to-all-start.1 = ((bf16[32,8,640]{2,1,0:T(8,128)(2,1)}), bf16[32,8,640]{2,1,0:T(8,128)(2,1)S(1)}, u32[]{:S(2)}, u32[]{:S(2)}) async-start(bf16[32,8,640]{2,1,0:T(8,128)(2,1)} %shard_map.84), calls=%async_computation.1 | async-start | bytes 655360 | tf_op jit(solution)/shard_map/all_to_all | solution.py:470
  41.1 8.5 %all-to-all-done.1.refs_1_ = bf16[32,8,640]{2,1,0:T(8,128)(2,1)S(1)} async-done(((bf16[32,8,640]{2,1,0:T(8,128)(2,1)}), bf16[32,8,640]{2,1,0:T(8,128)(2,1)S(1)}, u32[]{:S(2)}, u32[]{:S(2)}) %all-to-all-start.1) | async-done | bytes 327712 | tf_op jit(solution)/shard_map/all_to_all | solution.py:470
  49.8 3.4 %shard_map.85.hidden_ref = bf16[768,1280]{1,0:T(8,128)(2,1)S(1)} custom-call(bf16[16,2,8,640]{3,2,1,0:T(8,128)(2,1)S(1)} %bitcast.47, bf16[768,128]{1,0:T(8,128)(2,1)} %c_ref.3, bf16[768,1280]{1,0:T(8,128)(2,1)} %get-tuple-element.30.mark_ref.pre_ref.refs_4_, bf16[768,1280]{1,0:T(8,128)(2,1)} %get-tuple-element.31.gain_ref), custom_call_target="tpu_custom_call" | custom-call | flops 251658240 | bytes 5242880 | tf_op jit(solution)/shard_map/pallas_call | solution.py:286
  53.2 2.3 %shard_map.89 = (bf16[160,768]{1,0:T(8,128)(2,1)S(1)}, bf16[160,768]{1,0:T(8,128)(2,1)S(1)}, bf16[2,4,80,1280]{3,2,1,0:T(8,128)(2,1)S(1)}) custom-call(bf16[768,1280]{1,0:T(8,128)(2,1)S(1)} %shard_map.85.hidden_ref, bf16[4,80,1280]{2,1,0:T(8,128)(2,1)} %get-tuple-element.32.refs_0_, bf16[4,80,1280]{2,1,0:T(8,128)(2,1)} %get-tuple-element.33.refs_1_, ...), custom_call_target="tpu_custom_call" | custom-call | flops 629145600 | bytes 2097152 | tf_op jit(solution)/shard_map/pallas_call | solution.py:319
  55.5 2.0 %collective-permute-start.11 = (bf16[160,768]{1,0:T(8,128)(2,1)S(1)}, bf16[160,768]{1,0:T(8,128)(2,1)S(1)}, u32[]{:S(2)}, u32[]{:S(2)}) collective-permute-start(bf16[160,768]{1,0:T(8,128)(2,1)S(1)} %get-tuple-element.38), channel_id=1, source_target_pairs={{0,1},{1,2},{2,3},{3,4},{4,5},{5,6},{6,7},{7,0},{8,9},{9,10},{10,1... | collective-permute-start | bytes 737288 | tf_op jit(solution)/shard_map/ppermute | solution.py:381
  57.5 4.2 %collective-permute-start.10 = (bf16[160,768]{1,0:T(8,128)(2,1)S(1)}, bf16[160,768]{1,0:T(8,128)(2,1)S(1)}, u32[]{:S(2)}, u32[]{:S(2)}) collective-permute-start(bf16[160,768]{1,0:T(8,128)(2,1)S(1)} %get-tuple-element.37), channel_id=1, source_target_pairs={{0,7},{1,0},{2,1},{3,2},{4,3},{5,4},{6,5},{7,6},{8,15},{9,8},{10,9... | collective-permute-start | bytes 737288 | tf_op jit(solution)/shard_map/ppermute | solution.py:381
  61.7 2.5 %shard_map.90 = (bf16[160,768]{1,0:T(8,128)(2,1)S(1)}, bf16[160,768]{1,0:T(8,128)(2,1)S(1)}, bf16[2,160,768]{2,1,0:T(8,128)(2,1)S(1)}, bf16[2,4,80,1280]{3,2,1,0:T(8,128)(2,1)S(1)}) custom-call(bf16[768,1280]{1,0:T(8,128)(2,1)S(1)} %shard_map.85.hidden_ref, bf16[2,4,80,1280]{3,2,1,0:T(8,128)(2,1)S(1)} %get-tuple-element.35.held, ...), custom_call_target="tpu_custom_call" | custom-call | flops 1258291200 | bytes 2097152 | tf_op jit(solution)/shard_map/pallas_call | solution.py:343
  64.2 1.8 %collective-permute-start.13 = (bf16[160,768]{1,0:T(8,128)(2,1)S(1)}, bf16[160,768]{1,0:T(8,128)(2,1)S(1)}, u32[]{:S(2)}, u32[]{:S(2)}) collective-permute-start(bf16[160,768]{1,0:T(8,128)(2,1)S(1)} %get-tuple-element.45), channel_id=1, source_target_pairs={{0,7},{1,0},{2,1},{3,2},{4,3},{5,4},{6,5},{7,6},{8,15},{9,8},{10,9... | collective-permute-start | bytes 737288 | tf_op jit(solution)/shard_map/ppermute | solution.py:381
  66.3 1.9 %shard_map.91 = (bf16[2,2,160,768]{3,2,1,0:T(8,128)(2,1)S(1)}, bf16[3,4,80,1280]{3,2,1,0:T(8,128)(2,1)S(1)}) custom-call(bf16[768,1280]{1,0:T(8,128)(2,1)S(1)} %shard_map.85.hidden_ref, bf16[2,4,80,1280]{3,2,1,0:T(8,128)(2,1)S(1)} %get-tuple-element.39.held, bf16[4,80,1280]{2,1,0:T(8,128)(2,1)} %get-tuple-element.32.refs_0_, ...), custom_call_target="tpu_custom_call" | custom-call | flops 1258291200 | bytes 2097152 | tf_op jit(solution)/shard_map/pallas_call | solution.py:368
  68.3 4.0 %collective-permute-start.18 = (bf16[160,768]{1,0:T(8,128)(2,1)S(1)}, bf16[160,768]{1,0:T(8,128)(2,1)S(1)}, u32[]{:S(2)}, u32[]{:S(2)}) collective-permute-start(bf16[160,768]{1,0:T(8,128)(2,1)S(1)} %fusion.12), channel_id=1, source_target_pairs={{0,7},{1,0},{2,1},{3,2},{4,3},{5,4},{6,5},{7,6},{8,15},{9,8},{10,9... | collective-permute-start | bytes 737288 | tf_op jit(solution)/shard_map/ppermute | solution.py:381
  72.3 2.1 %shard_map.92 = bf16[3,2,160,768]{3,2,1,0:T(8,128)(2,1)S(1)} custom-call(bf16[768,1280]{1,0:T(8,128)(2,1)S(1)} %shard_map.85.hidden_ref, bf16[3,4,80,1280]{3,2,1,0:T(8,128)(2,1)S(1)} %get-tuple-element.44.held, bf16[4,80,1280]{2,1,0:T(8,128)(2,1)} %get-tuple-element.32.refs_0_, bf16[4,80,1280]{2,1,0:T(8,128)(2,1)} %get-tuple-element.33.refs_1_, ...), custom_call_target="tpu_custom_call" | custom-call | flops 1887436800 | bytes 3145728 | tf_op jit(solution)/shard_map/pallas_call | solution.py:368
  75.6 3.3 %collective-permute-start.16 = (bf16[160,768]{1,0:T(8,128)(2,1)S(1)}, bf16[160,768]{1,0:T(8,128)(2,1)S(1)}, u32[]{:S(2)}, u32[]{:S(2)}) collective-permute-start(bf16[160,768]{1,0:T(8,128)(2,1)S(1)} %fusion.8), channel_id=1, source_target_pairs={{0,7},{1,0},{2,1},{3,2},{4,3},{5,4},{6,5},{7,6},{8,15},{9,8},{10,9... | collective-permute-start | bytes 737288 | tf_op jit(solution)/shard_map/ppermute | solution.py:381
  78.8 3.6 %collective-permute-done.12 = bf16[160,768]{1,0:T(8,128)(2,1)S(1)} collective-permute-done((bf16[160,768]{1,0:T(8,128)(2,1)S(1)}, bf16[160,768]{1,0:T(8,128)(2,1)S(1)}, u32[]{:S(2)}, u32[]{:S(2)}) %collective-permute-start.12) | collective-permute-done | bytes 245792 | tf_op jit(solution)/shard_map/ppermute | solution.py:381
  82.7 3.3 %collective-permute-start.22 = (bf16[160,768]{1,0:T(8,128)(2,1)S(1)}, bf16[160,768]{1,0:T(8,128)(2,1)S(1)}, u32[]{:S(2)}, u32[]{:S(2)}) collective-permute-start(bf16[160,768]{1,0:T(8,128)(2,1)S(1)} %fusion.4), channel_id=1, source_target_pairs={{0,7},{1,0},{2,1},{3,2},{4,3},{5,4},{6,5},{7,6},{8,15},{9,8},{10,9... | collective-permute-start | bytes 737288 | tf_op jit(solution)/shard_map/ppermute | solution.py:381
  86.0 1.7 %collective-permute-done.17 = bf16[160,768]{1,0:T(8,128)(2,1)S(1)} collective-permute-done((bf16[160,768]{1,0:T(8,128)(2,1)S(1)}, bf16[160,768]{1,0:T(8,128)(2,1)S(1)}, u32[]{:S(2)}, u32[]{:S(2)}) %collective-permute-start.17) | collective-permute-done | bytes 245792 | tf_op jit(solution)/shard_map/ppermute | solution.py:381
  87.9 3.3 %collective-permute-start.21 = (bf16[160,768]{1,0:T(8,128)(2,1)S(1)}, bf16[160,768]{1,0:T(8,128)(2,1)S(1)}, u32[]{:S(2)}, u32[]{:S(2)}) collective-permute-start(bf16[160,768]{1,0:T(8,128)(2,1)S(1)} %fusion.6), channel_id=1, source_target_pairs={{0,7},{1,0},{2,1},{3,2},{4,3},{5,4},{6,5},{7,6},{8,15},{9,8},{10,9... | collective-permute-start | bytes 737288 | tf_op jit(solution)/shard_map/ppermute | solution.py:381
  91.2 1.7 %collective-permute-done.15 = bf16[160,768]{1,0:T(8,128)(2,1)S(1)} collective-permute-done((bf16[160,768]{1,0:T(8,128)(2,1)S(1)}, bf16[160,768]{1,0:T(8,128)(2,1)S(1)}, u32[]{:S(2)}, u32[]{:S(2)}) %collective-permute-start.15) | collective-permute-done | bytes 245792 | tf_op jit(solution)/shard_map/ppermute | solution.py:381
  93.1 2.9 %collective-permute-start.23 = (bf16[160,768]{1,0:T(8,128)(2,1)S(1)}, bf16[160,768]{1,0:T(8,128)(2,1)S(1)}, u32[]{:S(2)}, u32[]{:S(2)}) collective-permute-start(bf16[160,768]{1,0:T(8,128)(2,1)S(1)} %fusion.3), channel_id=1, source_target_pairs={{0,7},{1,0},{2,1},{3,2},{4,3},{5,4},{6,5},{7,6},{8,15},{9,8},{10,9... | collective-permute-start | bytes 737288 | tf_op jit(solution)/shard_map/ppermute | solution.py:381
  97.1 1.1 %collective-permute-done.20 = bf16[160,768]{1,0:T(8,128)(2,1)S(1)} collective-permute-done((bf16[160,768]{1,0:T(8,128)(2,1)S(1)}, bf16[160,768]{1,0:T(8,128)(2,1)S(1)}, u32[]{:S(2)}, u32[]{:S(2)}) %collective-permute-start.20) | collective-permute-done | bytes 245792 | tf_op jit(solution)/shard_map/ppermute | solution.py:381
  98.2 1.5 %collective-permute-done.23 = bf16[160,768]{1,0:T(8,128)(2,1)S(1)} collective-permute-done((bf16[160,768]{1,0:T(8,128)(2,1)S(1)}, bf16[160,768]{1,0:T(8,128)(2,1)S(1)}, u32[]{:S(2)}, u32[]{:S(2)}) %collective-permute-start.23) | collective-permute-done | bytes 245792 | tf_op jit(solution)/shard_map/ppermute | solution.py:381
  99.8 3.7 %collective-permute-done.19 = bf16[160,768]{1,0:T(8,128)(2,1)S(1)} collective-permute-done((bf16[160,768]{1,0:T(8,128)(2,1)S(1)}, bf16[160,768]{1,0:T(8,128)(2,1)S(1)}, u32[]{:S(2)}, u32[]{:S(2)}) %collective-permute-start.19) | collective-permute-done | bytes 245792 | tf_op jit(solution)/shard_map/ppermute | solution.py:381
  (57 shorter events, 8.3 us)
Async XLA Ops:
  0.0 11.3 %copy-start = (bf16[80,1280]{1,0:T(8,128)(2,1)S(1)}, bf16[80,1280]{1,0:T(8,128)(2,1)}, u32[]{:S(2)}) copy-start(bf16[80,1280]{1,0:T(8,128)(2,1)} %own.1) | copy-start | bytes 614404
  0.0 8.0 %collective-permute-start.1 = (bf16[80,1280]{1,0:T(8,128)(2,1)}, bf16[80,1280]{1,0:T(8,128)(2,1)S(1)}, u32[]{:S(2)}, u32[]{:S(2)}) collective-permute-start(bf16[80,1280]{1,0:T(8,128)(2,1)} %own.1), channel_id=1, source_target_pairs={{16,0},{24,8},{0,16},{8,24},{48,32},{56,40},{32,48},{40,56},{80,64... | collective-permute-start | bytes 614408 | tf_op jit(solution)/shard_map/ppermute | solution.py:406
  3.0 6.7 %collective-permute-start = (bf16[80,1280]{1,0:T(8,128)(2,1)}, bf16[80,1280]{1,0:T(8,128)(2,1)S(1)}, u32[]{:S(2)}, u32[]{:S(2)}) collective-permute-start(bf16[80,1280]{1,0:T(8,128)(2,1)} %own.1), channel_id=1, source_target_pairs={{8,0},{16,8},{24,16},{0,24},{40,32},{48,40},{56,48},{32,56},{72,64... | collective-permute-start | bytes 614408 | tf_op jit(solution)/shard_map/ppermute | solution.py:406
  4.2 7.2 %collective-permute-start.2 = (bf16[80,1280]{1,0:T(8,128)(2,1)}, bf16[80,1280]{1,0:T(8,128)(2,1)S(1)}, u32[]{:S(2)}, u32[]{:S(2)}) collective-permute-start(bf16[80,1280]{1,0:T(8,128)(2,1)} %own.1), channel_id=1, source_target_pairs={{24,0},{0,8},{8,16},{16,24},{56,32},{32,40},{40,48},{48,56},{88,64... | collective-permute-start | bytes 614408 | tf_op jit(solution)/shard_map/ppermute | solution.py:406
  8.0 11.9 %copy-start.1 = (f32[10]{0:T(128)S(1)}, f32[10]{0:T(128)}, u32[]{:S(2)}) copy-start(f32[10]{0:T(128)} %param.14) | copy-start | bytes 124
  12.3 18.1 %collective-permute-start.4 = (bf16[4,80,1280]{2,1,0:T(8,128)(2,1)}, bf16[4,80,1280]{2,1,0:T(8,128)(2,1)S(1)}, u32[]{:S(2)}, u32[]{:S(2)}) collective-permute-start(bf16[4,80,1280]{2,1,0:T(8,128)(2,1)} %shard_map.86.refs_0_), channel_id=1, source_target_pairs={{96,0},{104,8},{112,16},{120,24},{0,32},{8,40},{16,48},{24,56},{32... | collective-permute-start | bytes 2457608 | tf_op jit(solution)/shard_map/ppermute | solution.py:406
  12.6 17.9 %collective-permute-start.3 = (bf16[4,80,1280]{2,1,0:T(8,128)(2,1)}, bf16[4,80,1280]{2,1,0:T(8,128)(2,1)S(1)}, u32[]{:S(2)}, u32[]{:S(2)}) collective-permute-start(bf16[4,80,1280]{2,1,0:T(8,128)(2,1)} %shard_map.86.refs_0_), channel_id=1, source_target_pairs={{32,0},{40,8},{48,16},{56,24},{64,32},{72,40},{80,48},{88,56},{96,... | collective-permute-start | bytes 2457608 | tf_op jit(solution)/shard_map/ppermute | solution.py:406
  14.3 16.1 %all-to-all-start = ((bf16[32,8,768]{2,1,0:T(8,128)(2,1)}), bf16[32,8,768]{2,1,0:T(8,128)(2,1)S(1)}, u32[]{:S(2)}, u32[]{:S(2)}) async-start(bf16[32,8,768]{2,1,0:T(8,128)(2,1)} %bitcast.1), calls=%async_computation | async-start | bytes 786432 | tf_op jit(solution)/shard_map/all_to_all | solution.py:463
  30.4 1.2 %copy-start.5 = (bf16[4,80,1280]{2,1,0:T(8,128)(2,1)}, bf16[4,80,1280]{2,1,0:T(8,128)(2,1)S(1)}, u32[]{:S(2)}) copy-start(bf16[4,80,1280]{2,1,0:T(8,128)(2,1)S(1)} %collective-permute-done.3.refs_1_) | copy-start | bytes 2457604
  31.7 18.0 %collective-permute-start.5 = (bf16[4,80,1280]{2,1,0:T(8,128)(2,1)}, bf16[4,80,1280]{2,1,0:T(8,128)(2,1)}, u32[]{:S(2)}, u32[]{:S(2)}) collective-permute-start(bf16[4,80,1280]{2,1,0:T(8,128)(2,1)} %get-tuple-element.32.refs_0_), channel_id=1, source_target_pairs={{64,0},{72,8},{80,16},{88,24},{96,32},{104,40},{112,48},{120,56},{... | collective-permute-start | bytes 2457608 | tf_op jit(solution)/shard_map/ppermute | solution.py:406
  33.4 6.9 %copy-start.2 = (bf16[4,80,1280]{2,1,0:T(8,128)(2,1)S(1)}, bf16[4,80,1280]{2,1,0:T(8,128)(2,1)}, u32[]{:S(2)}) copy-start(bf16[4,80,1280]{2,1,0:T(8,128)(2,1)} %get-tuple-element.32.refs_0_) | copy-start | bytes 2457604
  33.4 7.1 %copy-start.6 = (bf16[4,80,1280]{2,1,0:T(8,128)(2,1)S(1)}, bf16[4,80,1280]{2,1,0:T(8,128)(2,1)}, u32[]{:S(2)}) copy-start(bf16[4,80,1280]{2,1,0:T(8,128)(2,1)} %get-tuple-element.33.refs_1_) | copy-start | bytes 2457604
  33.4 7.5 %copy-start.4 = (bf16[4,80,1280]{2,1,0:T(8,128)(2,1)S(1)}, bf16[4,80,1280]{2,1,0:T(8,128)(2,1)}, u32[]{:S(2)}) copy-start(bf16[4,80,1280]{2,1,0:T(8,128)(2,1)} %get-tuple-element.34.refs_3_) | copy-start | bytes 2457604
  34.6 15.0 %all-to-all-start.1 = ((bf16[32,8,640]{2,1,0:T(8,128)(2,1)}), bf16[32,8,640]{2,1,0:T(8,128)(2,1)S(1)}, u32[]{:S(2)}, u32[]{:S(2)}) async-start(bf16[32,8,640]{2,1,0:T(8,128)(2,1)} %shard_map.84), calls=%async_computation.1 | async-start | bytes 655360 | tf_op jit(solution)/shard_map/all_to_all | solution.py:470
  40.3 12.9 %collective-permute-start.6 = (bf16[4,80,1280]{2,1,0:T(8,128)(2,1)S(1)}, bf16[4,80,1280]{2,1,0:T(8,128)(2,1)}, u32[]{:S(2)}, u32[]{:S(2)}) collective-permute-start(bf16[4,80,1280]{2,1,0:T(8,128)(2,1)S(1)} %copy-done.2), channel_id=1, source_target_pairs={{0,128},{128,0},{1,129},{129,1},{2,130},{130,2},{3,131},{131,3},{4... | collective-permute-start | bytes 2457608 | tf_op jit(solution)/shard_map/ppermute | solution.py:381
  40.6 12.6 %collective-permute-start.7 = (bf16[4,80,1280]{2,1,0:T(8,128)(2,1)S(1)}, bf16[4,80,1280]{2,1,0:T(8,128)(2,1)}, u32[]{:S(2)}, u32[]{:S(2)}) collective-permute-start(bf16[4,80,1280]{2,1,0:T(8,128)(2,1)S(1)} %copy-done.6), channel_id=1, source_target_pairs={{0,128},{128,0},{1,129},{129,1},{2,130},{130,2},{3,131},{131,3},{4... | collective-permute-start | bytes 2457608 | tf_op jit(solution)/shard_map/ppermute | solution.py:381
  40.9 12.3 %collective-permute-start.9 = (bf16[4,80,1280]{2,1,0:T(8,128)(2,1)S(1)}, bf16[4,80,1280]{2,1,0:T(8,128)(2,1)}, u32[]{:S(2)}, u32[]{:S(2)}) collective-permute-start(bf16[4,80,1280]{2,1,0:T(8,128)(2,1)S(1)} %copy-done.4), channel_id=1, source_target_pairs={{0,128},{128,0},{1,129},{129,1},{2,130},{130,2},{3,131},{131,3},{4... | collective-permute-start | bytes 2457608 | tf_op jit(solution)/shard_map/ppermute | solution.py:381
  49.6 3.6 %collective-permute-start.8 = (bf16[4,80,1280]{2,1,0:T(8,128)(2,1)}, bf16[4,80,1280]{2,1,0:T(8,128)(2,1)S(1)}, u32[]{:S(2)}, u32[]{:S(2)}) collective-permute-start(bf16[4,80,1280]{2,1,0:T(8,128)(2,1)} %shard_map.88.refs_2_), channel_id=1, source_target_pairs={{0,128},{128,0},{1,129},{129,1},{2,130},{130,2},{3,131},{131,3},{4... | collective-permute-start | bytes 2457608 | tf_op jit(solution)/shard_map/ppermute | solution.py:381
  55.5 12.7 %collective-permute-start.11 = (bf16[160,768]{1,0:T(8,128)(2,1)S(1)}, bf16[160,768]{1,0:T(8,128)(2,1)S(1)}, u32[]{:S(2)}, u32[]{:S(2)}) collective-permute-start(bf16[160,768]{1,0:T(8,128)(2,1)S(1)} %get-tuple-element.38), channel_id=1, source_target_pairs={{0,1},{1,2},{2,3},{3,4},{4,5},{5,6},{6,7},{7,0},{8,9},{9,10},{10,1... | collective-permute-start | bytes 737288 | tf_op jit(solution)/shard_map/ppermute | solution.py:381
  57.5 10.8 %collective-permute-start.10 = (bf16[160,768]{1,0:T(8,128)(2,1)S(1)}, bf16[160,768]{1,0:T(8,128)(2,1)S(1)}, u32[]{:S(2)}, u32[]{:S(2)}) collective-permute-start(bf16[160,768]{1,0:T(8,128)(2,1)S(1)} %get-tuple-element.37), channel_id=1, source_target_pairs={{0,7},{1,0},{2,1},{3,2},{4,3},{5,4},{6,5},{7,6},{8,15},{9,8},{10,9... | collective-permute-start | bytes 737288 | tf_op jit(solution)/shard_map/ppermute | solution.py:381
  64.2 11.3 %collective-permute-start.13 = (bf16[160,768]{1,0:T(8,128)(2,1)S(1)}, bf16[160,768]{1,0:T(8,128)(2,1)S(1)}, u32[]{:S(2)}, u32[]{:S(2)}) collective-permute-start(bf16[160,768]{1,0:T(8,128)(2,1)S(1)} %get-tuple-element.45), channel_id=1, source_target_pairs={{0,7},{1,0},{2,1},{3,2},{4,3},{5,4},{6,5},{7,6},{8,15},{9,8},{10,9... | collective-permute-start | bytes 737288 | tf_op jit(solution)/shard_map/ppermute | solution.py:381
  66.0 9.3 %collective-permute-start.14 = (bf16[160,768]{1,0:T(8,128)(2,1)S(1)}, bf16[160,768]{1,0:T(8,128)(2,1)S(1)}, u32[]{:S(2)}, u32[]{:S(2)}) collective-permute-start(bf16[160,768]{1,0:T(8,128)(2,1)S(1)} %get-tuple-element.46), channel_id=1, source_target_pairs={{0,1},{1,2},{2,3},{3,4},{4,5},{5,6},{6,7},{7,0},{8,9},{9,10},{10,1... | collective-permute-start | bytes 737288 | tf_op jit(solution)/shard_map/ppermute | solution.py:381
  68.3 14.2 %collective-permute-start.18 = (bf16[160,768]{1,0:T(8,128)(2,1)S(1)}, bf16[160,768]{1,0:T(8,128)(2,1)S(1)}, u32[]{:S(2)}, u32[]{:S(2)}) collective-permute-start(bf16[160,768]{1,0:T(8,128)(2,1)S(1)} %fusion.12), channel_id=1, source_target_pairs={{0,7},{1,0},{2,1},{3,2},{4,3},{5,4},{6,5},{7,6},{8,15},{9,8},{10,9... | collective-permute-start | bytes 737288 | tf_op jit(solution)/shard_map/ppermute | solution.py:381
  72.3 10.1 %collective-permute-start.12 = (bf16[160,768]{1,0:T(8,128)(2,1)S(1)}, bf16[160,768]{1,0:T(8,128)(2,1)S(1)}, u32[]{:S(2)}, u32[]{:S(2)}) collective-permute-start(bf16[160,768]{1,0:T(8,128)(2,1)S(1)} %fusion.11), channel_id=1, source_target_pairs={{0,1},{1,2},{2,3},{3,4},{4,5},{5,6},{6,7},{7,0},{8,9},{9,10},{10,1... | collective-permute-start | bytes 737288 | tf_op jit(solution)/shard_map/ppermute | solution.py:381
  75.4 12.3 %collective-permute-start.17 = (bf16[160,768]{1,0:T(8,128)(2,1)S(1)}, bf16[160,768]{1,0:T(8,128)(2,1)S(1)}, u32[]{:S(2)}, u32[]{:S(2)}) collective-permute-start(bf16[160,768]{1,0:T(8,128)(2,1)S(1)} %fusion.7), channel_id=1, source_target_pairs={{0,1},{1,2},{2,3},{3,4},{4,5},{5,6},{6,7},{7,0},{8,9},{9,10},{10,1... | collective-permute-start | bytes 737288 | tf_op jit(solution)/shard_map/ppermute | solution.py:381
  75.6 12.3 %collective-permute-start.16 = (bf16[160,768]{1,0:T(8,128)(2,1)S(1)}, bf16[160,768]{1,0:T(8,128)(2,1)S(1)}, u32[]{:S(2)}, u32[]{:S(2)}) collective-permute-start(bf16[160,768]{1,0:T(8,128)(2,1)S(1)} %fusion.8), channel_id=1, source_target_pairs={{0,7},{1,0},{2,1},{3,2},{4,3},{5,4},{6,5},{7,6},{8,15},{9,8},{10,9... | collective-permute-start | bytes 737288 | tf_op jit(solution)/shard_map/ppermute | solution.py:381
  82.5 10.5 %collective-permute-start.15 = (bf16[160,768]{1,0:T(8,128)(2,1)S(1)}, bf16[160,768]{1,0:T(8,128)(2,1)S(1)}, u32[]{:S(2)}, u32[]{:S(2)}) collective-permute-start(bf16[160,768]{1,0:T(8,128)(2,1)S(1)} %fusion.9), channel_id=1, source_target_pairs={{0,1},{1,2},{2,3},{3,4},{4,5},{5,6},{6,7},{7,0},{8,9},{9,10},{10,1... | collective-permute-start | bytes 737288 | tf_op jit(solution)/shard_map/ppermute | solution.py:381
  82.7 10.4 %collective-permute-start.22 = (bf16[160,768]{1,0:T(8,128)(2,1)S(1)}, bf16[160,768]{1,0:T(8,128)(2,1)S(1)}, u32[]{:S(2)}, u32[]{:S(2)}) collective-permute-start(bf16[160,768]{1,0:T(8,128)(2,1)S(1)} %fusion.4), channel_id=1, source_target_pairs={{0,7},{1,0},{2,1},{3,2},{4,3},{5,4},{6,5},{7,6},{8,15},{9,8},{10,9... | collective-permute-start | bytes 737288 | tf_op jit(solution)/shard_map/ppermute | solution.py:381
  87.8 10.5 %collective-permute-start.20 = (bf16[160,768]{1,0:T(8,128)(2,1)S(1)}, bf16[160,768]{1,0:T(8,128)(2,1)S(1)}, u32[]{:S(2)}, u32[]{:S(2)}) collective-permute-start(bf16[160,768]{1,0:T(8,128)(2,1)S(1)} %fusion.5), channel_id=1, source_target_pairs={{0,1},{1,2},{2,3},{3,4},{4,5},{5,6},{6,7},{7,0},{8,9},{9,10},{10,1... | collective-permute-start | bytes 737288 | tf_op jit(solution)/shard_map/ppermute | solution.py:381
  87.9 9.2 %collective-permute-start.21 = (bf16[160,768]{1,0:T(8,128)(2,1)S(1)}, bf16[160,768]{1,0:T(8,128)(2,1)S(1)}, u32[]{:S(2)}, u32[]{:S(2)}) collective-permute-start(bf16[160,768]{1,0:T(8,128)(2,1)S(1)} %fusion.6), channel_id=1, source_target_pairs={{0,7},{1,0},{2,1},{3,2},{4,3},{5,4},{6,5},{7,6},{8,15},{9,8},{10,9... | collective-permute-start | bytes 737288 | tf_op jit(solution)/shard_map/ppermute | solution.py:381
  93.1 6.7 %collective-permute-start.23 = (bf16[160,768]{1,0:T(8,128)(2,1)S(1)}, bf16[160,768]{1,0:T(8,128)(2,1)S(1)}, u32[]{:S(2)}, u32[]{:S(2)}) collective-permute-start(bf16[160,768]{1,0:T(8,128)(2,1)S(1)} %fusion.3), channel_id=1, source_target_pairs={{0,7},{1,0},{2,1},{3,2},{4,3},{5,4},{6,5},{7,6},{8,15},{9,8},{10,9... | collective-permute-start | bytes 737288 | tf_op jit(solution)/shard_map/ppermute | solution.py:381
  96.1 7.4 %collective-permute-start.19 = (bf16[160,768]{1,0:T(8,128)(2,1)S(1)}, bf16[160,768]{1,0:T(8,128)(2,1)S(1)}, u32[]{:S(2)}, u32[]{:S(2)}) collective-permute-start(bf16[160,768]{1,0:T(8,128)(2,1)S(1)} %fusion.10), channel_id=1, source_target_pairs={{0,1},{1,2},{2,3},{3,4},{4,5},{5,6},{6,7},{7,0},{8,9},{9,10},{10,1... | collective-permute-start | bytes 737288 | tf_op jit(solution)/shard_map/ppermute | solution.py:381
  (1 other events, 0.9 us)

commit v5 on v4

--- a/solution.py
+++ b/solution.py
@@ -146,7 +146,10 @@
 
 
 def inner_body(x_ref, g_ref, b_ref, c_ref, step_ref, log_ref, skip_ref, mark_ref, pre_ref, gain_ref, state_ref, past_ref):
-    @pl.when(pl.program_id(0) == 0)
+    k = pl.program_id(0)
+    tokens = pl.ds(pl.multiple_of(k * BLK, BLK), BLK)
+
+    @pl.when(k == 0)
     def _():
         state_ref[...] = jnp.zeros_like(state_ref)
         past_ref[...] = jnp.zeros_like(past_ref)
@@ -188,7 +191,7 @@
         gate = g_ref[:, here].astype(F32)
         silu = 0.5 * gate * (1.0 + jnp.tanh(0.5 * gate))
         pre_ref[:, here] = (out * silu).astype(BF16)
-        gain_ref[:, here] = (silu * columns[:, 32 + h : 33 + h]).astype(BF16)
+        gain_ref[tokens, here] = (silu * columns[:, 32 + h : 33 + h]).astype(BF16)
         scaled = (turned * tail[h : h + 1, :]).astype(BF16)
         state_ref[:, here] = grow[h : h + 1, :] * state + jnp.dot(scaled, x_here, preferred_element_type=F32)
     past_ref[:HEADS, :] = past_ref[:HEADS, :] + total
@@ -208,8 +211,8 @@
             IN_SMEM,
             ANYWHERE,
         ],
-        out_specs=[pl.BlockSpec((BLK, CH), lambda i: (i, 0))] * 2,
-        out_shape=[pltpu.HBM((TOK, CH), BF16)] * 2,
+        out_specs=[pl.BlockSpec((BLK, CH), lambda i: (i, 0)), IN_VMEM],
+        out_shape=[pltpu.HBM((TOK, CH), BF16), pltpu.VMEM((TOK, CH), BF16)],
         scratch_shapes=[pltpu.VMEM((N, CH), F32), pltpu.VMEM((16, BLK), F32)],
         compiler_params=SMALL,
         cost_estimate=pl.CostEstimate(flops=1 << 20, bytes_accessed=40 << 20, transcendentals=0),
@@ -278,7 +281,7 @@
     for half in range(2):
         cols = slice(half * HALF, (half + 1) * HALF)
         carried = jnp.dot(c_ref[...], state_ref[half], preferred_element_type=F32)
-        hidden_ref[here, cols] = (pre_ref[:, cols].astype(F32) + gain_ref[:, cols].astype(F32) * carried).astype(BF16)
+        hidden_ref[here, cols] = (pre_ref[:, cols].astype(F32) + gain_ref[here, cols].astype(F32) * carried).astype(BF16)
 
 
 def hidden_of(entering, c, pre, gain):
@@ -290,14 +293,14 @@
             pl.BlockSpec((16, 2, 8, HALF), lambda i: (0, 0, 0, 0)),
             pl.BlockSpec((rows, N), lambda i: (i, 0)),
             pl.BlockSpec((rows, CH), lambda i: (i, 0)),
-            pl.BlockSpec((rows, CH), lambda i: (i, 0)),
+            IN_VMEM,
         ],
         out_specs=IN_VMEM,
         out_shape=pltpu.VMEM((TOK, CH), BF16),
         scratch_shapes=[pltpu.VMEM((2, N, HALF), BF16)],
         compiler_params=SMALL,
         cost_estimate=pl.CostEstimate(flops=2 * TOK * N * CH, bytes_accessed=5 << 20, transcendentals=0),
-    )(entering, *[in_hbm(v) for v in (c, pre, gain)])
+    )(entering, *[in_hbm(v) for v in (c, pre)], in_vmem(gain))
 
 
 def in_place(blocks):

time: 105 us -> 104 us (level)
  no operation moved by 1% of the time
where the time goes in v5:
time: 104 us
  starting transfers between devices  46.3 us (45%)
  waiting for transfers between devices  28.4 us (27%)
  Pallas kernels  26.2 us (25%)
  other arithmetic  1.59 us (2%)
    ppermute x18, starting transfers between devices, shift(): lax.ppermute(value, axis, [(i, (i + by) % size) for i in range(size)])  26.2 us
    ppermute x18, waiting for transfers between devices, shift(): lax.ppermute(value, axis, [(i, (i + by) % size) for i in range(size)])  15.4 us
    pallas_call x1, Pallas kernels, inner(): pl.pallas_call(inner_body, grid=(NBLK,), in_specs=[pl.BlockSpec((BLK, CH)...  9.3 us
    ppermute x6, starting transfers between devices, from_line(): return lax.ppermute(value, ('seq', 'row'), pairs)  8.85 us
    all_to_all x1, waiting for transfers between devices, shards(): entering = lax.all_to_all(slices, ('seq', 'row'), 0, 0)  8.59 us
    all_to_all x1, starting transfers between devices, shards(): lax.all_to_all(payload.reshape(SHARDS, 8, HALF + P_SIZE), ('seq', 'row'),...  5.63 us
    all_to_all x1, starting transfers between devices, shards(): entering = lax.all_to_all(slices, ('seq', 'row'), 0, 0)  5.62 us
    pallas_call x2, Pallas kernels, rest_parts(): pl.pallas_call(functools.partial(rest_body, ups), in_specs=[IN_VMEM, IN_V...  4.02 us
  transfers between devices with their start and end apart: 26, of which 12 were waited for; matrix products, arithmetic and copies ran while one was open for 1% of the time, Pallas kernels for 22%

profile of v5, /device:TPU:24, one launch (start us, length us, event | category | flops | bytes accessed | tf_op | source)
XLA Modules:
  0.0 103.8 jit_solution(8558823268042071375)
XLA Ops:
  0.0 3.0 %collective-permute-start.1 = (bf16[80,1280]{1,0:T(8,128)(2,1)}, bf16[80,1280]{1,0:T(8,128)(2,1)S(1)}, u32[]{:S(2)}, u32[]{:S(2)}) collective-permute-start(bf16[80,1280]{1,0:T(8,128)(2,1)} %own.1), channel_id=1, source_target_pairs={{16,0},{24,8},{0,16},{8,24},{48,32},{56,40},{32,48},{40,56},{80,64... | collective-permute-start | bytes 614408 | tf_op jit(solution)/shard_map/ppermute | solution.py:409
  3.0 1.1 %collective-permute-start = (bf16[80,1280]{1,0:T(8,128)(2,1)}, bf16[80,1280]{1,0:T(8,128)(2,1)S(1)}, u32[]{:S(2)}, u32[]{:S(2)}) collective-permute-start(bf16[80,1280]{1,0:T(8,128)(2,1)} %own.1), channel_id=1, source_target_pairs={{8,0},{16,8},{24,16},{0,24},{40,32},{48,40},{56,48},{32,56},{72,64... | collective-permute-start | bytes 614408 | tf_op jit(solution)/shard_map/ppermute | solution.py:409
  5.1 3.0 %shard_map.82.mark_ref.mark = bf16[16,2,8,768]{3,2,1,0:T(8,128)(2,1)} custom-call(bf16[768,1280]{1,0:T(8,128)(2,1)} %x_ref.3, bf16[768,128]{1,0:T(8,128)(2,1)} %b_ref.3, f32[10,768]{1,0:T(8,128)} %step_ref.3, f32[10,768]{1,0:T(8,128)} %log_ref.3), custom_call_target="tpu_custom_call" | custom-call | flops 251658240 | bytes 3145728 | tf_op jit(solution)/shard_map/pallas_call | solution.py:103
  8.0 1.7 %collective-permute-done.one = bf16[80,1280]{1,0:T(8,128)(2,1)S(1)} collective-permute-done((bf16[80,1280]{1,0:T(8,128)(2,1)}, bf16[80,1280]{1,0:T(8,128)(2,1)S(1)}, u32[]{:S(2)}, u32[]{:S(2)}) %collective-permute-start) | collective-permute-done | bytes 204832 | tf_op jit(solution)/shard_map/ppermute | solution.py:409
  9.8 1.6 %collective-permute-done.2.three = bf16[80,1280]{1,0:T(8,128)(2,1)S(1)} collective-permute-done((bf16[80,1280]{1,0:T(8,128)(2,1)}, bf16[80,1280]{1,0:T(8,128)(2,1)S(1)}, u32[]{:S(2)}, u32[]{:S(2)}) %collective-permute-start.2) | collective-permute-done | bytes 204832 | tf_op jit(solution)/shard_map/ppermute | solution.py:409
  12.6 1.7 %collective-permute-start.3 = (bf16[4,80,1280]{2,1,0:T(8,128)(2,1)}, bf16[4,80,1280]{2,1,0:T(8,128)(2,1)}, u32[]{:S(2)}, u32[]{:S(2)}) collective-permute-start(bf16[4,80,1280]{2,1,0:T(8,128)(2,1)} %shard_map.86.refs_0_), channel_id=1, source_target_pairs={{32,0},{40,8},{48,16},{56,24},{64,32},{72,40},{80,48},{88,56},{96,... | collective-permute-start | bytes 2457608 | tf_op jit(solution)/shard_map/ppermute | solution.py:409
  14.4 5.6 %all-to-all-start = ((bf16[32,8,768]{2,1,0:T(8,128)(2,1)}), bf16[32,8,768]{2,1,0:T(8,128)(2,1)S(1)}, u32[]{:S(2)}, u32[]{:S(2)}) async-start(bf16[32,8,768]{2,1,0:T(8,128)(2,1)} %bitcast.1), calls=%async_computation | async-start | bytes 786432 | tf_op jit(solution)/shard_map/all_to_all | solution.py:466
  20.0 9.3 %shard_map.83 = (bf16[768,1280]{1,0:T(8,128)(2,1)}, bf16[768,1280]{1,0:T(8,128)(2,1)S(1)}) custom-call(bf16[768,1280]{1,0:T(8,128)(2,1)} %x_ref.3, bf16[768,1280]{1,0:T(8,128)(2,1)} %g_ref.1, bf16[768,128]{1,0:T(8,128)(2,1)} %b_ref.3, bf16[768,128]{1,0:T(8,128)(2,1)} %c_ref.3, f32[10,768]{1,0:T(8,128)} %step_ref.3, f32[10,768]{1,0:T(8,128)} %log_ref.3, ...), custom_call_target="tpu_custom_call" | custom-call | flops 1048576 | bytes 41943040 | tf_op jit(solution)/shard_map/pallas_call | solution.py:201
  29.3 1.1 %all-to-all-done.in_ref.refs_3_ = bf16[32,8,768]{2,1,0:T(8,128)(2,1)S(1)} async-done(((bf16[32,8,768]{2,1,0:T(8,128)(2,1)}), bf16[32,8,768]{2,1,0:T(8,128)(2,1)S(1)}, u32[]{:S(2)}, u32[]{:S(2)}) %all-to-all-start) | async-done | bytes 393248 | tf_op jit(solution)/shard_map/all_to_all | solution.py:466
  31.4 1.8 %collective-permute-start.5 = (bf16[4,80,1280]{2,1,0:T(8,128)(2,1)}, bf16[4,80,1280]{2,1,0:T(8,128)(2,1)}, u32[]{:S(2)}, u32[]{:S(2)}) collective-permute-start(bf16[4,80,1280]{2,1,0:T(8,128)(2,1)} %get-tuple-element.32.refs_0_), channel_id=1, source_target_pairs={{64,0},{72,8},{80,16},{88,24},{96,32},{104,40},{112,48},{120,56},{... | collective-permute-start | bytes 2457608 | tf_op jit(solution)/shard_map/ppermute | solution.py:409
  33.1 1.2 %shard_map.84 = bf16[32,8,640]{2,1,0:T(8,128)(2,1)} custom-call(s32[1]{0:T(128)} %bitcast.half_ref, bf16[32,8,768]{2,1,0:T(8,128)(2,1)S(1)} %all-to-all-done.in_ref.refs_3_, bf16[768,1280]{1,0:T(8,128)(2,1)} %get-tuple-element.30.mark_ref.pre_ref.refs_4_), custom_call_target="tpu_custom_call" | custom-call | tf_op jit(solution)/shard_map/pallas_call | solution.py:134
  34.3 5.6 %all-to-all-start.1 = ((bf16[32,8,640]{2,1,0:T(8,128)(2,1)}), bf16[32,8,640]{2,1,0:T(8,128)(2,1)S(1)}, u32[]{:S(2)}, u32[]{:S(2)}) async-start(bf16[32,8,640]{2,1,0:T(8,128)(2,1)} %shard_map.84), calls=%async_computation.1 | async-start | bytes 655360 | tf_op jit(solution)/shard_map/all_to_all | solution.py:473
  40.7 8.6 %all-to-all-done.1.refs_1_ = bf16[32,8,640]{2,1,0:T(8,128)(2,1)S(1)} async-done(((bf16[32,8,640]{2,1,0:T(8,128)(2,1)}), bf16[32,8,640]{2,1,0:T(8,128)(2,1)S(1)}, u32[]{:S(2)}, u32[]{:S(2)}) %all-to-all-start.1) | async-done | bytes 327712 | tf_op jit(solution)/shard_map/all_to_all | solution.py:473
  49.5 3.0 %shard_map.85.hidden_ref = bf16[768,1280]{1,0:T(8,128)(2,1)S(1)} custom-call(bf16[16,2,8,640]{3,2,1,0:T(8,128)(2,1)S(1)} %bitcast.47, bf16[768,128]{1,0:T(8,128)(2,1)} %c_ref.3, bf16[768,1280]{1,0:T(8,128)(2,1)} %get-tuple-element.30.mark_ref.pre_ref.refs_4_, bf16[768,1280]{1,0:T(8,128)(2,1)S(1)} %get-tuple-element.31.gain_ref), custom_call_target="tpu_custom_call" | custom-call | flops 251658240 | bytes 5242880 | tf_op jit(solution)/shard_map/pallas_call | solution.py:289
  52.5 2.3 %shard_map.89 = (bf16[160,768]{1,0:T(8,128)(2,1)S(1)}, bf16[160,768]{1,0:T(8,128)(2,1)S(1)}, bf16[2,4,80,1280]{3,2,1,0:T(8,128)(2,1)S(1)}) custom-call(bf16[768,1280]{1,0:T(8,128)(2,1)S(1)} %shard_map.85.hidden_ref, bf16[4,80,1280]{2,1,0:T(8,128)(2,1)} %get-tuple-element.32.refs_0_, bf16[4,80,1280]{2,1,0:T(8,128)(2,1)} %get-tuple-element.33.refs_1_, ...), custom_call_target="tpu_custom_call" | custom-call | flops 629145600 | bytes 2097152 | tf_op jit(solution)/shard_map/pallas_call | solution.py:322
  54.8 2.0 %collective-permute-start.11 = (bf16[160,768]{1,0:T(8,128)(2,1)S(1)}, bf16[160,768]{1,0:T(8,128)(2,1)S(1)}, u32[]{:S(2)}, u32[]{:S(2)}) collective-permute-start(bf16[160,768]{1,0:T(8,128)(2,1)S(1)} %get-tuple-element.38), channel_id=1, source_target_pairs={{0,1},{1,2},{2,3},{3,4},{4,5},{5,6},{6,7},{7,0},{8,9},{9,10},{10,1... | collective-permute-start | bytes 737288 | tf_op jit(solution)/shard_map/ppermute | solution.py:384
  56.8 4.2 %collective-permute-start.10 = (bf16[160,768]{1,0:T(8,128)(2,1)S(1)}, bf16[160,768]{1,0:T(8,128)(2,1)S(1)}, u32[]{:S(2)}, u32[]{:S(2)}) collective-permute-start(bf16[160,768]{1,0:T(8,128)(2,1)S(1)} %get-tuple-element.37), channel_id=1, source_target_pairs={{0,7},{1,0},{2,1},{3,2},{4,3},{5,4},{6,5},{7,6},{8,15},{9,8},{10,9... | collective-permute-start | bytes 737288 | tf_op jit(solution)/shard_map/ppermute | solution.py:384
  61.0 2.5 %shard_map.90 = (bf16[160,768]{1,0:T(8,128)(2,1)S(1)}, bf16[160,768]{1,0:T(8,128)(2,1)S(1)}, bf16[2,160,768]{2,1,0:T(8,128)(2,1)S(1)}, bf16[2,4,80,1280]{3,2,1,0:T(8,128)(2,1)S(1)}) custom-call(bf16[768,1280]{1,0:T(8,128)(2,1)S(1)} %shard_map.85.hidden_ref, bf16[2,4,80,1280]{3,2,1,0:T(8,128)(2,1)S(1)} %get-tuple-element.35.held, ...), custom_call_target="tpu_custom_call" | custom-call | flops 1258291200 | bytes 2097152 | tf_op jit(solution)/shard_map/pallas_call | solution.py:346
  63.5 1.8 %collective-permute-start.13 = (bf16[160,768]{1,0:T(8,128)(2,1)S(1)}, bf16[160,768]{1,0:T(8,128)(2,1)S(1)}, u32[]{:S(2)}, u32[]{:S(2)}) collective-permute-start(bf16[160,768]{1,0:T(8,128)(2,1)S(1)} %get-tuple-element.45), channel_id=1, source_target_pairs={{0,7},{1,0},{2,1},{3,2},{4,3},{5,4},{6,5},{7,6},{8,15},{9,8},{10,9... | collective-permute-start | bytes 737288 | tf_op jit(solution)/shard_map/ppermute | solution.py:384
  65.6 1.9 %shard_map.91 = (bf16[2,2,160,768]{3,2,1,0:T(8,128)(2,1)S(1)}, bf16[3,4,80,1280]{3,2,1,0:T(8,128)(2,1)S(1)}) custom-call(bf16[768,1280]{1,0:T(8,128)(2,1)S(1)} %shard_map.85.hidden_ref, bf16[2,4,80,1280]{3,2,1,0:T(8,128)(2,1)S(1)} %get-tuple-element.39.held, bf16[4,80,1280]{2,1,0:T(8,128)(2,1)} %get-tuple-element.32.refs_0_, ...), custom_call_target="tpu_custom_call" | custom-call | flops 1258291200 | bytes 2097152 | tf_op jit(solution)/shard_map/pallas_call | solution.py:371
  67.7 4.0 %collective-permute-start.18 = (bf16[160,768]{1,0:T(8,128)(2,1)S(1)}, bf16[160,768]{1,0:T(8,128)(2,1)S(1)}, u32[]{:S(2)}, u32[]{:S(2)}) collective-permute-start(bf16[160,768]{1,0:T(8,128)(2,1)S(1)} %fusion.12), channel_id=1, source_target_pairs={{0,7},{1,0},{2,1},{3,2},{4,3},{5,4},{6,5},{7,6},{8,15},{9,8},{10,9... | collective-permute-start | bytes 737288 | tf_op jit(solution)/shard_map/ppermute | solution.py:384
  71.7 2.1 %shard_map.92 = bf16[3,2,160,768]{3,2,1,0:T(8,128)(2,1)S(1)} custom-call(bf16[768,1280]{1,0:T(8,128)(2,1)S(1)} %shard_map.85.hidden_ref, bf16[3,4,80,1280]{3,2,1,0:T(8,128)(2,1)S(1)} %get-tuple-element.44.held, bf16[4,80,1280]{2,1,0:T(8,128)(2,1)} %get-tuple-element.32.refs_0_, bf16[4,80,1280]{2,1,0:T(8,128)(2,1)} %get-tuple-element.33.refs_1_, ...), custom_call_target="tpu_custom_call" | custom-call | flops 1887436800 | bytes 3145728 | tf_op jit(solution)/shard_map/pallas_call | solution.py:371
  74.9 3.3 %collective-permute-start.16 = (bf16[160,768]{1,0:T(8,128)(2,1)S(1)}, bf16[160,768]{1,0:T(8,128)(2,1)S(1)}, u32[]{:S(2)}, u32[]{:S(2)}) collective-permute-start(bf16[160,768]{1,0:T(8,128)(2,1)S(1)} %fusion.8), channel_id=1, source_target_pairs={{0,7},{1,0},{2,1},{3,2},{4,3},{5,4},{6,5},{7,6},{8,15},{9,8},{10,9... | collective-permute-start | bytes 737288 | tf_op jit(solution)/shard_map/ppermute | solution.py:384
  78.2 3.6 %collective-permute-done.12 = bf16[160,768]{1,0:T(8,128)(2,1)S(1)} collective-permute-done((bf16[160,768]{1,0:T(8,128)(2,1)S(1)}, bf16[160,768]{1,0:T(8,128)(2,1)S(1)}, u32[]{:S(2)}, u32[]{:S(2)}) %collective-permute-start.12) | collective-permute-done | bytes 245792 | tf_op jit(solution)/shard_map/ppermute | solution.py:384
  82.0 3.3 %collective-permute-start.22 = (bf16[160,768]{1,0:T(8,128)(2,1)S(1)}, bf16[160,768]{1,0:T(8,128)(2,1)S(1)}, u32[]{:S(2)}, u32[]{:S(2)}) collective-permute-start(bf16[160,768]{1,0:T(8,128)(2,1)S(1)} %fusion.4), channel_id=1, source_target_pairs={{0,7},{1,0},{2,1},{3,2},{4,3},{5,4},{6,5},{7,6},{8,15},{9,8},{10,9... | collective-permute-start | bytes 737288 | tf_op jit(solution)/shard_map/ppermute | solution.py:384
  85.3 1.7 %collective-permute-done.17 = bf16[160,768]{1,0:T(8,128)(2,1)S(1)} collective-permute-done((bf16[160,768]{1,0:T(8,128)(2,1)S(1)}, bf16[160,768]{1,0:T(8,128)(2,1)S(1)}, u32[]{:S(2)}, u32[]{:S(2)}) %collective-permute-start.17) | collective-permute-done | bytes 245792 | tf_op jit(solution)/shard_map/ppermute | solution.py:384
  87.3 3.3 %collective-permute-start.21 = (bf16[160,768]{1,0:T(8,128)(2,1)S(1)}, bf16[160,768]{1,0:T(8,128)(2,1)S(1)}, u32[]{:S(2)}, u32[]{:S(2)}) collective-permute-start(bf16[160,768]{1,0:T(8,128)(2,1)S(1)} %fusion.6), channel_id=1, source_target_pairs={{0,7},{1,0},{2,1},{3,2},{4,3},{5,4},{6,5},{7,6},{8,15},{9,8},{10,9... | collective-permute-start | bytes 737288 | tf_op jit(solution)/shard_map/ppermute | solution.py:384
  90.6 1.7 %collective-permute-done.15 = bf16[160,768]{1,0:T(8,128)(2,1)S(1)} collective-permute-done((bf16[160,768]{1,0:T(8,128)(2,1)S(1)}, bf16[160,768]{1,0:T(8,128)(2,1)S(1)}, u32[]{:S(2)}, u32[]{:S(2)}) %collective-permute-start.15) | collective-permute-done | bytes 245792 | tf_op jit(solution)/shard_map/ppermute | solution.py:384
  92.4 2.9 %collective-permute-start.23 = (bf16[160,768]{1,0:T(8,128)(2,1)S(1)}, bf16[160,768]{1,0:T(8,128)(2,1)S(1)}, u32[]{:S(2)}, u32[]{:S(2)}) collective-permute-start(bf16[160,768]{1,0:T(8,128)(2,1)S(1)} %fusion.3), channel_id=1, source_target_pairs={{0,7},{1,0},{2,1},{3,2},{4,3},{5,4},{6,5},{7,6},{8,15},{9,8},{10,9... | collective-permute-start | bytes 737288 | tf_op jit(solution)/shard_map/ppermute | solution.py:384
  96.4 1.1 %collective-permute-done.20 = bf16[160,768]{1,0:T(8,128)(2,1)S(1)} collective-permute-done((bf16[160,768]{1,0:T(8,128)(2,1)S(1)}, bf16[160,768]{1,0:T(8,128)(2,1)S(1)}, u32[]{:S(2)}, u32[]{:S(2)}) %collective-permute-start.20) | collective-permute-done | bytes 245792 | tf_op jit(solution)/shard_map/ppermute | solution.py:384
  97.6 1.5 %collective-permute-done.23 = bf16[160,768]{1,0:T(8,128)(2,1)S(1)} collective-permute-done((bf16[160,768]{1,0:T(8,128)(2,1)S(1)}, bf16[160,768]{1,0:T(8,128)(2,1)S(1)}, u32[]{:S(2)}, u32[]{:S(2)}) %collective-permute-start.23) | collective-permute-done | bytes 245792 | tf_op jit(solution)/shard_map/ppermute | solution.py:384
  99.1 3.7 %collective-permute-done.19 = bf16[160,768]{1,0:T(8,128)(2,1)S(1)} collective-permute-done((bf16[160,768]{1,0:T(8,128)(2,1)S(1)}, bf16[160,768]{1,0:T(8,128)(2,1)S(1)}, u32[]{:S(2)}, u32[]{:S(2)}) %collective-permute-start.19) | collective-permute-done | bytes 245792 | tf_op jit(solution)/shard_map/ppermute | solution.py:384
  (51 shorter events, 8.0 us)
Async XLA Ops:
  0.0 11.3 %copy-start = (bf16[80,1280]{1,0:T(8,128)(2,1)S(1)}, bf16[80,1280]{1,0:T(8,128)(2,1)}, u32[]{:S(2)}) copy-start(bf16[80,1280]{1,0:T(8,128)(2,1)} %own.1) | copy-start | bytes 614404
  0.0 8.0 %collective-permute-start.1 = (bf16[80,1280]{1,0:T(8,128)(2,1)}, bf16[80,1280]{1,0:T(8,128)(2,1)S(1)}, u32[]{:S(2)}, u32[]{:S(2)}) collective-permute-start(bf16[80,1280]{1,0:T(8,128)(2,1)} %own.1), channel_id=1, source_target_pairs={{16,0},{24,8},{0,16},{8,24},{48,32},{56,40},{32,48},{40,56},{80,64... | collective-permute-start | bytes 614408 | tf_op jit(solution)/shard_map/ppermute | solution.py:409
  3.0 6.7 %collective-permute-start = (bf16[80,1280]{1,0:T(8,128)(2,1)}, bf16[80,1280]{1,0:T(8,128)(2,1)S(1)}, u32[]{:S(2)}, u32[]{:S(2)}) collective-permute-start(bf16[80,1280]{1,0:T(8,128)(2,1)} %own.1), channel_id=1, source_target_pairs={{8,0},{16,8},{24,16},{0,24},{40,32},{48,40},{56,48},{32,56},{72,64... | collective-permute-start | bytes 614408 | tf_op jit(solution)/shard_map/ppermute | solution.py:409
  4.2 7.2 %collective-permute-start.2 = (bf16[80,1280]{1,0:T(8,128)(2,1)}, bf16[80,1280]{1,0:T(8,128)(2,1)S(1)}, u32[]{:S(2)}, u32[]{:S(2)}) collective-permute-start(bf16[80,1280]{1,0:T(8,128)(2,1)} %own.1), channel_id=1, source_target_pairs={{24,0},{0,8},{8,16},{16,24},{56,32},{32,40},{40,48},{48,56},{88,64... | collective-permute-start | bytes 614408 | tf_op jit(solution)/shard_map/ppermute | solution.py:409
  8.0 12.0 %copy-start.1 = (f32[10]{0:T(128)S(1)}, f32[10]{0:T(128)}, u32[]{:S(2)}) copy-start(f32[10]{0:T(128)} %param.14) | copy-start | bytes 124
  12.3 18.1 %collective-permute-start.4 = (bf16[4,80,1280]{2,1,0:T(8,128)(2,1)}, bf16[4,80,1280]{2,1,0:T(8,128)(2,1)S(1)}, u32[]{:S(2)}, u32[]{:S(2)}) collective-permute-start(bf16[4,80,1280]{2,1,0:T(8,128)(2,1)} %shard_map.86.refs_0_), channel_id=1, source_target_pairs={{96,0},{104,8},{112,16},{120,24},{0,32},{8,40},{16,48},{24,56},{32... | collective-permute-start | bytes 2457608 | tf_op jit(solution)/shard_map/ppermute | solution.py:409
  12.6 17.9 %collective-permute-start.3 = (bf16[4,80,1280]{2,1,0:T(8,128)(2,1)}, bf16[4,80,1280]{2,1,0:T(8,128)(2,1)}, u32[]{:S(2)}, u32[]{:S(2)}) collective-permute-start(bf16[4,80,1280]{2,1,0:T(8,128)(2,1)} %shard_map.86.refs_0_), channel_id=1, source_target_pairs={{32,0},{40,8},{48,16},{56,24},{64,32},{72,40},{80,48},{88,56},{96,... | collective-permute-start | bytes 2457608 | tf_op jit(solution)/shard_map/ppermute | solution.py:409
  14.4 16.1 %all-to-all-start = ((bf16[32,8,768]{2,1,0:T(8,128)(2,1)}), bf16[32,8,768]{2,1,0:T(8,128)(2,1)S(1)}, u32[]{:S(2)}, u32[]{:S(2)}) async-start(bf16[32,8,768]{2,1,0:T(8,128)(2,1)} %bitcast.1), calls=%async_computation | async-start | bytes 786432 | tf_op jit(solution)/shard_map/all_to_all | solution.py:466
  30.5 0.9 copy-start.3
  31.4 18.0 %collective-permute-start.5 = (bf16[4,80,1280]{2,1,0:T(8,128)(2,1)}, bf16[4,80,1280]{2,1,0:T(8,128)(2,1)}, u32[]{:S(2)}, u32[]{:S(2)}) collective-permute-start(bf16[4,80,1280]{2,1,0:T(8,128)(2,1)} %get-tuple-element.32.refs_0_), channel_id=1, source_target_pairs={{64,0},{72,8},{80,16},{88,24},{96,32},{104,40},{112,48},{120,56},{... | collective-permute-start | bytes 2457608 | tf_op jit(solution)/shard_map/ppermute | solution.py:409
  33.1 6.8 %copy-start.2 = (bf16[4,80,1280]{2,1,0:T(8,128)(2,1)S(1)}, bf16[4,80,1280]{2,1,0:T(8,128)(2,1)}, u32[]{:S(2)}) copy-start(bf16[4,80,1280]{2,1,0:T(8,128)(2,1)} %get-tuple-element.32.refs_0_) | copy-start | bytes 2457604
  34.3 15.0 %all-to-all-start.1 = ((bf16[32,8,640]{2,1,0:T(8,128)(2,1)}), bf16[32,8,640]{2,1,0:T(8,128)(2,1)S(1)}, u32[]{:S(2)}, u32[]{:S(2)}) async-start(bf16[32,8,640]{2,1,0:T(8,128)(2,1)} %shard_map.84), calls=%async_computation.1 | async-start | bytes 655360 | tf_op jit(solution)/shard_map/all_to_all | solution.py:473
  40.0 12.6 %collective-permute-start.6 = (bf16[4,80,1280]{2,1,0:T(8,128)(2,1)S(1)}, bf16[4,80,1280]{2,1,0:T(8,128)(2,1)}, u32[]{:S(2)}, u32[]{:S(2)}) collective-permute-start(bf16[4,80,1280]{2,1,0:T(8,128)(2,1)S(1)} %copy-done.2), channel_id=1, source_target_pairs={{0,128},{128,0},{1,129},{129,1},{2,130},{130,2},{3,131},{131,3},{4... | collective-permute-start | bytes 2457608 | tf_op jit(solution)/shard_map/ppermute | solution.py:384
  40.2 12.3 %collective-permute-start.7 = (bf16[4,80,1280]{2,1,0:T(8,128)(2,1)}, bf16[4,80,1280]{2,1,0:T(8,128)(2,1)}, u32[]{:S(2)}, u32[]{:S(2)}) collective-permute-start(bf16[4,80,1280]{2,1,0:T(8,128)(2,1)} %get-tuple-element.33.refs_1_), channel_id=1, source_target_pairs={{0,128},{128,0},{1,129},{129,1},{2,130},{130,2},{3,131},{131,3},{4... | collective-permute-start | bytes 2457608 | tf_op jit(solution)/shard_map/ppermute | solution.py:384
  40.6 12.0 %collective-permute-start.9 = (bf16[4,80,1280]{2,1,0:T(8,128)(2,1)}, bf16[4,80,1280]{2,1,0:T(8,128)(2,1)}, u32[]{:S(2)}, u32[]{:S(2)}) collective-permute-start(bf16[4,80,1280]{2,1,0:T(8,128)(2,1)} %get-tuple-element.34.refs_3_), channel_id=1, source_target_pairs={{0,128},{128,0},{1,129},{129,1},{2,130},{130,2},{3,131},{131,3},{4... | collective-permute-start | bytes 2457608 | tf_op jit(solution)/shard_map/ppermute | solution.py:384
  49.3 3.2 %collective-permute-start.8 = (bf16[4,80,1280]{2,1,0:T(8,128)(2,1)}, bf16[4,80,1280]{2,1,0:T(8,128)(2,1)S(1)}, u32[]{:S(2)}, u32[]{:S(2)}) collective-permute-start(bf16[4,80,1280]{2,1,0:T(8,128)(2,1)} %shard_map.88.refs_2_), channel_id=1, source_target_pairs={{0,128},{128,0},{1,129},{129,1},{2,130},{130,2},{3,131},{131,3},{4... | collective-permute-start | bytes 2457608 | tf_op jit(solution)/shard_map/ppermute | solution.py:384
  54.8 12.7 %collective-permute-start.11 = (bf16[160,768]{1,0:T(8,128)(2,1)S(1)}, bf16[160,768]{1,0:T(8,128)(2,1)S(1)}, u32[]{:S(2)}, u32[]{:S(2)}) collective-permute-start(bf16[160,768]{1,0:T(8,128)(2,1)S(1)} %get-tuple-element.38), channel_id=1, source_target_pairs={{0,1},{1,2},{2,3},{3,4},{4,5},{5,6},{6,7},{7,0},{8,9},{9,10},{10,1... | collective-permute-start | bytes 737288 | tf_op jit(solution)/shard_map/ppermute | solution.py:384
  56.8 10.8 %collective-permute-start.10 = (bf16[160,768]{1,0:T(8,128)(2,1)S(1)}, bf16[160,768]{1,0:T(8,128)(2,1)S(1)}, u32[]{:S(2)}, u32[]{:S(2)}) collective-permute-start(bf16[160,768]{1,0:T(8,128)(2,1)S(1)} %get-tuple-element.37), channel_id=1, source_target_pairs={{0,7},{1,0},{2,1},{3,2},{4,3},{5,4},{6,5},{7,6},{8,15},{9,8},{10,9... | collective-permute-start | bytes 737288 | tf_op jit(solution)/shard_map/ppermute | solution.py:384
  63.5 11.3 %collective-permute-start.13 = (bf16[160,768]{1,0:T(8,128)(2,1)S(1)}, bf16[160,768]{1,0:T(8,128)(2,1)S(1)}, u32[]{:S(2)}, u32[]{:S(2)}) collective-permute-start(bf16[160,768]{1,0:T(8,128)(2,1)S(1)} %get-tuple-element.45), channel_id=1, source_target_pairs={{0,7},{1,0},{2,1},{3,2},{4,3},{5,4},{6,5},{7,6},{8,15},{9,8},{10,9... | collective-permute-start | bytes 737288 | tf_op jit(solution)/shard_map/ppermute | solution.py:384
  65.3 9.3 %collective-permute-start.14 = (bf16[160,768]{1,0:T(8,128)(2,1)S(1)}, bf16[160,768]{1,0:T(8,128)(2,1)S(1)}, u32[]{:S(2)}, u32[]{:S(2)}) collective-permute-start(bf16[160,768]{1,0:T(8,128)(2,1)S(1)} %get-tuple-element.46), channel_id=1, source_target_pairs={{0,1},{1,2},{2,3},{3,4},{4,5},{5,6},{6,7},{7,0},{8,9},{9,10},{10,1... | collective-permute-start | bytes 737288 | tf_op jit(solution)/shard_map/ppermute | solution.py:384
  67.7 14.2 %collective-permute-start.18 = (bf16[160,768]{1,0:T(8,128)(2,1)S(1)}, bf16[160,768]{1,0:T(8,128)(2,1)S(1)}, u32[]{:S(2)}, u32[]{:S(2)}) collective-permute-start(bf16[160,768]{1,0:T(8,128)(2,1)S(1)} %fusion.12), channel_id=1, source_target_pairs={{0,7},{1,0},{2,1},{3,2},{4,3},{5,4},{6,5},{7,6},{8,15},{9,8},{10,9... | collective-permute-start | bytes 737288 | tf_op jit(solution)/shard_map/ppermute | solution.py:384
  71.7 10.1 %collective-permute-start.12 = (bf16[160,768]{1,0:T(8,128)(2,1)S(1)}, bf16[160,768]{1,0:T(8,128)(2,1)S(1)}, u32[]{:S(2)}, u32[]{:S(2)}) collective-permute-start(bf16[160,768]{1,0:T(8,128)(2,1)S(1)} %fusion.11), channel_id=1, source_target_pairs={{0,1},{1,2},{2,3},{3,4},{4,5},{5,6},{6,7},{7,0},{8,9},{9,10},{10,1... | collective-permute-start | bytes 737288 | tf_op jit(solution)/shard_map/ppermute | solution.py:384
  74.7 12.3 %collective-permute-start.17 = (bf16[160,768]{1,0:T(8,128)(2,1)S(1)}, bf16[160,768]{1,0:T(8,128)(2,1)S(1)}, u32[]{:S(2)}, u32[]{:S(2)}) collective-permute-start(bf16[160,768]{1,0:T(8,128)(2,1)S(1)} %fusion.7), channel_id=1, source_target_pairs={{0,1},{1,2},{2,3},{3,4},{4,5},{5,6},{6,7},{7,0},{8,9},{9,10},{10,1... | collective-permute-start | bytes 737288 | tf_op jit(solution)/shard_map/ppermute | solution.py:384
  74.9 12.3 %collective-permute-start.16 = (bf16[160,768]{1,0:T(8,128)(2,1)S(1)}, bf16[160,768]{1,0:T(8,128)(2,1)S(1)}, u32[]{:S(2)}, u32[]{:S(2)}) collective-permute-start(bf16[160,768]{1,0:T(8,128)(2,1)S(1)} %fusion.8), channel_id=1, source_target_pairs={{0,7},{1,0},{2,1},{3,2},{4,3},{5,4},{6,5},{7,6},{8,15},{9,8},{10,9... | collective-permute-start | bytes 737288 | tf_op jit(solution)/shard_map/ppermute | solution.py:384
  81.8 10.5 %collective-permute-start.15 = (bf16[160,768]{1,0:T(8,128)(2,1)S(1)}, bf16[160,768]{1,0:T(8,128)(2,1)S(1)}, u32[]{:S(2)}, u32[]{:S(2)}) collective-permute-start(bf16[160,768]{1,0:T(8,128)(2,1)S(1)} %fusion.9), channel_id=1, source_target_pairs={{0,1},{1,2},{2,3},{3,4},{4,5},{5,6},{6,7},{7,0},{8,9},{9,10},{10,1... | collective-permute-start | bytes 737288 | tf_op jit(solution)/shard_map/ppermute | solution.py:384
  82.0 10.4 %collective-permute-start.22 = (bf16[160,768]{1,0:T(8,128)(2,1)S(1)}, bf16[160,768]{1,0:T(8,128)(2,1)S(1)}, u32[]{:S(2)}, u32[]{:S(2)}) collective-permute-start(bf16[160,768]{1,0:T(8,128)(2,1)S(1)} %fusion.4), channel_id=1, source_target_pairs={{0,7},{1,0},{2,1},{3,2},{4,3},{5,4},{6,5},{7,6},{8,15},{9,8},{10,9... | collective-permute-start | bytes 737288 | tf_op jit(solution)/shard_map/ppermute | solution.py:384
  87.1 10.5 %collective-permute-start.20 = (bf16[160,768]{1,0:T(8,128)(2,1)S(1)}, bf16[160,768]{1,0:T(8,128)(2,1)S(1)}, u32[]{:S(2)}, u32[]{:S(2)}) collective-permute-start(bf16[160,768]{1,0:T(8,128)(2,1)S(1)} %fusion.5), channel_id=1, source_target_pairs={{0,1},{1,2},{2,3},{3,4},{4,5},{5,6},{6,7},{7,0},{8,9},{9,10},{10,1... | collective-permute-start | bytes 737288 | tf_op jit(solution)/shard_map/ppermute | solution.py:384
  87.3 9.2 %collective-permute-start.21 = (bf16[160,768]{1,0:T(8,128)(2,1)S(1)}, bf16[160,768]{1,0:T(8,128)(2,1)S(1)}, u32[]{:S(2)}, u32[]{:S(2)}) collective-permute-start(bf16[160,768]{1,0:T(8,128)(2,1)S(1)} %fusion.6), channel_id=1, source_target_pairs={{0,7},{1,0},{2,1},{3,2},{4,3},{5,4},{6,5},{7,6},{8,15},{9,8},{10,9... | collective-permute-start | bytes 737288 | tf_op jit(solution)/shard_map/ppermute | solution.py:384
  92.4 6.7 %collective-permute-start.23 = (bf16[160,768]{1,0:T(8,128)(2,1)S(1)}, bf16[160,768]{1,0:T(8,128)(2,1)S(1)}, u32[]{:S(2)}, u32[]{:S(2)}) collective-permute-start(bf16[160,768]{1,0:T(8,128)(2,1)S(1)} %fusion.3), channel_id=1, source_target_pairs={{0,7},{1,0},{2,1},{3,2},{4,3},{5,4},{6,5},{7,6},{8,15},{9,8},{10,9... | collective-permute-start | bytes 737288 | tf_op jit(solution)/shard_map/ppermute | solution.py:384
  95.4 7.4 %collective-permute-start.19 = (bf16[160,768]{1,0:T(8,128)(2,1)S(1)}, bf16[160,768]{1,0:T(8,128)(2,1)S(1)}, u32[]{:S(2)}, u32[]{:S(2)}) collective-permute-start(bf16[160,768]{1,0:T(8,128)(2,1)S(1)} %fusion.10), channel_id=1, source_target_pairs={{0,1},{1,2},{2,3},{3,4},{4,5},{5,6},{6,7},{7,0},{8,9},{9,10},{10,1... | collective-permute-start | bytes 737288 | tf_op jit(solution)/shard_map/ppermute | solution.py:384

commit v6 on v5

--- a/solution.py
+++ b/solution.py
@@ -17,6 +17,7 @@
 SHARDS = 32
 ROWS = 80
 PIECE = 160
+KEPT = 2
 FAR, NEAR, NEXT, REST = (4,), (3, -3), (2, -2), (1, -1, 0)
 NBLK = TOK // BLK
 F32 = jnp.float32
@@ -145,9 +146,10 @@
     )(half, received, mark)
 
 
-def inner_body(x_ref, g_ref, b_ref, c_ref, step_ref, log_ref, skip_ref, mark_ref, pre_ref, gain_ref, state_ref, past_ref):
+def inner_body(x_ref, g_ref, b_ref, c_ref, step_ref, log_ref, skip_ref, mark_ref, near_ref, pre_ref, gain_ref, state_ref, past_ref):
     k = pl.program_id(0)
     tokens = pl.ds(pl.multiple_of(k * BLK, BLK), BLK)
+    kept = pl.ds(pl.multiple_of(jnp.minimum(k, KEPT) * BLK, BLK), BLK)
 
     @pl.when(k == 0)
     def _():
@@ -190,7 +192,9 @@
         out = out + skip_ref[0, h] * x_here.astype(F32)
         gate = g_ref[:, here].astype(F32)
         silu = 0.5 * gate * (1.0 + jnp.tanh(0.5 * gate))
-        pre_ref[:, here] = (out * silu).astype(BF16)
+        pre = (out * silu).astype(BF16)
+        near_ref[kept, here] = pre
+        pre_ref[:, here] = pre
         gain_ref[tokens, here] = (silu * columns[:, 32 + h : 33 + h]).astype(BF16)
         scaled = (turned * tail[h : h + 1, :]).astype(BF16)
         state_ref[:, here] = grow[h : h + 1, :] * state + jnp.dot(scaled, x_here, preferred_element_type=F32)
@@ -211,8 +215,12 @@
             IN_SMEM,
             ANYWHERE,
         ],
-        out_specs=[pl.BlockSpec((BLK, CH), lambda i: (i, 0)), IN_VMEM],
-        out_shape=[pltpu.HBM((TOK, CH), BF16), pltpu.VMEM((TOK, CH), BF16)],
+        out_specs=[IN_VMEM, pl.BlockSpec((BLK, CH), lambda i: (jnp.maximum(i - KEPT, 0), 0)), IN_VMEM],
+        out_shape=[
+            pltpu.VMEM(((KEPT + 1) * BLK, CH), BF16),
+            pltpu.HBM((TOK - KEPT * BLK, CH), BF16),
+            pltpu.VMEM((TOK, CH), BF16),
+        ],
         scratch_shapes=[pltpu.VMEM((N, CH), F32), pltpu.VMEM((16, BLK), F32)],
         compiler_params=SMALL,
         cost_estimate=pl.CostEstimate(flops=1 << 20, bytes_accessed=40 << 20, transcendentals=0),
@@ -269,7 +277,7 @@
     return pltpu.VMEM((count, 4, ROWS, CH), BF16)
 
 
-def hidden_body(in_ref, c_ref, pre_ref, gain_ref, hidden_ref, state_ref):
+def hidden_body(in_ref, c_ref, near_ref, pre_ref, gain_ref, hidden_ref, state_ref):
     rows = c_ref.shape[0]
     here = pl.ds(pl.multiple_of(pl.program_id(0) * rows, rows), rows)
 
@@ -281,18 +289,20 @@
     for half in range(2):
         cols = slice(half * HALF, (half + 1) * HALF)
         carried = jnp.dot(c_ref[...], state_ref[half], preferred_element_type=F32)
-        hidden_ref[here, cols] = (pre_ref[:, cols].astype(F32) + gain_ref[here, cols].astype(F32) * carried).astype(BF16)
-
-
-def hidden_of(entering, c, pre, gain):
-    rows = 256
+        pre = jnp.where(pl.program_id(0) == 0, near_ref[:rows, cols], pre_ref[:, cols])
+        hidden_ref[here, cols] = (pre.astype(F32) + gain_ref[here, cols].astype(F32) * carried).astype(BF16)
+
+
+def hidden_of(entering, c, near, pre, gain):
+    rows = KEPT * BLK
     return pl.pallas_call(
         hidden_body,
         grid=(TOK // rows,),
         in_specs=[
             pl.BlockSpec((16, 2, 8, HALF), lambda i: (0, 0, 0, 0)),
             pl.BlockSpec((rows, N), lambda i: (i, 0)),
-            pl.BlockSpec((rows, CH), lambda i: (i, 0)),
+            IN_VMEM,
+            pl.BlockSpec((rows, CH), lambda i: (jnp.maximum(i - 1, 0), 0)),
             IN_VMEM,
         ],
         out_specs=IN_VMEM,
@@ -300,7 +310,7 @@
         scratch_shapes=[pltpu.VMEM((2, N, HALF), BF16)],
         compiler_params=SMALL,
         cost_estimate=pl.CostEstimate(flops=2 * TOK * N * CH, bytes_accessed=5 << 20, transcendentals=0),
-    )(entering, *[in_hbm(v) for v in (c, pre)], in_vmem(gain))
+    )(entering, in_hbm(c), in_vmem(near), in_hbm(pre), in_vmem(gain))
 
 
 def in_place(blocks):
@@ -465,11 +475,11 @@
     one, three = (from_line(line, 1, offset) for offset in (1, 3))
     received = lax.all_to_all(payload.reshape(SHARDS, 8, HALF + P_SIZE), ("seq", "row"), 0, 0)
     parts = inner(x, g, b, c, step, log_gate, skip, payload)
-    line, one, three = hold([line, one, three], received, in_hbm(parts[0]))
+    line, one, three = hold([line, one, three], received, in_hbm(parts[1]))
     two = from_line(line, 1, 2)
     other = [shift(v, "seq", 1) for v in (line, one, three)]
     half = lax.rem(lax.axis_index("row"), 2).reshape(1)
-    slices = scan_shards(half, received, in_hbm(parts[0]))
+    slices = scan_shards(half, received, in_hbm(parts[1]))
     entering = lax.all_to_all(slices, ("seq", "row"), 0, 0)
     (two,) = hold([two], entering)
     other.insert(2, shift(two, "seq", 1))

time: 104 us -> 103 us (level)
  no operation moved by 1% of the time
where the time goes in v6:
time: 103 us
  starting transfers between devices  46.5 us (45%)
  waiting for transfers between devices  28.3 us (27%)
  Pallas kernels  26.3 us (26%)
  other arithmetic  1.59 us (2%)
    ppermute x18, starting transfers between devices, shift(): lax.ppermute(value, axis, [(i, (i + by) % size) for i in range(size)])  26.2 us
    ppermute x18, waiting for transfers between devices, shift(): lax.ppermute(value, axis, [(i, (i + by) % size) for i in range(size)])  15.4 us
    pallas_call x1, Pallas kernels, inner(): pl.pallas_call(inner_body, grid=(NBLK,), in_specs=[pl.BlockSpec((BLK, CH)...  9.35 us
    ppermute x6, starting transfers between devices, from_line(): return lax.ppermute(value, ('seq', 'row'), pairs)  8.93 us
    all_to_all x1, waiting for transfers between devices, shards(): entering = lax.all_to_all(slices, ('seq', 'row'), 0, 0)  8.53 us
    all_to_all x1, starting transfers between devices, shards(): entering = lax.all_to_all(slices, ('seq', 'row'), 0, 0)  5.7 us
    all_to_all x1, starting transfers between devices, shards(): lax.all_to_all(payload.reshape(SHARDS, 8, HALF + P_SIZE), ('seq', 'row'),...  5.64 us
    pallas_call x2, Pallas kernels, rest_parts(): pl.pallas_call(functools.partial(rest_body, ups), in_specs=[IN_VMEM, IN_V...  4.03 us
  transfers between devices with their start and end apart: 26, of which 12 were waited for; matrix products, arithmetic and copies ran while one was open for 1% of the time, Pallas kernels for 22%

profile of v6, /device:TPU:24, one launch (start us, length us, event | category | flops | bytes accessed | tf_op | source)
XLA Modules:
  0.0 103.0 jit_solution(16672672954691762795)
XLA Ops:
  0.0 3.0 %collective-permute-start.1 = (bf16[80,1280]{1,0:T(8,128)(2,1)}, bf16[80,1280]{1,0:T(8,128)(2,1)S(1)}, u32[]{:S(2)}, u32[]{:S(2)}) collective-permute-start(bf16[80,1280]{1,0:T(8,128)(2,1)} %own.1), channel_id=1, source_target_pairs={{16,0},{24,8},{0,16},{8,24},{48,32},{56,40},{32,48},{40,56},{80,64... | collective-permute-start | bytes 614408 | tf_op jit(solution)/shard_map/ppermute | solution.py:419
  3.0 1.1 %collective-permute-start = (bf16[80,1280]{1,0:T(8,128)(2,1)}, bf16[80,1280]{1,0:T(8,128)(2,1)S(1)}, u32[]{:S(2)}, u32[]{:S(2)}) collective-permute-start(bf16[80,1280]{1,0:T(8,128)(2,1)} %own.1), channel_id=1, source_target_pairs={{8,0},{16,8},{24,16},{0,24},{40,32},{48,40},{56,48},{32,56},{72,64... | collective-permute-start | bytes 614408 | tf_op jit(solution)/shard_map/ppermute | solution.py:419
  5.1 3.0 %shard_map.82.mark_ref.mark = bf16[16,2,8,768]{3,2,1,0:T(8,128)(2,1)} custom-call(bf16[768,1280]{1,0:T(8,128)(2,1)} %x_ref.3, bf16[768,128]{1,0:T(8,128)(2,1)} %b_ref.3, f32[10,768]{1,0:T(8,128)} %step_ref.3, f32[10,768]{1,0:T(8,128)} %log_ref.3), custom_call_target="tpu_custom_call" | custom-call | flops 251658240 | bytes 3145728 | tf_op jit(solution)/shard_map/pallas_call | solution.py:104
  8.0 1.7 %collective-permute-done.one = bf16[80,1280]{1,0:T(8,128)(2,1)S(1)} collective-permute-done((bf16[80,1280]{1,0:T(8,128)(2,1)}, bf16[80,1280]{1,0:T(8,128)(2,1)S(1)}, u32[]{:S(2)}, u32[]{:S(2)}) %collective-permute-start) | collective-permute-done | bytes 204832 | tf_op jit(solution)/shard_map/ppermute | solution.py:419
  9.8 1.6 %collective-permute-done.2.three = bf16[80,1280]{1,0:T(8,128)(2,1)S(1)} collective-permute-done((bf16[80,1280]{1,0:T(8,128)(2,1)}, bf16[80,1280]{1,0:T(8,128)(2,1)S(1)}, u32[]{:S(2)}, u32[]{:S(2)}) %collective-permute-start.2) | collective-permute-done | bytes 204832 | tf_op jit(solution)/shard_map/ppermute | solution.py:419
  12.6 1.7 %collective-permute-start.3 = (bf16[4,80,1280]{2,1,0:T(8,128)(2,1)}, bf16[4,80,1280]{2,1,0:T(8,128)(2,1)}, u32[]{:S(2)}, u32[]{:S(2)}) collective-permute-start(bf16[4,80,1280]{2,1,0:T(8,128)(2,1)} %shard_map.86.refs_0_), channel_id=1, source_target_pairs={{32,0},{40,8},{48,16},{56,24},{64,32},{72,40},{80,48},{88,56},{96,... | collective-permute-start | bytes 2457608 | tf_op jit(solution)/shard_map/ppermute | solution.py:419
  14.3 5.6 %all-to-all-start = ((bf16[32,8,768]{2,1,0:T(8,128)(2,1)}), bf16[32,8,768]{2,1,0:T(8,128)(2,1)S(1)}, u32[]{:S(2)}, u32[]{:S(2)}) async-start(bf16[32,8,768]{2,1,0:T(8,128)(2,1)} %bitcast.1), calls=%async_computation | async-start | bytes 786432 | tf_op jit(solution)/shard_map/all_to_all | solution.py:476
  20.0 9.4 %shard_map.83 = (bf16[384,1280]{1,0:T(8,128)(2,1)S(1)}, bf16[512,1280]{1,0:T(8,128)(2,1)}, bf16[768,1280]{1,0:T(8,128)(2,1)S(1)}) custom-call(bf16[768,1280]{1,0:T(8,128)(2,1)} %x_ref.3, bf16[768,1280]{1,0:T(8,128)(2,1)} %g_ref.1, bf16[768,128]{1,0:T(8,128)(2,1)} %b_ref.3, bf16[768,128]{1,0:T(8,128)(2,1)} %c_ref.3, f32[10,768]{1,0:T(8,128)} %step_ref.3, ...), custom_call_target="tpu_custom_call" | custom-call | flops 1048576 | bytes 41943040 | tf_op jit(solution)/shard_map/pallas_call | solution.py:205
  29.3 1.1 %all-to-all-done.in_ref.refs_3_ = bf16[32,8,768]{2,1,0:T(8,128)(2,1)S(1)} async-done(((bf16[32,8,768]{2,1,0:T(8,128)(2,1)}), bf16[32,8,768]{2,1,0:T(8,128)(2,1)S(1)}, u32[]{:S(2)}, u32[]{:S(2)}) %all-to-all-start) | async-done | bytes 393248 | tf_op jit(solution)/shard_map/all_to_all | solution.py:476
  30.4 1.9 %collective-permute-start.5 = (bf16[4,80,1280]{2,1,0:T(8,128)(2,1)}, bf16[4,80,1280]{2,1,0:T(8,128)(2,1)}, u32[]{:S(2)}, u32[]{:S(2)}) collective-permute-start(bf16[4,80,1280]{2,1,0:T(8,128)(2,1)} %get-tuple-element.34.refs_0_), channel_id=1, source_target_pairs={{64,0},{72,8},{80,16},{88,24},{96,32},{104,40},{112,48},{120,56},{... | collective-permute-start | bytes 2457608 | tf_op jit(solution)/shard_map/ppermute | solution.py:419
  32.3 1.2 %shard_map.84 = bf16[32,8,640]{2,1,0:T(8,128)(2,1)} custom-call(s32[1]{0:T(128)} %bitcast.half_ref, bf16[32,8,768]{2,1,0:T(8,128)(2,1)S(1)} %all-to-all-done.in_ref.refs_3_, bf16[512,1280]{1,0:T(8,128)(2,1)} %get-tuple-element.31.mark_ref.pre_ref.refs_4_), custom_call_target="tpu_custom_call" | custom-call | tf_op jit(solution)/shard_map/pallas_call | solution.py:135
  33.5 5.7 %all-to-all-start.1 = ((bf16[32,8,640]{2,1,0:T(8,128)(2,1)}), bf16[32,8,640]{2,1,0:T(8,128)(2,1)S(1)}, u32[]{:S(2)}, u32[]{:S(2)}) async-start(bf16[32,8,640]{2,1,0:T(8,128)(2,1)} %shard_map.84), calls=%async_computation.1 | async-start | bytes 655360 | tf_op jit(solution)/shard_map/all_to_all | solution.py:483
  40.0 8.5 %all-to-all-done.1.refs_1_ = bf16[32,8,640]{2,1,0:T(8,128)(2,1)S(1)} async-done(((bf16[32,8,640]{2,1,0:T(8,128)(2,1)}), bf16[32,8,640]{2,1,0:T(8,128)(2,1)S(1)}, u32[]{:S(2)}, u32[]{:S(2)}) %all-to-all-start.1) | async-done | bytes 327712 | tf_op jit(solution)/shard_map/all_to_all | solution.py:483
  48.6 3.1 %shard_map.85.hidden_ref = bf16[768,1280]{1,0:T(8,128)(2,1)S(1)} custom-call(bf16[16,2,8,640]{3,2,1,0:T(8,128)(2,1)S(1)} %bitcast.47, bf16[768,128]{1,0:T(8,128)(2,1)} %c_ref.3, bf16[384,1280]{1,0:T(8,128)(2,1)S(1)} %get-tuple-element.32.near_ref, bf16[512,1280]{1,0:T(8,128)(2,1)} %get-tuple-element.31.mark_ref.pre_ref.refs_4_, ...), custom_call_target="tpu_custom_call" | custom-call | flops 251658240 | bytes 5242880 | tf_op jit(solution)/shard_map/pallas_call | solution.py:298
  51.7 2.3 %shard_map.89 = (bf16[160,768]{1,0:T(8,128)(2,1)S(1)}, bf16[160,768]{1,0:T(8,128)(2,1)S(1)}, bf16[2,4,80,1280]{3,2,1,0:T(8,128)(2,1)S(1)}) custom-call(bf16[768,1280]{1,0:T(8,128)(2,1)S(1)} %shard_map.85.hidden_ref, bf16[4,80,1280]{2,1,0:T(8,128)(2,1)} %get-tuple-element.34.refs_0_, bf16[4,80,1280]{2,1,0:T(8,128)(2,1)} %get-tuple-element.35.refs_1_, ...), custom_call_target="tpu_custom_call" | custom-call | flops 629145600 | bytes 2097152 | tf_op jit(solution)/shard_map/pallas_call | solution.py:332
  54.0 2.0 %collective-permute-start.11 = (bf16[160,768]{1,0:T(8,128)(2,1)S(1)}, bf16[160,768]{1,0:T(8,128)(2,1)S(1)}, u32[]{:S(2)}, u32[]{:S(2)}) collective-permute-start(bf16[160,768]{1,0:T(8,128)(2,1)S(1)} %get-tuple-element.40), channel_id=1, source_target_pairs={{0,1},{1,2},{2,3},{3,4},{4,5},{5,6},{6,7},{7,0},{8,9},{9,10},{10,1... | collective-permute-start | bytes 737288 | tf_op jit(solution)/shard_map/ppermute | solution.py:394
  56.0 4.2 %collective-permute-start.10 = (bf16[160,768]{1,0:T(8,128)(2,1)S(1)}, bf16[160,768]{1,0:T(8,128)(2,1)S(1)}, u32[]{:S(2)}, u32[]{:S(2)}) collective-permute-start(bf16[160,768]{1,0:T(8,128)(2,1)S(1)} %get-tuple-element.39), channel_id=1, source_target_pairs={{0,7},{1,0},{2,1},{3,2},{4,3},{5,4},{6,5},{7,6},{8,15},{9,8},{10,9... | collective-permute-start | bytes 737288 | tf_op jit(solution)/shard_map/ppermute | solution.py:394
  60.2 2.5 %shard_map.90 = (bf16[160,768]{1,0:T(8,128)(2,1)S(1)}, bf16[160,768]{1,0:T(8,128)(2,1)S(1)}, bf16[2,160,768]{2,1,0:T(8,128)(2,1)S(1)}, bf16[2,4,80,1280]{3,2,1,0:T(8,128)(2,1)S(1)}) custom-call(bf16[768,1280]{1,0:T(8,128)(2,1)S(1)} %shard_map.85.hidden_ref, bf16[2,4,80,1280]{3,2,1,0:T(8,128)(2,1)S(1)} %get-tuple-element.37.held, ...), custom_call_target="tpu_custom_call" | custom-call | flops 1258291200 | bytes 2097152 | tf_op jit(solution)/shard_map/pallas_call | solution.py:356
  62.7 1.8 %collective-permute-start.13 = (bf16[160,768]{1,0:T(8,128)(2,1)S(1)}, bf16[160,768]{1,0:T(8,128)(2,1)S(1)}, u32[]{:S(2)}, u32[]{:S(2)}) collective-permute-start(bf16[160,768]{1,0:T(8,128)(2,1)S(1)} %get-tuple-element.47), channel_id=1, source_target_pairs={{0,7},{1,0},{2,1},{3,2},{4,3},{5,4},{6,5},{7,6},{8,15},{9,8},{10,9... | collective-permute-start | bytes 737288 | tf_op jit(solution)/shard_map/ppermute | solution.py:394
  64.8 1.9 %shard_map.91 = (bf16[2,2,160,768]{3,2,1,0:T(8,128)(2,1)S(1)}, bf16[3,4,80,1280]{3,2,1,0:T(8,128)(2,1)S(1)}) custom-call(bf16[768,1280]{1,0:T(8,128)(2,1)S(1)} %shard_map.85.hidden_ref, bf16[2,4,80,1280]{3,2,1,0:T(8,128)(2,1)S(1)} %get-tuple-element.41.held, bf16[4,80,1280]{2,1,0:T(8,128)(2,1)} %get-tuple-element.34.refs_0_, ...), custom_call_target="tpu_custom_call" | custom-call | flops 1258291200 | bytes 2097152 | tf_op jit(solution)/shard_map/pallas_call | solution.py:381
  66.9 4.0 %collective-permute-start.18 = (bf16[160,768]{1,0:T(8,128)(2,1)S(1)}, bf16[160,768]{1,0:T(8,128)(2,1)S(1)}, u32[]{:S(2)}, u32[]{:S(2)}) collective-permute-start(bf16[160,768]{1,0:T(8,128)(2,1)S(1)} %fusion.12), channel_id=1, source_target_pairs={{0,7},{1,0},{2,1},{3,2},{4,3},{5,4},{6,5},{7,6},{8,15},{9,8},{10,9... | collective-permute-start | bytes 737288 | tf_op jit(solution)/shard_map/ppermute | solution.py:394
  70.8 2.1 %shard_map.92 = bf16[3,2,160,768]{3,2,1,0:T(8,128)(2,1)S(1)} custom-call(bf16[768,1280]{1,0:T(8,128)(2,1)S(1)} %shard_map.85.hidden_ref, bf16[3,4,80,1280]{3,2,1,0:T(8,128)(2,1)S(1)} %get-tuple-element.46.held, bf16[4,80,1280]{2,1,0:T(8,128)(2,1)} %get-tuple-element.34.refs_0_, bf16[4,80,1280]{2,1,0:T(8,128)(2,1)} %get-tuple-element.35.refs_1_, ...), custom_call_target="tpu_custom_call" | custom-call | flops 1887436800 | bytes 3145728 | tf_op jit(solution)/shard_map/pallas_call | solution.py:381
  74.1 3.3 %collective-permute-start.16 = (bf16[160,768]{1,0:T(8,128)(2,1)S(1)}, bf16[160,768]{1,0:T(8,128)(2,1)S(1)}, u32[]{:S(2)}, u32[]{:S(2)}) collective-permute-start(bf16[160,768]{1,0:T(8,128)(2,1)S(1)} %fusion.8), channel_id=1, source_target_pairs={{0,7},{1,0},{2,1},{3,2},{4,3},{5,4},{6,5},{7,6},{8,15},{9,8},{10,9... | collective-permute-start | bytes 737288 | tf_op jit(solution)/shard_map/ppermute | solution.py:394
  77.4 3.6 %collective-permute-done.12 = bf16[160,768]{1,0:T(8,128)(2,1)S(1)} collective-permute-done((bf16[160,768]{1,0:T(8,128)(2,1)S(1)}, bf16[160,768]{1,0:T(8,128)(2,1)S(1)}, u32[]{:S(2)}, u32[]{:S(2)}) %collective-permute-start.12) | collective-permute-done | bytes 245792 | tf_op jit(solution)/shard_map/ppermute | solution.py:394
  81.2 3.3 %collective-permute-start.22 = (bf16[160,768]{1,0:T(8,128)(2,1)S(1)}, bf16[160,768]{1,0:T(8,128)(2,1)S(1)}, u32[]{:S(2)}, u32[]{:S(2)}) collective-permute-start(bf16[160,768]{1,0:T(8,128)(2,1)S(1)} %fusion.4), channel_id=1, source_target_pairs={{0,7},{1,0},{2,1},{3,2},{4,3},{5,4},{6,5},{7,6},{8,15},{9,8},{10,9... | collective-permute-start | bytes 737288 | tf_op jit(solution)/shard_map/ppermute | solution.py:394
  84.5 1.7 %collective-permute-done.17 = bf16[160,768]{1,0:T(8,128)(2,1)S(1)} collective-permute-done((bf16[160,768]{1,0:T(8,128)(2,1)S(1)}, bf16[160,768]{1,0:T(8,128)(2,1)S(1)}, u32[]{:S(2)}, u32[]{:S(2)}) %collective-permute-start.17) | collective-permute-done | bytes 245792 | tf_op jit(solution)/shard_map/ppermute | solution.py:394
  86.4 3.3 %collective-permute-start.21 = (bf16[160,768]{1,0:T(8,128)(2,1)S(1)}, bf16[160,768]{1,0:T(8,128)(2,1)S(1)}, u32[]{:S(2)}, u32[]{:S(2)}) collective-permute-start(bf16[160,768]{1,0:T(8,128)(2,1)S(1)} %fusion.6), channel_id=1, source_target_pairs={{0,7},{1,0},{2,1},{3,2},{4,3},{5,4},{6,5},{7,6},{8,15},{9,8},{10,9... | collective-permute-start | bytes 737288 | tf_op jit(solution)/shard_map/ppermute | solution.py:394
  89.7 1.7 %collective-permute-done.15 = bf16[160,768]{1,0:T(8,128)(2,1)S(1)} collective-permute-done((bf16[160,768]{1,0:T(8,128)(2,1)S(1)}, bf16[160,768]{1,0:T(8,128)(2,1)S(1)}, u32[]{:S(2)}, u32[]{:S(2)}) %collective-permute-start.15) | collective-permute-done | bytes 245792 | tf_op jit(solution)/shard_map/ppermute | solution.py:394
  91.6 2.9 %collective-permute-start.23 = (bf16[160,768]{1,0:T(8,128)(2,1)S(1)}, bf16[160,768]{1,0:T(8,128)(2,1)S(1)}, u32[]{:S(2)}, u32[]{:S(2)}) collective-permute-start(bf16[160,768]{1,0:T(8,128)(2,1)S(1)} %fusion.3), channel_id=1, source_target_pairs={{0,7},{1,0},{2,1},{3,2},{4,3},{5,4},{6,5},{7,6},{8,15},{9,8},{10,9... | collective-permute-start | bytes 737288 | tf_op jit(solution)/shard_map/ppermute | solution.py:394
  95.6 1.1 %collective-permute-done.20 = bf16[160,768]{1,0:T(8,128)(2,1)S(1)} collective-permute-done((bf16[160,768]{1,0:T(8,128)(2,1)S(1)}, bf16[160,768]{1,0:T(8,128)(2,1)S(1)}, u32[]{:S(2)}, u32[]{:S(2)}) %collective-permute-start.20) | collective-permute-done | bytes 245792 | tf_op jit(solution)/shard_map/ppermute | solution.py:394
  96.7 1.5 %collective-permute-done.23 = bf16[160,768]{1,0:T(8,128)(2,1)S(1)} collective-permute-done((bf16[160,768]{1,0:T(8,128)(2,1)S(1)}, bf16[160,768]{1,0:T(8,128)(2,1)S(1)}, u32[]{:S(2)}, u32[]{:S(2)}) %collective-permute-start.23) | collective-permute-done | bytes 245792 | tf_op jit(solution)/shard_map/ppermute | solution.py:394
  98.3 3.7 %collective-permute-done.19 = bf16[160,768]{1,0:T(8,128)(2,1)S(1)} collective-permute-done((bf16[160,768]{1,0:T(8,128)(2,1)S(1)}, bf16[160,768]{1,0:T(8,128)(2,1)S(1)}, u32[]{:S(2)}, u32[]{:S(2)}) %collective-permute-start.19) | collective-permute-done | bytes 245792 | tf_op jit(solution)/shard_map/ppermute | solution.py:394
  (47 shorter events, 7.1 us)
Async XLA Ops:
  0.0 11.3 %copy-start = (bf16[80,1280]{1,0:T(8,128)(2,1)S(1)}, bf16[80,1280]{1,0:T(8,128)(2,1)}, u32[]{:S(2)}) copy-start(bf16[80,1280]{1,0:T(8,128)(2,1)} %own.1) | copy-start | bytes 614404
  0.0 8.0 %collective-permute-start.1 = (bf16[80,1280]{1,0:T(8,128)(2,1)}, bf16[80,1280]{1,0:T(8,128)(2,1)S(1)}, u32[]{:S(2)}, u32[]{:S(2)}) collective-permute-start(bf16[80,1280]{1,0:T(8,128)(2,1)} %own.1), channel_id=1, source_target_pairs={{16,0},{24,8},{0,16},{8,24},{48,32},{56,40},{32,48},{40,56},{80,64... | collective-permute-start | bytes 614408 | tf_op jit(solution)/shard_map/ppermute | solution.py:419
  3.0 6.7 %collective-permute-start = (bf16[80,1280]{1,0:T(8,128)(2,1)}, bf16[80,1280]{1,0:T(8,128)(2,1)S(1)}, u32[]{:S(2)}, u32[]{:S(2)}) collective-permute-start(bf16[80,1280]{1,0:T(8,128)(2,1)} %own.1), channel_id=1, source_target_pairs={{8,0},{16,8},{24,16},{0,24},{40,32},{48,40},{56,48},{32,56},{72,64... | collective-permute-start | bytes 614408 | tf_op jit(solution)/shard_map/ppermute | solution.py:419
  4.2 7.2 %collective-permute-start.2 = (bf16[80,1280]{1,0:T(8,128)(2,1)}, bf16[80,1280]{1,0:T(8,128)(2,1)S(1)}, u32[]{:S(2)}, u32[]{:S(2)}) collective-permute-start(bf16[80,1280]{1,0:T(8,128)(2,1)} %own.1), channel_id=1, source_target_pairs={{24,0},{0,8},{8,16},{16,24},{56,32},{32,40},{40,48},{48,56},{88,64... | collective-permute-start | bytes 614408 | tf_op jit(solution)/shard_map/ppermute | solution.py:419
  8.0 11.9 %copy-start.1 = (f32[10]{0:T(128)S(1)}, f32[10]{0:T(128)}, u32[]{:S(2)}) copy-start(f32[10]{0:T(128)} %param.14) | copy-start | bytes 124
  12.3 18.1 %collective-permute-start.4 = (bf16[4,80,1280]{2,1,0:T(8,128)(2,1)}, bf16[4,80,1280]{2,1,0:T(8,128)(2,1)}, u32[]{:S(2)}, u32[]{:S(2)}) collective-permute-start(bf16[4,80,1280]{2,1,0:T(8,128)(2,1)} %shard_map.86.refs_0_), channel_id=1, source_target_pairs={{96,0},{104,8},{112,16},{120,24},{0,32},{8,40},{16,48},{24,56},{32... | collective-permute-start | bytes 2457608 | tf_op jit(solution)/shard_map/ppermute | solution.py:419
  12.6 17.9 %collective-permute-start.3 = (bf16[4,80,1280]{2,1,0:T(8,128)(2,1)}, bf16[4,80,1280]{2,1,0:T(8,128)(2,1)}, u32[]{:S(2)}, u32[]{:S(2)}) collective-permute-start(bf16[4,80,1280]{2,1,0:T(8,128)(2,1)} %shard_map.86.refs_0_), channel_id=1, source_target_pairs={{32,0},{40,8},{48,16},{56,24},{64,32},{72,40},{80,48},{88,56},{96,... | collective-permute-start | bytes 2457608 | tf_op jit(solution)/shard_map/ppermute | solution.py:419
  14.3 16.1 %all-to-all-start = ((bf16[32,8,768]{2,1,0:T(8,128)(2,1)}), bf16[32,8,768]{2,1,0:T(8,128)(2,1)S(1)}, u32[]{:S(2)}, u32[]{:S(2)}) async-start(bf16[32,8,768]{2,1,0:T(8,128)(2,1)} %bitcast.1), calls=%async_computation | async-start | bytes 786432 | tf_op jit(solution)/shard_map/all_to_all | solution.py:476
  30.4 18.1 %collective-permute-start.5 = (bf16[4,80,1280]{2,1,0:T(8,128)(2,1)}, bf16[4,80,1280]{2,1,0:T(8,128)(2,1)}, u32[]{:S(2)}, u32[]{:S(2)}) collective-permute-start(bf16[4,80,1280]{2,1,0:T(8,128)(2,1)} %get-tuple-element.34.refs_0_), channel_id=1, source_target_pairs={{64,0},{72,8},{80,16},{88,24},{96,32},{104,40},{112,48},{120,56},{... | collective-permute-start | bytes 2457608 | tf_op jit(solution)/shard_map/ppermute | solution.py:419
  33.5 15.0 %all-to-all-start.1 = ((bf16[32,8,640]{2,1,0:T(8,128)(2,1)}), bf16[32,8,640]{2,1,0:T(8,128)(2,1)S(1)}, u32[]{:S(2)}, u32[]{:S(2)}) async-start(bf16[32,8,640]{2,1,0:T(8,128)(2,1)} %shard_map.84), calls=%async_computation.1 | async-start | bytes 655360 | tf_op jit(solution)/shard_map/all_to_all | solution.py:483
  39.2 12.5 %collective-permute-start.6 = (bf16[4,80,1280]{2,1,0:T(8,128)(2,1)}, bf16[4,80,1280]{2,1,0:T(8,128)(2,1)}, u32[]{:S(2)}, u32[]{:S(2)}) collective-permute-start(bf16[4,80,1280]{2,1,0:T(8,128)(2,1)} %get-tuple-element.34.refs_0_), channel_id=1, source_target_pairs={{0,128},{128,0},{1,129},{129,1},{2,130},{130,2},{3,131},{131,3},{4... | collective-permute-start | bytes 2457608 | tf_op jit(solution)/shard_map/ppermute | solution.py:394
  39.4 12.2 %collective-permute-start.7 = (bf16[4,80,1280]{2,1,0:T(8,128)(2,1)}, bf16[4,80,1280]{2,1,0:T(8,128)(2,1)}, u32[]{:S(2)}, u32[]{:S(2)}) collective-permute-start(bf16[4,80,1280]{2,1,0:T(8,128)(2,1)} %get-tuple-element.35.refs_1_), channel_id=1, source_target_pairs={{0,128},{128,0},{1,129},{129,1},{2,130},{130,2},{3,131},{131,3},{4... | collective-permute-start | bytes 2457608 | tf_op jit(solution)/shard_map/ppermute | solution.py:394
  39.8 11.9 %collective-permute-start.9 = (bf16[4,80,1280]{2,1,0:T(8,128)(2,1)}, bf16[4,80,1280]{2,1,0:T(8,128)(2,1)}, u32[]{:S(2)}, u32[]{:S(2)}) collective-permute-start(bf16[4,80,1280]{2,1,0:T(8,128)(2,1)} %get-tuple-element.36.refs_3_), channel_id=1, source_target_pairs={{0,128},{128,0},{1,129},{129,1},{2,130},{130,2},{3,131},{131,3},{4... | collective-permute-start | bytes 2457608 | tf_op jit(solution)/shard_map/ppermute | solution.py:394
  48.5 3.2 %collective-permute-start.8 = (bf16[4,80,1280]{2,1,0:T(8,128)(2,1)}, bf16[4,80,1280]{2,1,0:T(8,128)(2,1)S(1)}, u32[]{:S(2)}, u32[]{:S(2)}) collective-permute-start(bf16[4,80,1280]{2,1,0:T(8,128)(2,1)} %shard_map.88.refs_2_), channel_id=1, source_target_pairs={{0,128},{128,0},{1,129},{129,1},{2,130},{130,2},{3,131},{131,3},{4... | collective-permute-start | bytes 2457608 | tf_op jit(solution)/shard_map/ppermute | solution.py:394
  54.0 12.7 %collective-permute-start.11 = (bf16[160,768]{1,0:T(8,128)(2,1)S(1)}, bf16[160,768]{1,0:T(8,128)(2,1)S(1)}, u32[]{:S(2)}, u32[]{:S(2)}) collective-permute-start(bf16[160,768]{1,0:T(8,128)(2,1)S(1)} %get-tuple-element.40), channel_id=1, source_target_pairs={{0,1},{1,2},{2,3},{3,4},{4,5},{5,6},{6,7},{7,0},{8,9},{9,10},{10,1... | collective-permute-start | bytes 737288 | tf_op jit(solution)/shard_map/ppermute | solution.py:394
  56.0 10.8 %collective-permute-start.10 = (bf16[160,768]{1,0:T(8,128)(2,1)S(1)}, bf16[160,768]{1,0:T(8,128)(2,1)S(1)}, u32[]{:S(2)}, u32[]{:S(2)}) collective-permute-start(bf16[160,768]{1,0:T(8,128)(2,1)S(1)} %get-tuple-element.39), channel_id=1, source_target_pairs={{0,7},{1,0},{2,1},{3,2},{4,3},{5,4},{6,5},{7,6},{8,15},{9,8},{10,9... | collective-permute-start | bytes 737288 | tf_op jit(solution)/shard_map/ppermute | solution.py:394
  62.7 11.3 %collective-permute-start.13 = (bf16[160,768]{1,0:T(8,128)(2,1)S(1)}, bf16[160,768]{1,0:T(8,128)(2,1)S(1)}, u32[]{:S(2)}, u32[]{:S(2)}) collective-permute-start(bf16[160,768]{1,0:T(8,128)(2,1)S(1)} %get-tuple-element.47), channel_id=1, source_target_pairs={{0,7},{1,0},{2,1},{3,2},{4,3},{5,4},{6,5},{7,6},{8,15},{9,8},{10,9... | collective-permute-start | bytes 737288 | tf_op jit(solution)/shard_map/ppermute | solution.py:394
  64.5 9.3 %collective-permute-start.14 = (bf16[160,768]{1,0:T(8,128)(2,1)S(1)}, bf16[160,768]{1,0:T(8,128)(2,1)S(1)}, u32[]{:S(2)}, u32[]{:S(2)}) collective-permute-start(bf16[160,768]{1,0:T(8,128)(2,1)S(1)} %get-tuple-element.48), channel_id=1, source_target_pairs={{0,1},{1,2},{2,3},{3,4},{4,5},{5,6},{6,7},{7,0},{8,9},{9,10},{10,1... | collective-permute-start | bytes 737288 | tf_op jit(solution)/shard_map/ppermute | solution.py:394
  66.9 14.2 %collective-permute-start.18 = (bf16[160,768]{1,0:T(8,128)(2,1)S(1)}, bf16[160,768]{1,0:T(8,128)(2,1)S(1)}, u32[]{:S(2)}, u32[]{:S(2)}) collective-permute-start(bf16[160,768]{1,0:T(8,128)(2,1)S(1)} %fusion.12), channel_id=1, source_target_pairs={{0,7},{1,0},{2,1},{3,2},{4,3},{5,4},{6,5},{7,6},{8,15},{9,8},{10,9... | collective-permute-start | bytes 737288 | tf_op jit(solution)/shard_map/ppermute | solution.py:394
  70.8 10.1 %collective-permute-start.12 = (bf16[160,768]{1,0:T(8,128)(2,1)S(1)}, bf16[160,768]{1,0:T(8,128)(2,1)S(1)}, u32[]{:S(2)}, u32[]{:S(2)}) collective-permute-start(bf16[160,768]{1,0:T(8,128)(2,1)S(1)} %fusion.11), channel_id=1, source_target_pairs={{0,1},{1,2},{2,3},{3,4},{4,5},{5,6},{6,7},{7,0},{8,9},{9,10},{10,1... | collective-permute-start | bytes 737288 | tf_op jit(solution)/shard_map/ppermute | solution.py:394
  73.9 12.3 %collective-permute-start.17 = (bf16[160,768]{1,0:T(8,128)(2,1)S(1)}, bf16[160,768]{1,0:T(8,128)(2,1)S(1)}, u32[]{:S(2)}, u32[]{:S(2)}) collective-permute-start(bf16[160,768]{1,0:T(8,128)(2,1)S(1)} %fusion.7), channel_id=1, source_target_pairs={{0,1},{1,2},{2,3},{3,4},{4,5},{5,6},{6,7},{7,0},{8,9},{9,10},{10,1... | collective-permute-start | bytes 737288 | tf_op jit(solution)/shard_map/ppermute | solution.py:394
  74.1 12.3 %collective-permute-start.16 = (bf16[160,768]{1,0:T(8,128)(2,1)S(1)}, bf16[160,768]{1,0:T(8,128)(2,1)S(1)}, u32[]{:S(2)}, u32[]{:S(2)}) collective-permute-start(bf16[160,768]{1,0:T(8,128)(2,1)S(1)} %fusion.8), channel_id=1, source_target_pairs={{0,7},{1,0},{2,1},{3,2},{4,3},{5,4},{6,5},{7,6},{8,15},{9,8},{10,9... | collective-permute-start | bytes 737288 | tf_op jit(solution)/shard_map/ppermute | solution.py:394
  81.0 10.5 %collective-permute-start.15 = (bf16[160,768]{1,0:T(8,128)(2,1)S(1)}, bf16[160,768]{1,0:T(8,128)(2,1)S(1)}, u32[]{:S(2)}, u32[]{:S(2)}) collective-permute-start(bf16[160,768]{1,0:T(8,128)(2,1)S(1)} %fusion.9), channel_id=1, source_target_pairs={{0,1},{1,2},{2,3},{3,4},{4,5},{5,6},{6,7},{7,0},{8,9},{9,10},{10,1... | collective-permute-start | bytes 737288 | tf_op jit(solution)/shard_map/ppermute | solution.py:394
  81.2 10.4 %collective-permute-start.22 = (bf16[160,768]{1,0:T(8,128)(2,1)S(1)}, bf16[160,768]{1,0:T(8,128)(2,1)S(1)}, u32[]{:S(2)}, u32[]{:S(2)}) collective-permute-start(bf16[160,768]{1,0:T(8,128)(2,1)S(1)} %fusion.4), channel_id=1, source_target_pairs={{0,7},{1,0},{2,1},{3,2},{4,3},{5,4},{6,5},{7,6},{8,15},{9,8},{10,9... | collective-permute-start | bytes 737288 | tf_op jit(solution)/shard_map/ppermute | solution.py:394
  86.3 10.5 %collective-permute-start.20 = (bf16[160,768]{1,0:T(8,128)(2,1)S(1)}, bf16[160,768]{1,0:T(8,128)(2,1)S(1)}, u32[]{:S(2)}, u32[]{:S(2)}) collective-permute-start(bf16[160,768]{1,0:T(8,128)(2,1)S(1)} %fusion.5), channel_id=1, source_target_pairs={{0,1},{1,2},{2,3},{3,4},{4,5},{5,6},{6,7},{7,0},{8,9},{9,10},{10,1... | collective-permute-start | bytes 737288 | tf_op jit(solution)/shard_map/ppermute | solution.py:394
  86.4 9.2 %collective-permute-start.21 = (bf16[160,768]{1,0:T(8,128)(2,1)S(1)}, bf16[160,768]{1,0:T(8,128)(2,1)S(1)}, u32[]{:S(2)}, u32[]{:S(2)}) collective-permute-start(bf16[160,768]{1,0:T(8,128)(2,1)S(1)} %fusion.6), channel_id=1, source_target_pairs={{0,7},{1,0},{2,1},{3,2},{4,3},{5,4},{6,5},{7,6},{8,15},{9,8},{10,9... | collective-permute-start | bytes 737288 | tf_op jit(solution)/shard_map/ppermute | solution.py:394
  91.6 6.7 %collective-permute-start.23 = (bf16[160,768]{1,0:T(8,128)(2,1)S(1)}, bf16[160,768]{1,0:T(8,128)(2,1)S(1)}, u32[]{:S(2)}, u32[]{:S(2)}) collective-permute-start(bf16[160,768]{1,0:T(8,128)(2,1)S(1)} %fusion.3), channel_id=1, source_target_pairs={{0,7},{1,0},{2,1},{3,2},{4,3},{5,4},{6,5},{7,6},{8,15},{9,8},{10,9... | collective-permute-start | bytes 737288 | tf_op jit(solution)/shard_map/ppermute | solution.py:394
  94.6 7.4 %collective-permute-start.19 = (bf16[160,768]{1,0:T(8,128)(2,1)S(1)}, bf16[160,768]{1,0:T(8,128)(2,1)S(1)}, u32[]{:S(2)}, u32[]{:S(2)}) collective-permute-start(bf16[160,768]{1,0:T(8,128)(2,1)S(1)} %fusion.10), channel_id=1, source_target_pairs={{0,1},{1,2},{2,3},{3,4},{4,5},{5,6},{6,7},{7,0},{8,9},{9,10},{10,1... | collective-permute-start | bytes 737288 | tf_op jit(solution)/shard_map/ppermute | solution.py:394
